TPU v7x, 512 devices: a whole 4x8x8 slice. The times are simulated.
512 devices in a mesh: lon: 64 (over z_hi, y, core), lat: 8 (over z_lo, x).
Axes of the slice: x: 4, y: 8, z: 8 (z_hi: 4, z_lo: 2; z = z_hi * 2 + z_lo), core: 2. Of those that a mesh axis runs over, the one named last changes fastest.
Arguments:
- tokens: bfloat16 [2, 48, 768, 512], P(None, 'lat', 'lon'), may hold values from -20 to 20
- cotangent: bfloat16 [2, 48, 768, 512], P(None, 'lat', 'lon'), may hold values from -6 to 6
- w_qkv: bfloat16 [512, 1536], replicated, may hold values from -8 to 8
- w_proj: bfloat16 [512, 512], replicated, may hold values from -0.25 to 0.25
Outputs:
- d_tokens: bfloat16 [2, 48, 768, 512], P(None, 'lat', 'lon')
- d_weight: float32 [512, 1536], P('lon', 'lat')
All inputs are finite; a program needn't handle non-finite values.
Results may differ from a plain program's by a relative error of at most 0.017.
The roundings to bfloat16 on the way count: a program that leaves them out, or rounds other values in their place, can miss the bound.
Values may be sent and summed in bfloat16 or wider, within the bound.
No kernel may reach another device: no remote copies, remote signals or barrier semaphores. Data moves between devices by JAX's collectives and lax.ppermute only.
A program may use at most 64 MiB of HBM per device.

v0:
```python
import jax
import jax.numpy as jnp
from jax import lax
from jax.sharding import PartitionSpec as P

HEADS = 16
WLEV = 2
WLAT = 6
WLON = 12


EPS = 1e-05
NEG = -1e30


def shifted(block, axis, distance):
    devices = range(lax.axis_size(axis))
    route = [((i - distance) % len(devices), i) for i in devices]
    return lax.ppermute(block, axis, route)


def to_windows(source):
    level_count, lat_rows, lon_cols, channels = source.shape
    shaped = source.reshape(
        level_count // WLEV, WLEV, lat_rows // WLAT, WLAT, lon_cols // WLON, WLON, channels
    )
    return shaped.transpose(0, 2, 4, 1, 3, 5, 6).reshape(-1, WLEV * WLAT * WLON, channels)


def from_windows(source, level_count, lat_rows, lon_cols):
    channels = source.shape[-1]
    shaped = source.reshape(
        level_count // WLEV, lat_rows // WLAT, lon_cols // WLON, WLEV, WLAT, WLON, channels
    )
    return shaped.transpose(0, 3, 1, 4, 2, 5, 6).reshape(level_count, lat_rows, lon_cols, channels)


def shift_rows_in(source):
    margin = WLAT // 2
    border = shifted(source[:, :, :margin], "lat", -1)
    return jnp.concatenate([source[:, :, margin:], border], axis=2)


def shift_cols_in(source):
    margin = WLON // 2
    border = shifted(source[:, :, :, :margin], "lon", -1)
    return jnp.concatenate([source[:, :, :, margin:], border], axis=3)


def shift_rows_out(source):
    margin = WLAT // 2
    border = shifted(source[:, -margin:], "lat", 1)
    return jnp.concatenate([border, source[:, :-margin]], axis=1)


def shift_cols_out(source):
    margin = WLON // 2
    border = shifted(source[:, :, -margin:], "lon", 1)
    return jnp.concatenate([border, source[:, :, :-margin]], axis=2)


def window_pass(inputs_win, grads_win, region_win, w_qkv, w_proj):
    width = w_proj.shape[0]
    head_width = width // HEADS
    window_count, length, _ = inputs_win.shape
    values32 = inputs_win.astype(jnp.float32)
    means = jnp.mean(values32, axis=-1, keepdims=True)
    centred = values32 - means
    inv_std = lax.rsqrt(jnp.mean(centred * centred, axis=-1, keepdims=True) + EPS)
    unit = centred * inv_std
    flat_normed = unit.astype(jnp.bfloat16).reshape(-1, width)
    projected = jnp.dot(flat_normed, w_qkv, preferred_element_type=jnp.float32).astype(jnp.bfloat16)
    projected = projected.reshape(window_count, length, 3, HEADS, head_width)
    queries = projected[:, :, 0]
    key_heads = projected[:, :, 1]
    value_heads = projected[:, :, 2]
    scaling = head_width ** (-0.5)
    scores = (
        jnp.einsum("wqhe,wkhe->whqk", queries, key_heads, preferred_element_type=jnp.float32)
        * scaling
    )
    allowed = region_win[:, :, None] == region_win[:, None, :]
    scores = jnp.where(allowed[:, None], scores, NEG)
    peak = jnp.max(scores, axis=-1, keepdims=True)
    expo = jnp.exp(scores - peak)
    probs = expo / jnp.sum(expo, axis=-1, keepdims=True)
    probs_low = probs.astype(jnp.bfloat16)
    grad_rows = grads_win.reshape(-1, width)
    d_att = jnp.dot(grad_rows, w_proj.T, preferred_element_type=jnp.float32).astype(jnp.bfloat16)
    d_att = d_att.reshape(window_count, length, HEADS, head_width)
    d_probs = jnp.einsum("wqhe,wkhe->whqk", d_att, value_heads, preferred_element_type=jnp.float32)
    d_values = jnp.einsum(
        "whqk,wqhe->wkhe", probs_low, d_att, preferred_element_type=jnp.float32
    ).astype(jnp.bfloat16)
    d_scores = probs * (d_probs - jnp.sum(probs * d_probs, axis=-1, keepdims=True))
    d_low = (d_scores * scaling).astype(jnp.bfloat16)
    d_queries = jnp.einsum(
        "whqk,wkhe->wqhe", d_low, key_heads, preferred_element_type=jnp.float32
    ).astype(jnp.bfloat16)
    d_keys = jnp.einsum(
        "whqk,wqhe->wkhe", d_low, queries, preferred_element_type=jnp.float32
    ).astype(jnp.bfloat16)
    d_proj = jnp.stack((d_queries, d_keys, d_values), axis=2).reshape(-1, 3 * width)
    d_normed = jnp.dot(d_proj, w_qkv.T, preferred_element_type=jnp.float32).reshape(
        window_count, length, width
    )
    d_inputs = inv_std * (
        d_normed
        - jnp.mean(d_normed, axis=-1, keepdims=True)
        - unit * jnp.mean(d_normed * unit, axis=-1, keepdims=True)
    )
    return (d_inputs.astype(jnp.bfloat16), flat_normed, d_proj)


def per_device(tokens, cotangent, w_qkv, w_proj):
    level_count, lat_rows, lon_cols, width = tokens.shape
    stacked = jnp.roll(jnp.stack((tokens, cotangent)), -(WLEV // 2), axis=1)
    stacked = shift_cols_in(shift_rows_in(stacked))
    level_region = (jnp.arange(level_count) >= level_count - WLEV // 2).astype(jnp.int32) * 2
    lat_global = lax.axis_index("lat") * lat_rows + jnp.arange(lat_rows)
    lat_region = (lat_global >= lax.axis_size("lat") * lat_rows - WLAT // 2).astype(jnp.int32)
    region = jnp.broadcast_to(
        level_region[:, None, None] + lat_region[None, :, None], (level_count, lat_rows, lon_cols)
    )
    region_win = to_windows(region[..., None])[..., 0]
    d_win, flat_normed, d_proj = window_pass(
        to_windows(stacked[0]), to_windows(stacked[1]), region_win, w_qkv, w_proj
    )
    d_shifted = from_windows(d_win, level_count, lat_rows, lon_cols)
    d_shifted = shift_cols_out(shift_rows_out(d_shifted))
    d_back = jnp.roll(d_shifted, WLEV // 2, axis=0)
    d_tokens = (cotangent.astype(jnp.float32) + d_back.astype(jnp.float32)).astype(jnp.bfloat16)
    partial_rows = lax.psum_scatter(
        jnp.einsum("tc,tk->ck", flat_normed, d_proj, preferred_element_type=jnp.float32),
        "lon",
        scatter_dimension=0,
        tiled=True,
    )
    d_weight = lax.psum_scatter(
        partial_rows.astype(jnp.bfloat16), "lat", scatter_dimension=1, tiled=True
    ).astype(jnp.float32)
    return (d_tokens, d_weight)


def solution(mesh):
    in_specs = (P(None, "lat", "lon", None), P(None, "lat", "lon", None), P(), P())
    out_specs = (P(None, "lat", "lon", None), P("lon", "lat"))
    return jax.shard_map(
        per_device, mesh=mesh, in_specs=in_specs, out_specs=out_specs, check_vma=False
    )
```

profile of v0, /device:TPU:6, one launch (start us, length us, event | category | flops | bytes accessed | tf_op | source)
XLA Modules:
  0.0 261.2 jit_solution(12790541499914222420)
XLA Ops:
  7.2 0.0 reduce-scatter.5.cloned.1.call-start
  7.2 1.7 slice_maximum_fusion
  8.9 1.6 fusion.33
  10.5 0.2 fusion.59
  10.7 2.7 %collective-permute-start = (bf16[2,2,3,12,512]{4,1,3,2,0:T(2,128)(2,1)S(1)}, bf16[2,2,3,12,512]{4,1,3,2,0:T(2,128)(2,1)S(1)}, u32[]{:S(2)}, u32[]{:S(2)}) collective-permute-start(bf16[2,2,3,12,512]{4,1,3,2,0:T(2,128)(2,1)S(1)} %get-tuple-element.15), channel_id=1, source_target_pairs={{1,0},{2,1},{3,2},{4,3},{5,4},{6,5},{7,6},{0,7},{9,8},{10,9},{11,1... | collective-permute-start | bytes 442376 | tf_op jit(solution)/shard_map/ppermute | solution.py:19
  13.5 0.1 broadcast_add_fusion
  13.6 0.1 broadcast_in_dim_broadcast_in_dim.2
  13.6 0.1 eq.21
  13.7 6.6 %collective-permute-done = bf16[2,2,3,12,512]{4,1,3,2,0:T(2,128)(2,1)S(1)} collective-permute-done((bf16[2,2,3,12,512]{4,1,3,2,0:T(2,128)(2,1)S(1)}, bf16[2,2,3,12,512]{4,1,3,2,0:T(2,128)(2,1)S(1)}, u32[]{:S(2)}, u32[]{:S(2)}) %collective-permute-start) | collective-permute-done | bytes 147488 | tf_op jit(solution)/shard_map/ppermute | solution.py:19
  20.3 0.4 fusion.41
  20.7 12.4 %collective-permute-start.1 = (bf16[2,2,6,6,512]{4,1,3,2,0:T(2,128)(2,1)S(1)}, bf16[2,2,6,6,512]{4,1,3,2,0:T(2,128)(2,1)S(1)}, u32[]{:S(2)}, u32[]{:S(2)}) collective-permute-start(bf16[2,2,6,6,512]{4,1,3,2,0:T(2,128)(2,1)S(1)} %get-tuple-element.13), channel_id=1, source_target_pairs={{8,0},{16,8},{24,16},{32,24},{40,32},{48,40},{56,48},{64,56},{72,6... | collective-permute-start | bytes 442376 | tf_op jit(solution)/shard_map/ppermute | solution.py:19
  33.1 0.1 broadcast_compare_fusion
  33.2 2.6 collective-permute-done.1
  35.8 0.2 fusion.57
  36.0 0.3 copy.41
  36.3 0.1 copy.44
  36.4 0.2 pad_maximum_fusion.3
  36.7 0.1 copy.43
  36.8 0.1 div.24
  36.9 0.3 convolution_convert_fusion.2
  37.2 0.8 copy.47
  38.1 1.9 fusion.35
  40.1 0.4 convolution_convert_fusion
  40.5 0.3 copy.45
  40.8 2.4 fusion.62
  43.2 1.9 fusion.36
  45.1 0.1 copy-done.4
  45.3 1.2 fusion.30
  46.5 5.3 %fusion.27 = bf16[1,144,1,16,32]{1,4,3,2,0:T(8,128)(2,1)} fusion(f32[16,144,144]{1,2,0:T(8,128)} %fusion.36, bf16[1,144,3,16,32]{1,4,3,2,0:T(8,128)(2,1)S(1)} %bitcast.76, f32[16,144,144]{1,2,0:T(8,128)} %get-tuple-element.21, f32[16,144]{1,0:T(8,128)S(1)} %get-tuple-element.20), kind=kOutput, calls=%fused_computation.22 | convolution fusion | flops 23632272 | bytes 9879552 | tf_op jit(solution)/shard_map/whqk,wkhe->wqhe/dot_general | solution.py:97
  51.8 5.3 %fusion.24 = bf16[1,144,1,16,32]{1,4,3,2,0:T(8,128)(2,1)} fusion(f32[16,144,144]{1,2,0:T(8,128)} %fusion.36, bf16[1,144,3,16,32]{1,4,3,2,0:T(8,128)(2,1)S(1)} %bitcast.77, f32[16,144,144]{1,2,0:T(8,128)} %get-tuple-element.21, f32[16,144]{1,0:T(8,128)S(1)} %get-tuple-element.20), kind=kOutput, calls=%fused_computation.21 | convolution fusion | flops 23632272 | bytes 9879552 | tf_op jit(solution)/shard_map/whqk,wqhe->wkhe/dot_general | solution.py:100
  57.1 0.4 multiply_convert_fusion.1
  57.5 1.3 pad_maximum_fusion
  58.8 2.3 fusion.44
  61.1 0.0 reduce-scatter.7.cloned.1.call-start
  61.2 0.8 fusion.56
  62.0 0.2 multiply_convert_fusion.2
  62.2 1.9 collective-permute-start.2
  64.1 4.6 %collective-permute-done.2 = bf16[2,3,12,512]{3,2,1,0:T(8,128)(2,1)S(1)} collective-permute-done((bf16[2,3,12,512]{3,2,1,0:T(8,128)(2,1)S(1)}, bf16[2,3,12,512]{3,2,1,0:T(8,128)(2,1)S(1)}, u32[]{:S(2)}, u32[]{:S(2)}) %collective-permute-start.2) | collective-permute-done | bytes 73760 | tf_op jit(solution)/shard_map/ppermute | solution.py:19
  68.8 1.9 collective-permute-start.3
  70.7 9.3 %collective-permute-done.3 = bf16[2,6,6,512]{3,2,1,0:T(8,128)(2,1)S(1)} collective-permute-done((bf16[2,6,6,512]{3,2,1,0:T(8,128)(2,1)S(1)}, bf16[2,6,6,512]{3,2,1,0:T(8,128)(2,1)S(1)}, u32[]{:S(2)}, u32[]{:S(2)}) %collective-permute-start.3) | collective-permute-done | bytes 73760 | tf_op jit(solution)/shard_map/ppermute | solution.py:19
  80.0 0.1 fusion.39
  80.1 132.3 %reduce-scatter.5.cloned.1.call-done = f32[8,1536]{1,0:T(8,128)} async-done(((f32[512,1536]{1,0:T(8,128)}), f32[8,1536]{1,0:T(8,128)}) %reduce-scatter.5.cloned.1.call-update) | async-done | bytes 49168 | tf_op jit(solution)/shard_map/reduce_scatter | solution.py:133
  212.4 0.8 convert_element_type.162
  213.2 0.9 copy.56
  214.2 0.8 copy.52
  215.0 37.8 %reduce-scatter.7.cloned.1.call-done = bf16[192,8]{1,0:T(8,128)(2,1)} async-done(((bf16[1536,8]{1,0:T(8,128)(2,1)}), bf16[192,8]{1,0:T(8,128)(2,1)}) %reduce-scatter.7.cloned.1.call-update) | async-done | bytes 3088
  252.8 0.8 copy.57
  253.7 0.6 convert_element_type.163
  (24 shorter events, 0.3 us)
Async XLA Ops:
  7.2 32.9 %copy-start = (bf16[512,1536]{1,0:T(8,128)(2,1)S(1)}, bf16[512,1536]{1,0:T(8,128)(2,1)}, u32[]{:S(2)}) copy-start(bf16[512,1536]{1,0:T(8,128)(2,1)} %param.6) | copy-start | bytes 4718596
  7.2 205.2 %reduce-scatter.5.cloned.1.call-start = ((), (), s32[]{:S(2)}) async-start(), calls=%async_computation.2 | async-start | bytes 3194880 | tf_op jit(solution)/shard_map/reduce_scatter | solution.py:133
  10.5 26.4 %copy-start.3 = (bf16[512,512]{1,0:T(8,128)(2,1)S(1)}, bf16[512,512]{1,0:T(8,128)(2,1)}, u32[]{:S(2)}) copy-start(bf16[512,512]{1,0:T(8,128)(2,1)} %param.7) | copy-start | bytes 1572868
  10.7 9.6 %collective-permute-start = (bf16[2,2,3,12,512]{4,1,3,2,0:T(2,128)(2,1)S(1)}, bf16[2,2,3,12,512]{4,1,3,2,0:T(2,128)(2,1)S(1)}, u32[]{:S(2)}, u32[]{:S(2)}) collective-permute-start(bf16[2,2,3,12,512]{4,1,3,2,0:T(2,128)(2,1)S(1)} %get-tuple-element.15), channel_id=1, source_target_pairs={{1,0},{2,1},{3,2},{4,3},{5,4},{6,5},{7,6},{0,7},{9,8},{10,9},{11,1... | collective-permute-start | bytes 442376 | tf_op jit(solution)/shard_map/ppermute | solution.py:19
  20.7 15.1 %collective-permute-start.1 = (bf16[2,2,6,6,512]{4,1,3,2,0:T(2,128)(2,1)S(1)}, bf16[2,2,6,6,512]{4,1,3,2,0:T(2,128)(2,1)S(1)}, u32[]{:S(2)}, u32[]{:S(2)}) collective-permute-start(bf16[2,2,6,6,512]{4,1,3,2,0:T(2,128)(2,1)S(1)} %get-tuple-element.13), channel_id=1, source_target_pairs={{8,0},{16,8},{24,16},{32,24},{40,32},{48,40},{56,48},{64,56},{72,6... | collective-permute-start | bytes 442376 | tf_op jit(solution)/shard_map/ppermute | solution.py:19
  40.8 2.4 copy-start.2
  43.2 2.1 copy-start.4
  61.1 191.7 %reduce-scatter.7.cloned.1.call-start = ((), (), s32[]{:S(2)}) async-start(), calls=%async_computation.3 | async-start | bytes 442368
  62.0 152.2 %copy-start.1 = (bf16[2,6,12,512]{3,0,2,1:T(2,128)(2,1)S(1)}, bf16[2,6,12,512]{3,0,2,1:T(2,128)(2,1)}, u32[]{:S(2)}) copy-start(bf16[2,6,12,512]{3,0,2,1:T(2,128)(2,1)} %param.5) | copy-start | bytes 442372
  62.2 6.5 %collective-permute-start.2 = (bf16[2,3,12,512]{3,2,1,0:T(8,128)(2,1)S(1)}, bf16[2,3,12,512]{3,2,1,0:T(8,128)(2,1)S(1)}, u32[]{:S(2)}, u32[]{:S(2)}) collective-permute-start(bf16[2,3,12,512]{3,2,1,0:T(8,128)(2,1)S(1)} %get-tuple-element.18), channel_id=1, source_target_pairs={{7,0},{0,1},{1,2},{2,3},{3,4},{4,5},{5,6},{6,7},{15,8},{8,9},{9,10... | collective-permute-start | bytes 221192 | tf_op jit(solution)/shard_map/ppermute | solution.py:19
  68.8 11.2 %collective-permute-start.3 = (bf16[2,6,6,512]{3,2,1,0:T(8,128)(2,1)S(1)}, bf16[2,6,6,512]{3,2,1,0:T(8,128)(2,1)S(1)}, u32[]{:S(2)}, u32[]{:S(2)}) collective-permute-start(bf16[2,6,6,512]{3,2,1,0:T(8,128)(2,1)S(1)} %fusion.49), channel_id=1, source_target_pairs={{504,0},{0,8},{8,16},{16,24},{24,32},{32,40},{40,48},{48,56},{56,6... | collective-permute-start | bytes 221192 | tf_op jit(solution)/shard_map/ppermute | solution.py:19
Sparse Core Ops, SparseCore 0:
  61.2 151.1 reduce-scatter.4
  215.4 37.3 reduce-scatter.6
where the time goes:
time: 264 us; the launch traced here: 261 us
  waiting for transfers between devices  193 us (73%)
  matrix products  20 us (8%)
  starting transfers between devices  19.1 us (7%)
  between operations  14.3 us (5%)
  other arithmetic  9.6 us (4%)
  local copies, waits for them, and re-layouts  4.97 us (2%)
    reduce_scatter x1, waiting for transfers between devices, per_device(): lax.psum_scatter(jnp.einsum('tc,tk->ck', flat_normed, d_proj, preferred_e...  132 us
    unnamed x3, waiting for transfers between devices  37.9 us
    ppermute x4, waiting for transfers between devices, shifted(): return lax.ppermute(block, axis, route)  23 us
    ppermute x4, starting transfers between devices, shifted(): return lax.ppermute(block, axis, route)  19 us
    dot_general x1, matrix products, window_pass(): jnp.einsum('whqk,wkhe->wqhe', d_low, key_heads, preferred_element_type=jn...  5.3 us
  transfers between devices with their start and end apart: 6, of which 6 were waited for; matrix products, arithmetic and copies ran while one was open for 1% of the time, Pallas kernels for 0%

commit v1 on v0

v1 whole, which is shorter than its diff:
```python
import functools

import jax
import jax.numpy as jnp
from jax import lax
from jax.experimental import pallas as pl
from jax.experimental.pallas import tpu as pltpu
from jax.sharding import Mesh, PartitionSpec as P

HEADS = 16
WIDTH = 512
HEAD_WIDTH = WIDTH // HEADS
QUAD = 18
PIECE = 2 * QUAD
TOKENS = 4 * PIECE
GROUP = 8
LANES = GROUP * HEAD_WIDTH
SPREAD = GROUP * TOKENS

EPS = 1e-05
NEG = -1e30
LON = ("zh", "y", "c")
LAT = ("zl", "x")
F32 = jnp.float32
BF16 = jnp.bfloat16

NT = (((1,), (1,)), ((), ()))
TN = (((0,), (0,)), ((), ()))


def dot(a, b, dims):
    return lax.dot_general(a, b, dims, preferred_element_type=F32)


def pack_kernel(tokens_ref, grads_ref, own_ref, lat_ref, lon_ref, diag_ref, hold_ref):
    outs = ((diag_ref, lat_ref), (lon_ref, own_ref))
    for half in range(2):
        for side in range(2):
            for array, ref in enumerate((tokens_ref, grads_ref)):
                for level in range(2):
                    for row in range(3):
                        block = ref[level, 3 * half + row].astype(F32)
                        start = array * PIECE + level * QUAD + row * 6
                        hold_ref[start:start + 6, :] = block[6 * side:6 * side + 6, :]
            outs[half][side][...] = hold_ref[...].astype(BF16)


def pack(tokens, grads):
    piece = jax.ShapeDtypeStruct((2 * PIECE, WIDTH), BF16)
    return pl.pallas_call(
        pack_kernel,
        out_shape=[piece] * 4,
        scratch_shapes=[pltpu.VMEM((2 * PIECE, WIDTH), F32)],
    )(tokens, grads)


def window_kernel(
    place_ref, own_ref, lon_ref, lat_ref, diag_ref, w_qkv_ref, w_proj_ref,
    d_own_ref, d_lon_ref, d_lat_ref, d_diag_ref, keep_ref, send_ref, d_qkv_ref,
):
    pieces = [ref[...].astype(F32) for ref in (own_ref, lon_ref, lat_ref, diag_ref)]
    values = jnp.concatenate([piece[:PIECE] for piece in pieces], axis=0)
    grads = jnp.concatenate([piece[PIECE:] for piece in pieces], axis=0).astype(BF16)
    means = jnp.mean(values, axis=-1, keepdims=True)
    centred = values - means
    inv_std = lax.rsqrt(jnp.mean(centred * centred, axis=-1, keepdims=True) + EPS)
    unit = centred * inv_std
    normed = unit.astype(BF16)
    w_qkv = w_qkv_ref[...]
    qkv = jnp.dot(normed, w_qkv, preferred_element_type=F32).astype(BF16)
    d_att = dot(grads, w_proj_ref[...], NT).astype(BF16)

    last = place_ref[0]

    def region(index):
        quad = index // PIECE
        level = (index - quad * PIECE) // QUAD
        return level + jnp.where(quad >= 2, 2 * last, 0)

    key_region = region(lax.broadcasted_iota(jnp.int32, (TOKENS, 1), 0))
    query_region = region(lax.broadcasted_iota(jnp.int32, (1, SPREAD), 1) % TOKENS)
    allowed = key_region == query_region
    column_head = lax.broadcasted_iota(jnp.int32, (1, LANES), 1) // HEAD_WIDTH
    masks = [(column_head == head).astype(F32).astype(BF16) for head in range(GROUP)]
    scaling = HEAD_WIDTH ** (-0.5)

    for group in range(HEADS // GROUP):
        part = slice(group * LANES, (group + 1) * LANES)
        queries = qkv[:, part]
        keys = qkv[:, WIDTH + group * LANES:WIDTH + (group + 1) * LANES]
        vals = qkv[:, 2 * WIDTH + group * LANES:2 * WIDTH + (group + 1) * LANES]
        outer = d_att[:, part]
        queries_spread = jnp.concatenate([queries * mask for mask in masks], axis=0)
        outer_spread = jnp.concatenate([outer * mask for mask in masks], axis=0)
        scores = dot(keys, queries_spread, NT) * scaling
        scores = jnp.where(allowed, scores, NEG)
        peak = jnp.max(scores, axis=0, keepdims=True)
        expo = jnp.exp(scores - peak)
        probs = expo * (1.0 / jnp.sum(expo, axis=0, keepdims=True))
        d_probs = dot(vals, outer_spread, NT)
        d_vals = jnp.dot(probs.astype(BF16), outer_spread, preferred_element_type=F32)
        inner = jnp.sum(probs * d_probs, axis=0, keepdims=True)
        d_scores = (probs * (d_probs - inner) * scaling).astype(BF16)
        d_keys = jnp.dot(d_scores, queries_spread, preferred_element_type=F32)
        d_queries_spread = dot(d_scores, keys, TN)
        d_queries = jnp.zeros((TOKENS, LANES), F32)
        for head in range(GROUP):
            rows = d_queries_spread[head * TOKENS:(head + 1) * TOKENS]
            d_queries = jnp.where(column_head == head, rows, d_queries)
        for where, block in ((0, d_queries), (1, d_keys), (2, d_vals)):
            start = where * WIDTH + group * LANES
            d_qkv_ref[:, start:start + LANES] = block.astype(BF16)

    d_qkv = d_qkv_ref[...]
    d_normed = dot(d_qkv, w_qkv, NT)
    d_inputs = inv_std * (
        d_normed
        - jnp.mean(d_normed, axis=-1, keepdims=True)
        - unit * jnp.mean(d_normed * unit, axis=-1, keepdims=True)
    )
    for index, ref in enumerate((d_own_ref, d_lon_ref, d_lat_ref, d_diag_ref)):
        ref[...] = d_inputs[index * PIECE:(index + 1) * PIECE].astype(BF16)

    left = lax.broadcasted_iota(jnp.int32, (128, 128), 1) < 64
    core = place_ref[1]

    def write(refs):
        for pair in range(4):
            block = dot(normed, d_qkv[:, pair * 384:(pair + 1) * 384], TN)
            block = block.reshape(32, 2, 8, 384)
            for parity in range(2):
                half = block[:, parity].reshape(256, 384)
                middle = half[:, 128:256]
                turned = pltpu.roll(middle, 64, 1)
                ref = refs[parity]
                ref[2 * pair, :256, :] = half[:, :128].astype(BF16)
                ref[2 * pair, 256:, :] = jnp.where(left, middle[:128], turned[128:]).astype(BF16)
                ref[2 * pair + 1, :256, :] = half[:, 256:].astype(BF16)
                ref[2 * pair + 1, 256:, :] = jnp.where(left, turned[:128], middle[128:]).astype(BF16)

    @pl.when(core == 0)
    def _():
        write((keep_ref, send_ref))

    @pl.when(core == 1)
    def _():
        write((send_ref, keep_ref))


def window_pass(place, own, lon, lat, diag, w_qkv, w_proj):
    piece = jax.ShapeDtypeStruct((PIECE, WIDTH), BF16)
    weight = jax.ShapeDtypeStruct((8, 384, 128), BF16)
    vmem = pl.BlockSpec(memory_space=pltpu.VMEM)
    return pl.pallas_call(
        window_kernel,
        out_shape=[piece] * 4 + [weight] * 2,
        in_specs=[pl.BlockSpec(memory_space=pltpu.SMEM)] + [vmem] * 6,
        out_specs=[vmem] * 6,
        scratch_shapes=[pltpu.VMEM((TOKENS, 3 * WIDTH), BF16)],
        compiler_params=pltpu.CompilerParams(vmem_limit_bytes=40 * 1024 * 1024),
    )(place, own, lon, lat, diag, w_qkv, w_proj)


def join_kernel(grads_ref, own_ref, lon_ref, lat_ref, diag_ref, out_ref, hold_ref):
    pieces = ((diag_ref, lat_ref), (lon_ref, own_ref))
    for half in range(2):
        sides = [ref[...].astype(F32) for ref in pieces[half]]
        for level in range(2):
            for row in range(3):
                start = level * QUAD + row * 6
                for side in range(2):
                    hold_ref[6 * side:6 * side + 6, :] = sides[side][start:start + 6]
                total = grads_ref[level, 3 * half + row].astype(F32) + hold_ref[...]
                out_ref[level, 3 * half + row] = total.astype(BF16)


def join(grads, own, lon, lat, diag):
    return pl.pallas_call(
        join_kernel,
        out_shape=jax.ShapeDtypeStruct(grads.shape, BF16),
        scratch_shapes=[pltpu.VMEM((12, WIDTH), F32)],
    )(grads, own, lon, lat, diag)


def columns_kernel(parts_ref, out_ref):
    total = parts_ref[0].astype(F32)
    for index in range(1, 8):
        total = total + parts_ref[index].astype(F32)
    out_ref[:, :, :128] = total[:256].reshape(32, 8, 128).astype(BF16)
    rest = total[256:]
    out_ref[:16, :, 128:] = rest[:, :64].reshape(16, 8, 64).astype(BF16)
    out_ref[16:, :, 128:] = pltpu.roll(rest, 64, 1)[:, :64].reshape(16, 8, 64).astype(BF16)


def columns(parts):
    return pl.pallas_call(
        columns_kernel, out_shape=jax.ShapeDtypeStruct((32, 8, 192), BF16)
    )(parts)


def turn(block, axes, distance):
    count = lax.axis_size(axes)
    return lax.ppermute(block, axes, [(i, (i + distance) % count) for i in range(count)])


def turn_both(block, distance):
    lons, lats = lax.axis_size(LON), lax.axis_size(LAT)
    route = [
        (i * lats + j, (i + distance) % lons * lats + (j + distance) % lats)
        for i in range(lons)
        for j in range(lats)
    ]
    return lax.ppermute(block, LON + LAT, route)


def per_device(tokens, cotangent, w_qkv, w_proj):
    place = jnp.stack((
        (lax.axis_index(LAT) == lax.axis_size(LAT) - 1).astype(jnp.int32),
        lax.axis_index("c"),
    ))
    own, to_lat, to_lon, to_diag = pack(tokens, cotangent)
    lat = turn(to_lat, LAT, -1)
    lon = turn(to_lon, LON, -1)
    diag = turn_both(to_diag, -1)
    d_own, d_lon, d_lat, d_diag, keep, send = window_pass(
        place, own, lon, lat, diag, w_qkv, w_proj
    )
    taken = lax.ppermute(send, "c", [(0, 1), (1, 0)])
    chip = (keep.astype(F32) + taken.astype(F32)).astype(BF16)
    by_columns = lax.all_to_all(chip, LAT, 0, 0)
    by_rows = lax.all_to_all(columns(by_columns), ("zh", "y"), 0, 0)
    d_weight = jnp.sum(by_rows.astype(F32), axis=0)
    odd = lax.axis_index("x") % 2 == 1
    d_weight = jnp.where(odd, jnp.roll(d_weight, 64, axis=1), d_weight)
    d_lat = turn(d_lat, LAT, 1)
    d_lon = turn(d_lon, LON, 1)
    d_diag = turn_both(d_diag, 1)
    return (join(cotangent, d_own, d_lon, d_lat, d_diag), d_weight)


def solution(mesh):
    cut = Mesh(mesh.devices.reshape(4, 8, 2, 2, 4), LON + LAT)
    grid = P(None, LAT, LON, None)
    return jax.shard_map(
        per_device, mesh=cut, in_specs=(grid, grid, P(), P()), out_specs=(grid, P(LON, LAT)),
        check_vma=False,
    )
```

time: 264 us -> 90.2 us (0.34)
  waiting for transfers between devices: 193 us -> 14.4 us
  matrix products: 20 us -> 0 us
  starting transfers between devices: 19.1 us -> 38 us
  blocking collectives: 0 us -> 16 us
  between operations: 14.3 us -> 0.78 us
  Pallas kernels: 0 us -> 9.75 us
  other arithmetic: 9.6 us -> 1 us
  local copies, waits for them, and re-layouts: 4.97 us -> 8.94 us
    reduce_scatter x1 -> x0, waiting for transfers between devices: 132 us -> none  [per_device(): lax.psum_scatter(jnp.einsum('tc,tk->ck', flat_normed, d_proj, preferred_e...]
    unnamed x3 -> x0, waiting for transfers between devices: 37.9 us -> none
    dot_general x8 -> x0, matrix products: 17.6 us -> none  [the longest x1 5.3 us: window_pass(): jnp.einsum('whqk,wkhe->wqhe', d_low, key_heads, preferred_element_type=jn...]
    all_to_all x0 -> x1, blocking collectives: none -> 16 us  [per_device(): by_columns = lax.all_to_all(chip, LAT, 0, 0)]
    ppermute x4 -> x7, starting transfers between devices: 19 us -> 30.6 us  [the longest x4 22.5 us: turn(): lax.ppermute(block, axes, [(i, (i + distance) % count) for i in range(cou...]
    pallas_call x0 -> x4, Pallas kernels: none -> 9.75 us  [the longest x1 4.32 us: window_pass(): pl.pallas_call(window_kernel, out_shape=[piece] * 4 + [weight] * 2, in_sp...]
    ppermute x4 -> x7, waiting for transfers between devices: 23 us -> 14.4 us  [the longest x2 8.66 us: turn_both(): return lax.ppermute(block, LON + LAT, route)]
    all_to_all x0 -> x1, starting transfers between devices: none -> 7.34 us  [per_device(): by_rows = lax.all_to_all(columns(by_columns), ('zh', 'y'), 0, 0)]
  transfers between devices with their start and end apart: 6 -> 8, of which waited for: 6 -> 4; matrix products, arithmetic and copies ran while one was open for 1% -> 2% of each run, Pallas kernels for 0% -> 2%
where the time goes in v1:
time: 90.2 us; the launch traced here: 88.9 us
  starting transfers between devices  38 us (42%)
  blocking collectives  16 us (18%)
  waiting for transfers between devices  14.4 us (16%)
  Pallas kernels  9.75 us (11%)
  local copies, waits for them, and re-layouts  8.94 us (10%)
  other arithmetic  1 us (1%)
    ppermute x4, starting transfers between devices, turn(): lax.ppermute(block, axes, [(i, (i + distance) % count) for i in range(cou...  22.5 us
    all_to_all x1, blocking collectives, per_device(): by_columns = lax.all_to_all(chip, LAT, 0, 0)  16 us
    unnamed x17, local copies, waits for them, and re-layouts  8.94 us
    ppermute x2, waiting for transfers between devices, turn_both(): return lax.ppermute(block, LON + LAT, route)  8.66 us
    all_to_all x1, starting transfers between devices, per_device(): by_rows = lax.all_to_all(columns(by_columns), ('zh', 'y'), 0, 0)  7.34 us
    ppermute x2, starting transfers between devices, turn_both(): return lax.ppermute(block, LON + LAT, route)  6.24 us
    pallas_call x1, Pallas kernels, window_pass(): pl.pallas_call(window_kernel, out_shape=[piece] * 4 + [weight] * 2, in_sp...  4.32 us
    ppermute x4, waiting for transfers between devices, turn(): lax.ppermute(block, axes, [(i, (i + distance) % count) for i in range(cou...  3.49 us
  transfers between devices with their start and end apart: 8, of which 4 were waited for; matrix products, arithmetic and copies ran while one was open for 2% of the time, Pallas kernels for 2%

profile of v1, /device:TPU:6, one launch (start us, length us, event | category | flops | bytes accessed | tf_op | source)
XLA Modules:
  0.0 88.9 jit_solution(8376570926301021628)
XLA Ops:
  0.6 1.6 %copy.8.grads_ref = bf16[2,6,12,512]{3,2,1,0:T(8,128)(2,1)} copy(bf16[2,6,12,512]{3,0,2,1:T(2,128)(2,1)} %param.5) | data formatting | bytes 294912 | tf_op args[1]
  2.3 1.6 %copy.6.tokens_ref = bf16[2,6,12,512]{3,2,1,0:T(8,128)(2,1)} copy(bf16[2,6,12,512]{3,0,2,1:T(2,128)(2,1)} %param.4) | data formatting | bytes 294912 | tf_op args[0]
  3.9 1.8 %shard_map.59 = (bf16[72,512]{1,0:T(8,128)(2,1)}, bf16[72,512]{1,0:T(8,128)(2,1)}, bf16[72,512]{1,0:T(8,128)(2,1)}, bf16[72,512]{1,0:T(8,128)(2,1)}) custom-call(bf16[2,6,12,512]{3,2,1,0:T(8,128)(2,1)} %copy.6.tokens_ref, bf16[2,6,12,512]{3,2,1,0:T(8,128)(2,1)} %copy.8.grads_ref), custom_call_target="tpu_custom_call" | custom-call | tf_op jit(solution)/shard_map/pallas_call | solution.py:50
  5.7 13.3 %collective-permute-start = (bf16[72,512]{1,0:T(8,128)(2,1)}, bf16[72,512]{1,0:T(8,128)(2,1)S(1)}, u32[]{:S(2)}, u32[]{:S(2)}) collective-permute-start(bf16[72,512]{1,0:T(8,128)(2,1)} %get-tuple-element.13), channel_id=1, source_target_pairs={{0,504},{8,0},{16,8},{24,16},{32,24},{40,32},{48,40},{56,48},{64,5... | collective-permute-start | bytes 221192 | tf_op jit(solution)/shard_map/ppermute | solution.py:203
  18.9 2.7 %collective-permute-start.1 = (bf16[72,512]{1,0:T(8,128)(2,1)}, bf16[72,512]{1,0:T(8,128)(2,1)S(1)}, u32[]{:S(2)}, u32[]{:S(2)}) collective-permute-start(bf16[72,512]{1,0:T(8,128)(2,1)} %get-tuple-element.14), channel_id=1, source_target_pairs={{0,7},{1,0},{2,1},{3,2},{4,3},{5,4},{6,5},{7,6},{8,15},{9,8},{10,9... | collective-permute-start | bytes 221192 | tf_op jit(solution)/shard_map/ppermute | solution.py:203
  21.7 2.3 %collective-permute-start.2 = (bf16[72,512]{1,0:T(8,128)(2,1)}, bf16[72,512]{1,0:T(8,128)(2,1)S(1)}, u32[]{:S(2)}, u32[]{:S(2)}) collective-permute-start(bf16[72,512]{1,0:T(8,128)(2,1)} %get-tuple-element.15), channel_id=1, source_target_pairs={{0,511},{1,504},{2,505},{3,506},{4,507},{5,508},{6,509},{7,510},{8... | collective-permute-start | bytes 221192 | tf_op jit(solution)/shard_map/ppermute | solution.py:213
  24.0 0.1 pad_add_fusion.place_ref
  24.0 0.0 collective-permute-done.lon_ref
  24.1 3.5 %collective-permute-done.1.lat_ref = bf16[72,512]{1,0:T(8,128)(2,1)S(1)} collective-permute-done((bf16[72,512]{1,0:T(8,128)(2,1)}, bf16[72,512]{1,0:T(8,128)(2,1)S(1)}, u32[]{:S(2)}, u32[]{:S(2)}) %collective-permute-start.1) | collective-permute-done | bytes 73760 | tf_op jit(solution)/shard_map/ppermute | solution.py:203
  27.5 2.2 %collective-permute-done.2.diag_ref = bf16[72,512]{1,0:T(8,128)(2,1)S(1)} collective-permute-done((bf16[72,512]{1,0:T(8,128)(2,1)}, bf16[72,512]{1,0:T(8,128)(2,1)S(1)}, u32[]{:S(2)}, u32[]{:S(2)}) %collective-permute-start.2) | collective-permute-done | bytes 73760 | tf_op jit(solution)/shard_map/ppermute | solution.py:213
  29.7 0.0 copy-start
  29.7 1.4 %copy-done = bf16[512,1536]{1,0:T(8,128)(2,1)S(1)} copy-done((bf16[512,1536]{1,0:T(8,128)(2,1)S(1)}, bf16[512,1536]{1,0:T(8,128)(2,1)}, u32[]{:S(2)}) %copy-start) | copy-done | bytes 1572888
  31.1 0.0 copy-start.1
  31.1 1.0 %copy-done.1 = bf16[512,512]{1,0:T(8,128)(2,1)S(1)} copy-done((bf16[512,512]{1,0:T(8,128)(2,1)S(1)}, bf16[512,512]{1,0:T(8,128)(2,1)}, u32[]{:S(2)}) %copy-start.1) | copy-done | bytes 524312
  32.1 0.0 copy-start.2
  32.1 0.9 copy-done.2
  33.0 4.3 %shard_map.60 = (bf16[36,512]{1,0:T(8,128)(2,1)S(1)}, bf16[36,512]{1,0:T(8,128)(2,1)S(1)}, bf16[36,512]{1,0:T(8,128)(2,1)S(1)}, bf16[36,512]{1,0:T(8,128)(2,1)S(...) custom-call(s32[2]{0:T(128)S(1)} %pad_add_fusion.place_ref, bf16[72,512]{1,0:T(8,128)(2,1)S(1)} %copy-done.2, ...), custom_call_target="tpu_custom_call" | custom-call | tf_op jit(solution)/shard_map/pallas_call | solution.py:154
  37.3 0.0 copy-start.3
  37.3 1.9 %collective-permute-start.6 = (bf16[8,384,128]{2,1,0:T(8,128)(2,1)S(1)}, bf16[8,384,128]{2,1,0:T(8,128)(2,1)S(1)}, u32[]{:S(2)}, u32[]{:S(2)}) collective-permute-start(bf16[8,384,128]{2,1,0:T(8,128)(2,1)S(1)} %get-tuple-element.21), channel_id=1, source_target_pairs={{0,8},{8,0},{1,9},{9,1},{2,10},{10,2},{3,11},{11,3},{4,12},{12,4},... | collective-permute-start | bytes 2359304 | tf_op jit(solution)/shard_map/ppermute | solution.py:228
  39.3 2.3 %collective-permute-done.6 = bf16[8,384,128]{2,1,0:T(8,128)(2,1)S(1)} collective-permute-done((bf16[8,384,128]{2,1,0:T(8,128)(2,1)S(1)}, bf16[8,384,128]{2,1,0:T(8,128)(2,1)S(1)}, u32[]{:S(2)}, u32[]{:S(2)}) %collective-permute-start.6) | collective-permute-done | bytes 786464 | tf_op jit(solution)/shard_map/ppermute | solution.py:228
  41.5 0.2 add_convert_fusion
  41.7 0.0 copy-done.3
  41.8 16.0 %all_to_all.10.parts_ref = bf16[8,384,128]{2,1,0:T(8,128)(2,1)} all-to-all(bf16[8,384,128]{2,1,0:T(8,128)(2,1)S(1)} %add_convert_fusion), channel_id=1, replica_groups=mesh['zh'=4,'y'=8,'c'=2,'zl'=2,'x'=4] {'zl','x'}, dimensions={0} | all-to-all | bytes 1572864 | tf_op jit(solution)/shard_map/all_to_all | solution.py:230
  57.8 1.9 %shard_map.62 = bf16[32,8,192]{2,1,0:T(8,128)(2,1)} custom-call(bf16[8,384,128]{2,1,0:T(8,128)(2,1)} %all_to_all.10.parts_ref), custom_call_target="tpu_custom_call" | custom-call | tf_op jit(solution)/shard_map/pallas_call | solution.py:196
  59.7 7.3 %all-to-all-start.1 = ((bf16[32,8,192]{2,1,0:T(8,128)(2,1)}), bf16[32,8,192]{2,1,0:T(8,128)(2,1)S(1)}, u32[]{:S(2)}, u32[]{:S(2)}) async-start(bf16[32,8,192]{2,1,0:T(8,128)(2,1)} %shard_map.62), calls=%async_computation.1 | async-start | bytes 262144 | tf_op jit(solution)/shard_map/all_to_all | solution.py:231
  67.0 1.9 %collective-permute-start.3 = (bf16[36,512]{1,0:T(8,128)(2,1)S(1)}, bf16[36,512]{1,0:T(8,128)(2,1)S(1)}, u32[]{:S(2)}, u32[]{:S(2)}) collective-permute-start(bf16[36,512]{1,0:T(8,128)(2,1)S(1)} %get-tuple-element.17), channel_id=1, source_target_pairs={{0,8},{8,16},{16,24},{24,32},{32,40},{40,48},{48,56},{56,64},{64,7... | collective-permute-start | bytes 110600 | tf_op jit(solution)/shard_map/ppermute | solution.py:203
  69.0 4.5 %collective-permute-start.4 = (bf16[36,512]{1,0:T(8,128)(2,1)S(1)}, bf16[36,512]{1,0:T(8,128)(2,1)S(1)}, u32[]{:S(2)}, u32[]{:S(2)}) collective-permute-start(bf16[36,512]{1,0:T(8,128)(2,1)S(1)} %get-tuple-element.18), channel_id=1, source_target_pairs={{0,1},{1,2},{2,3},{3,4},{4,5},{5,6},{6,7},{7,0},{8,9},{9,10},{10,1... | collective-permute-start | bytes 110600 | tf_op jit(solution)/shard_map/ppermute | solution.py:203
  73.5 4.0 %collective-permute-start.5 = (bf16[36,512]{1,0:T(8,128)(2,1)S(1)}, bf16[36,512]{1,0:T(8,128)(2,1)S(1)}, u32[]{:S(2)}, u32[]{:S(2)}) collective-permute-start(bf16[36,512]{1,0:T(8,128)(2,1)S(1)} %get-tuple-element.19), channel_id=1, source_target_pairs={{0,9},{1,10},{2,11},{3,12},{4,13},{5,14},{6,15},{7,8},{8,17},{9,18... | collective-permute-start | bytes 110600 | tf_op jit(solution)/shard_map/ppermute | solution.py:213
  77.5 0.0 collective-permute-done.3.lon_ref
  77.5 0.0 copy-start.4
  77.5 0.0 collective-permute-done.4.lat_ref
  77.5 0.0 copy-start.5
  77.5 6.5 %collective-permute-done.5.diag_ref = bf16[36,512]{1,0:T(8,128)(2,1)S(1)} collective-permute-done((bf16[36,512]{1,0:T(8,128)(2,1)S(1)}, bf16[36,512]{1,0:T(8,128)(2,1)S(1)}, u32[]{:S(2)}, u32[]{:S(2)}) %collective-permute-start.5) | collective-permute-done | bytes 36896 | tf_op jit(solution)/shard_map/ppermute | solution.py:213
  84.0 0.0 copy-start.6
  84.0 0.0 copy-done.4
  84.0 0.0 copy-done.5
  84.0 0.6 copy-done.6
  84.7 1.8 %shard_map.61 = bf16[2,6,12,512]{3,2,1,0:T(8,128)(2,1)} custom-call(bf16[2,6,12,512]{3,2,1,0:T(8,128)(2,1)} %copy.8.grads_ref, bf16[36,512]{1,0:T(8,128)(2,1)} %copy-done.3, bf16[36,512]{1,0:T(8,128)(2,1)} %copy-done.4, bf16[36,512]{1,0:T(8,128)(2,1)} %copy-done.5, bf16[36,512]{1,0:T(8,128)(2,1)} %copy-done.6), custom_call_target="tpu_custom_call" | custom-call | tf_op jit(solution)/shard_map/pallas_call | solution.py:178
  86.4 1.7 %copy.9 = bf16[2,6,12,512]{3,0,2,1:T(2,128)(2,1)} copy(bf16[2,6,12,512]{3,2,1,0:T(8,128)(2,1)} %shard_map.61) | data formatting | bytes 294912
  88.1 0.0 all-to-all-done.1
  88.2 0.7 maximum_select_fusion
  (3 shorter events, 0.0 us)
Async XLA Ops:
  5.7 18.4 %collective-permute-start = (bf16[72,512]{1,0:T(8,128)(2,1)}, bf16[72,512]{1,0:T(8,128)(2,1)S(1)}, u32[]{:S(2)}, u32[]{:S(2)}) collective-permute-start(bf16[72,512]{1,0:T(8,128)(2,1)} %get-tuple-element.13), channel_id=1, source_target_pairs={{0,504},{8,0},{16,8},{24,16},{32,24},{40,32},{48,40},{56,48},{64,5... | collective-permute-start | bytes 221192 | tf_op jit(solution)/shard_map/ppermute | solution.py:203
  18.9 8.6 %collective-permute-start.1 = (bf16[72,512]{1,0:T(8,128)(2,1)}, bf16[72,512]{1,0:T(8,128)(2,1)S(1)}, u32[]{:S(2)}, u32[]{:S(2)}) collective-permute-start(bf16[72,512]{1,0:T(8,128)(2,1)} %get-tuple-element.14), channel_id=1, source_target_pairs={{0,7},{1,0},{2,1},{3,2},{4,3},{5,4},{6,5},{7,6},{8,15},{9,8},{10,9... | collective-permute-start | bytes 221192 | tf_op jit(solution)/shard_map/ppermute | solution.py:203
  21.7 8.0 %collective-permute-start.2 = (bf16[72,512]{1,0:T(8,128)(2,1)}, bf16[72,512]{1,0:T(8,128)(2,1)S(1)}, u32[]{:S(2)}, u32[]{:S(2)}) collective-permute-start(bf16[72,512]{1,0:T(8,128)(2,1)} %get-tuple-element.15), channel_id=1, source_target_pairs={{0,511},{1,504},{2,505},{3,506},{4,507},{5,508},{6,509},{7,510},{8... | collective-permute-start | bytes 221192 | tf_op jit(solution)/shard_map/ppermute | solution.py:213
  29.7 1.4 %copy-start = (bf16[512,1536]{1,0:T(8,128)(2,1)S(1)}, bf16[512,1536]{1,0:T(8,128)(2,1)}, u32[]{:S(2)}) copy-start(bf16[512,1536]{1,0:T(8,128)(2,1)} %w_qkv_ref.1) | copy-start | bytes 4718596
  31.1 1.0 %copy-start.1 = (bf16[512,512]{1,0:T(8,128)(2,1)S(1)}, bf16[512,512]{1,0:T(8,128)(2,1)}, u32[]{:S(2)}) copy-start(bf16[512,512]{1,0:T(8,128)(2,1)} %w_proj_ref.1) | copy-start | bytes 1572868
  32.1 0.9 copy-start.2
  37.3 4.4 %copy-start.3 = (bf16[36,512]{1,0:T(8,128)(2,1)}, bf16[36,512]{1,0:T(8,128)(2,1)S(1)}, u32[]{:S(2)}) copy-start(bf16[36,512]{1,0:T(8,128)(2,1)S(1)} %get-tuple-element.16.own_ref) | copy-start | bytes 110596
  37.3 4.2 %collective-permute-start.6 = (bf16[8,384,128]{2,1,0:T(8,128)(2,1)S(1)}, bf16[8,384,128]{2,1,0:T(8,128)(2,1)S(1)}, u32[]{:S(2)}, u32[]{:S(2)}) collective-permute-start(bf16[8,384,128]{2,1,0:T(8,128)(2,1)S(1)} %get-tuple-element.21), channel_id=1, source_target_pairs={{0,8},{8,0},{1,9},{9,1},{2,10},{10,2},{3,11},{11,3},{4,12},{12,4},... | collective-permute-start | bytes 2359304 | tf_op jit(solution)/shard_map/ppermute | solution.py:228
  59.7 28.5 %all-to-all-start.1 = ((bf16[32,8,192]{2,1,0:T(8,128)(2,1)}), bf16[32,8,192]{2,1,0:T(8,128)(2,1)S(1)}, u32[]{:S(2)}, u32[]{:S(2)}) async-start(bf16[32,8,192]{2,1,0:T(8,128)(2,1)} %shard_map.62), calls=%async_computation.1 | async-start | bytes 262144 | tf_op jit(solution)/shard_map/all_to_all | solution.py:231
  67.0 10.5 %collective-permute-start.3 = (bf16[36,512]{1,0:T(8,128)(2,1)S(1)}, bf16[36,512]{1,0:T(8,128)(2,1)S(1)}, u32[]{:S(2)}, u32[]{:S(2)}) collective-permute-start(bf16[36,512]{1,0:T(8,128)(2,1)S(1)} %get-tuple-element.17), channel_id=1, source_target_pairs={{0,8},{8,16},{16,24},{24,32},{32,40},{40,48},{48,56},{56,64},{64,7... | collective-permute-start | bytes 110600 | tf_op jit(solution)/shard_map/ppermute | solution.py:203
  69.0 8.6 %collective-permute-start.4 = (bf16[36,512]{1,0:T(8,128)(2,1)S(1)}, bf16[36,512]{1,0:T(8,128)(2,1)S(1)}, u32[]{:S(2)}, u32[]{:S(2)}) collective-permute-start(bf16[36,512]{1,0:T(8,128)(2,1)S(1)} %get-tuple-element.18), channel_id=1, source_target_pairs={{0,1},{1,2},{2,3},{3,4},{4,5},{5,6},{6,7},{7,0},{8,9},{9,10},{10,1... | collective-permute-start | bytes 110600 | tf_op jit(solution)/shard_map/ppermute | solution.py:203
  73.5 10.5 %collective-permute-start.5 = (bf16[36,512]{1,0:T(8,128)(2,1)S(1)}, bf16[36,512]{1,0:T(8,128)(2,1)S(1)}, u32[]{:S(2)}, u32[]{:S(2)}) collective-permute-start(bf16[36,512]{1,0:T(8,128)(2,1)S(1)} %get-tuple-element.19), channel_id=1, source_target_pairs={{0,9},{1,10},{2,11},{3,12},{4,13},{5,14},{6,15},{7,8},{8,17},{9,18... | collective-permute-start | bytes 110600 | tf_op jit(solution)/shard_map/ppermute | solution.py:213
  77.5 6.5 %copy-start.4 = (bf16[36,512]{1,0:T(8,128)(2,1)}, bf16[36,512]{1,0:T(8,128)(2,1)S(1)}, u32[]{:S(2)}) copy-start(bf16[36,512]{1,0:T(8,128)(2,1)S(1)} %collective-permute-done.3.lon_ref) | copy-start | bytes 110596
  77.5 6.5 %copy-start.5 = (bf16[36,512]{1,0:T(8,128)(2,1)}, bf16[36,512]{1,0:T(8,128)(2,1)S(1)}, u32[]{:S(2)}) copy-start(bf16[36,512]{1,0:T(8,128)(2,1)S(1)} %collective-permute-done.4.lat_ref) | copy-start | bytes 110596
  84.0 0.6 copy-start.6

commit v2 on v1

v2 whole, which is shorter than its diff:
```python
import functools

import jax
import jax.numpy as jnp
from jax import lax
from jax.experimental import pallas as pl
from jax.experimental.pallas import tpu as pltpu
from jax.sharding import Mesh, PartitionSpec as P

HEADS = 16
WIDTH = 512
HEAD_WIDTH = WIDTH // HEADS
QUAD = 18
PIECE = 2 * QUAD
TOKENS = 4 * PIECE
GROUP = 8
LANES = GROUP * HEAD_WIDTH
SPREAD = GROUP * TOKENS
VMEM = 60 * 1024 * 1024
WINDOW_VMEM = 54656 * 1024
SMALL = pltpu.CompilerParams(vmem_limit_bytes=8 * 1024 * 1024)

EPS = 1e-05
NEG = -1e30
LON = ("zh", "y", "c")
LAT = ("zl", "x")
F32 = jnp.float32
BF16 = jnp.bfloat16

NT = (((1,), (1,)), ((), ()))
TN = (((0,), (0,)), ((), ()))


def dot(a, b, dims):
    return lax.dot_general(a, b, dims, preferred_element_type=F32)


def split_kernel(tokens_ref, grads_ref, own_ref, lat_ref, lon_ref, diag_ref, sems):
    copies = []
    for ref, rows, side in (
        (lat_ref, 0, 6), (lon_ref, 3, 0), (diag_ref, 0, 0), (own_ref, 3, 6)
    ):
        for array, source in enumerate((tokens_ref, grads_ref)):
            copies.append(pltpu.make_async_copy(
                source.at[rows:rows + 3, side:side + 6], ref.at[array], sems.at[len(copies)]
            ))
    for copy in copies:
        copy.start()
    for copy in copies:
        copy.wait()


def split(tokens, grads):
    anywhere = pl.BlockSpec(memory_space=pl.ANY)
    return pl.pallas_call(
        split_kernel,
        out_shape=[jax.ShapeDtypeStruct((2, 3, 6, 2, WIDTH), BF16)] * 4,
        in_specs=[anywhere] * 2,
        out_specs=[anywhere] * 4,
        scratch_shapes=[pltpu.SemaphoreType.DMA((8,))],
        compiler_params=pltpu.CompilerParams(vmem_limit_bytes=VMEM),
    )(tokens, grads)


def window_kernel(
    place_ref, own_ref, lon_ref, lat_ref, diag_ref, w_qkv_in, w_proj_in,
    d_own_ref, d_lon_ref, d_lat_ref, d_diag_ref, keep_ref, send_ref,
    d_qkv_ref, piece_ref, w_qkv_ref, w_proj_ref, weight_ref, load_sems, store_sems,
):
    loads = [
        (own_ref, piece_ref.at[0]),
        (lon_ref, piece_ref.at[1]),
        (lat_ref, piece_ref.at[2]),
        (diag_ref, piece_ref.at[3]),
        (w_qkv_in, w_qkv_ref),
        (w_proj_in, w_proj_ref),
    ]
    loads = [
        pltpu.make_async_copy(source, target, load_sems.at[index])
        for index, (source, target) in enumerate(loads)
    ]
    for load in loads:
        load.start()
    for load in loads[:4]:
        load.wait()
    pieces = [
        [piece_ref[quad, array].astype(F32).reshape(PIECE, WIDTH) for array in range(2)]
        for quad in range(4)
    ]
    values = jnp.concatenate([piece[0] for piece in pieces], axis=0)
    grads = jnp.concatenate([piece[1] for piece in pieces], axis=0).astype(BF16)
    means = jnp.mean(values, axis=-1, keepdims=True)
    centred = values - means
    inv_std = lax.rsqrt(jnp.mean(centred * centred, axis=-1, keepdims=True) + EPS)
    unit = centred * inv_std
    normed = unit.astype(BF16)
    loads[4].wait()
    w_qkv = w_qkv_ref[...]
    qkv = jnp.dot(normed, w_qkv, preferred_element_type=F32).astype(BF16)
    loads[5].wait()
    d_att = dot(grads, w_proj_ref[...], NT).astype(BF16)

    last = place_ref[0]

    def region(index):
        quad = index // PIECE
        level = index % 2
        return level + jnp.where(quad >= 2, 2 * last, 0)

    key_region = region(lax.broadcasted_iota(jnp.int32, (TOKENS, 1), 0))
    query_region = region(lax.broadcasted_iota(jnp.int32, (1, SPREAD), 1) % TOKENS)
    allowed = key_region == query_region
    column_head = lax.broadcasted_iota(jnp.int32, (1, LANES), 1) // HEAD_WIDTH
    masks = [(column_head == head).astype(F32).astype(BF16) for head in range(GROUP)]
    scaling = HEAD_WIDTH ** (-0.5)

    for group in range(HEADS // GROUP):
        part = slice(group * LANES, (group + 1) * LANES)
        queries = qkv[:, part]
        keys = qkv[:, WIDTH + group * LANES:WIDTH + (group + 1) * LANES]
        vals = qkv[:, 2 * WIDTH + group * LANES:2 * WIDTH + (group + 1) * LANES]
        outer = d_att[:, part]
        queries_spread = jnp.concatenate([queries * mask for mask in masks], axis=0)
        outer_spread = jnp.concatenate([outer * mask for mask in masks], axis=0)
        scores = dot(keys, queries_spread, NT) * scaling
        scores = jnp.where(allowed, scores, NEG)
        peak = jnp.max(scores, axis=0, keepdims=True)
        expo = jnp.exp(scores - peak)
        probs = expo * (1.0 / jnp.sum(expo, axis=0, keepdims=True))
        d_probs = dot(vals, outer_spread, NT)
        d_vals = jnp.dot(probs.astype(BF16), outer_spread, preferred_element_type=F32)
        inner = jnp.sum(probs * d_probs, axis=0, keepdims=True)
        d_scores = (probs * (d_probs - inner) * scaling).astype(BF16)
        d_keys = jnp.dot(d_scores, queries_spread, preferred_element_type=F32)
        d_queries_spread = dot(d_scores, keys, TN)
        d_queries = jnp.zeros((TOKENS, LANES), F32)
        for head in range(GROUP):
            rows = d_queries_spread[head * TOKENS:(head + 1) * TOKENS]
            d_queries = jnp.where(column_head == head, rows, d_queries)
        for where, block in ((0, d_queries), (1, d_keys), (2, d_vals)):
            start = where * WIDTH + group * LANES
            d_qkv_ref[:, start:start + LANES] = block.astype(BF16)

    d_qkv = d_qkv_ref[...]
    left = lax.broadcasted_iota(jnp.int32, (128, 128), 1) < 64
    core = place_ref[1]
    for pair in range(4):
        block = dot(normed, d_qkv[:, pair * 384:(pair + 1) * 384], TN).reshape(32, 2, 8, 384)
        for parity in range(2):
            half = block[:, parity].reshape(256, 384)
            middle = half[:, 128:256]
            turned = pltpu.roll(middle, 64, 1)
            ref = weight_ref.at[parity]
            ref[2 * pair, :256, :] = half[:, :128].astype(BF16)
            ref[2 * pair, 256:, :] = jnp.where(left, middle[:128], turned[128:]).astype(BF16)
            ref[2 * pair + 1, :256, :] = half[:, 256:].astype(BF16)
            ref[2 * pair + 1, 256:, :] = jnp.where(left, turned[:128], middle[128:]).astype(BF16)

    def stores(kept):
        return [
            pltpu.make_async_copy(weight_ref.at[parity], ref, store_sems.at[index])
            for index, (parity, ref) in enumerate(((kept, keep_ref), (1 - kept, send_ref)))
        ]

    for store in stores(core):
        store.start()
    d_normed = dot(d_qkv, w_qkv, NT)
    d_inputs = inv_std * (
        d_normed
        - jnp.mean(d_normed, axis=-1, keepdims=True)
        - unit * jnp.mean(d_normed * unit, axis=-1, keepdims=True)
    )
    for index, ref in enumerate((d_own_ref, d_lon_ref, d_lat_ref, d_diag_ref)):
        block = d_inputs[index * PIECE:(index + 1) * PIECE]
        ref[...] = block.reshape(3, 6, 2, WIDTH).astype(BF16)

    for store in stores(core):
        store.wait()


def window_pass(place, own, lon, lat, diag, w_qkv, w_proj):
    piece = jax.ShapeDtypeStruct((3, 6, 2, WIDTH), BF16)
    weight = jax.ShapeDtypeStruct((8, 384, 128), BF16)
    anywhere = pl.BlockSpec(memory_space=pl.ANY)
    return pl.pallas_call(
        window_kernel,
        out_shape=[piece] * 4 + [weight] * 2,
        in_specs=[pl.BlockSpec(memory_space=pltpu.SMEM)] + [anywhere] * 6,
        out_specs=[pl.BlockSpec(memory_space=pltpu.VMEM)] * 4 + [anywhere] * 2,
        scratch_shapes=[
            pltpu.VMEM((TOKENS, 3 * WIDTH), BF16),
            pltpu.VMEM((4, 2, 3, 6, 2, WIDTH), BF16),
            pltpu.VMEM(w_qkv.shape, BF16),
            pltpu.VMEM(w_proj.shape, BF16),
            pltpu.VMEM((2, 8, 384, 128), BF16),
            pltpu.SemaphoreType.DMA((6,)),
            pltpu.SemaphoreType.DMA((2,)),
        ],
        compiler_params=pltpu.CompilerParams(vmem_limit_bytes=WINDOW_VMEM),
    )(place, own, lon, lat, diag, w_qkv, w_proj)


def add_kernel(keep_ref, taken_ref, lon_ref, lat_ref, diag_ref, out_ref, *passed):
    out_ref[...] = (keep_ref[...].astype(F32) + taken_ref[...].astype(F32)).astype(BF16)


def add(keep, taken, *grads):
    vmem = pl.BlockSpec(memory_space=pltpu.VMEM)
    anywhere = pl.BlockSpec(memory_space=pl.ANY)
    return pl.pallas_call(
        add_kernel,
        out_shape=[jax.ShapeDtypeStruct(a.shape, a.dtype) for a in (keep,) + grads],
        in_specs=[vmem] * 2 + [anywhere] * 3,
        out_specs=[vmem] + [anywhere] * 3,
        input_output_aliases={2: 1, 3: 2, 4: 3},
        compiler_params=SMALL,
    )(keep, taken, *grads)


def join_kernel(grads_ref, own_ref, lon_ref, lat_ref, diag_ref, rows_ref, out_ref):
    for ref, rows, side in (
        (diag_ref, 0, 0), (lat_ref, 0, 6), (lon_ref, 3, 0), (own_ref, 3, 6)
    ):
        block = grads_ref[rows:rows + 3, side:side + 6].astype(F32)
        out_ref[rows:rows + 3, side:side + 6] = (block + ref[...].astype(F32)).astype(BF16)


def join(grads, own, lon, lat, diag, rows):
    vmem = pl.BlockSpec(memory_space=pltpu.VMEM)
    return pl.pallas_call(
        join_kernel,
        out_shape=jax.ShapeDtypeStruct(grads.shape, BF16),
        in_specs=[vmem] * 5 + [pl.BlockSpec(memory_space=pl.ANY)],
        out_specs=vmem,
        compiler_params=SMALL,
    )(grads, own, lon, lat, diag, rows)


def columns_kernel(parts_ref, lon_ref, lat_ref, diag_ref, out_ref):
    total = parts_ref[0].astype(F32)
    for index in range(1, 8):
        total = total + parts_ref[index].astype(F32)
    out_ref[:, :, :128] = total[:256].reshape(32, 8, 128).astype(BF16)
    rest = total[256:]
    out_ref[:16, :, 128:] = rest[:, :64].reshape(16, 8, 64).astype(BF16)
    out_ref[16:, :, 128:] = pltpu.roll(rest, 64, 1)[:, :64].reshape(16, 8, 64).astype(BF16)


def columns(parts, *grads):
    return pl.pallas_call(
        columns_kernel,
        out_shape=jax.ShapeDtypeStruct((32, 8, 192), BF16),
        in_specs=[pl.BlockSpec(memory_space=pltpu.VMEM)]
        + [pl.BlockSpec(memory_space=pl.ANY)] * 3,
        compiler_params=SMALL,
    )(parts, *grads)


def turn(block, axes, distance):
    count = lax.axis_size(axes)
    return lax.ppermute(block, axes, [(i, (i + distance) % count) for i in range(count)])


def turn_both(block, distance):
    lons, lats = lax.axis_size(LON), lax.axis_size(LAT)
    route = [
        (i * lats + j, (i + distance) % lons * lats + (j + distance) % lats)
        for i in range(lons)
        for j in range(lats)
    ]
    return lax.ppermute(block, LON + LAT, route)


def per_device(tokens, cotangent, w_qkv, w_proj):
    place = jnp.stack((
        (lax.axis_index(LAT) == lax.axis_size(LAT) - 1).astype(jnp.int32),
        lax.axis_index("c"),
    ))
    tokens = jnp.transpose(tokens, (1, 2, 0, 3))
    cotangent = jnp.transpose(cotangent, (1, 2, 0, 3))
    own, to_lat, to_lon, to_diag = split(tokens, cotangent)
    lat = turn(to_lat, LAT, -1)
    lon = turn(to_lon, LON, -1)
    diag = turn_both(to_diag, -1)
    d_own, d_lon, d_lat, d_diag, keep, send = window_pass(
        place, own, lon, lat, diag, w_qkv, w_proj
    )
    taken = lax.ppermute(send, "c", [(0, 1), (1, 0)])
    chip, d_lon, d_lat, d_diag = add(keep, taken, d_lon, d_lat, d_diag)
    by_columns = lax.all_to_all(chip, LAT, 0, 0)
    d_lat = turn(d_lat, LAT, 1)
    d_lon = turn(d_lon, LON, 1)
    d_diag = turn_both(d_diag, 1)
    rows = columns(by_columns, d_lon, d_lat, d_diag)
    by_rows = lax.all_to_all(rows, ("zh", "y"), 0, 0)
    d_tokens = join(cotangent, d_own, d_lon, d_lat, d_diag, rows)
    d_weight = jnp.sum(by_rows.astype(F32), axis=0)
    odd = lax.axis_index("x") % 2 == 1
    d_weight = jnp.where(odd, jnp.roll(d_weight, 64, axis=1), d_weight)
    return (jnp.transpose(d_tokens, (2, 0, 1, 3)), d_weight)


def solution(mesh):
    cut = Mesh(mesh.devices.reshape(4, 8, 2, 2, 4), LON + LAT)
    grid = P(None, LAT, LON, None)
    return jax.shard_map(
        per_device, mesh=cut, in_specs=(grid, grid, P(), P()), out_specs=(grid, P(LON, LAT)),
        check_vma=False,
    )
```

time: 90.2 us -> 91.9 us (1.019)
  the two profiles are of different devices: /device:TPU:6 before, /device:TPU:8 now
where the time goes in v2:
time: 91.9 us; the launch traced here: 91.3 us
  starting transfers between devices  40.5 us (44%)
  waiting for transfers between devices  27.2 us (30%)
  Pallas kernels  20.1 us (22%)
  local copies, waits for them, and re-layouts  2.03 us (2%)
    ppermute x4, starting transfers between devices, turn(): lax.ppermute(block, axes, [(i, (i + distance) % count) for i in range(cou...  14.2 us
    all_to_all x1, starting transfers between devices, per_device(): by_rows = lax.all_to_all(rows, ('zh', 'y'), 0, 0)  12 us
    all_to_all x1, waiting for transfers between devices, per_device(): by_rows = lax.all_to_all(rows, ('zh', 'y'), 0, 0)  11.7 us
    pallas_call x1, Pallas kernels, split(): pl.pallas_call(split_kernel, out_shape=[jax.ShapeDtypeStruct((2, 3, 6, 2,...  10.1 us
    ppermute x2, waiting for transfers between devices, turn_both(): return lax.ppermute(block, LON + LAT, route)  9.38 us
    pallas_call x1, Pallas kernels, window_pass(): pl.pallas_call(window_kernel, out_shape=[piece] * 4 + [weight] * 2, in_sp...  7.28 us
    ppermute x2, starting transfers between devices, turn_both(): return lax.ppermute(block, LON + LAT, route)  6.82 us
    all_to_all x1, starting transfers between devices, per_device(): by_columns = lax.all_to_all(chip, LAT, 0, 0)  4.36 us
  transfers between devices with their start and end apart: 9, of which 6 were waited for; matrix products, arithmetic and copies ran while one was open for 0% of the time, Pallas kernels for 1%

profile of v2, /device:TPU:8, one launch (start us, length us, event | category | flops | bytes accessed | tf_op | source)
XLA Modules:
  0.0 91.3 jit_solution(4538097310585261594)
XLA Ops:
  0.6 10.1 %shard_map.59 = (bf16[2,3,6,2,512]{4,3,2,1,0:T(2,128)(2,1)}, bf16[2,3,6,2,512]{4,3,2,1,0:T(2,128)(2,1)}, bf16[2,3,6,2,512]{4,3,2,1,0:T(2,128)(2,1)}, bf16[2,3,6,2,512]{4,3,2,1,0:T(2,128)(2,1)}) custom-call(bf16[6,12,2,512]{3,2,1,0:T(2,128)(2,1)} %bitcast.8, bf16[6,12,2,512]{3,2,1,0:T(2,128)(2,1)} %bitcast.5), custom_call_target="tpu_custom_call" | custom-call | tf_op jit(solution)/shard_map/pallas_call | solution.py:55
  10.7 1.9 %collective-permute-start = (bf16[2,3,6,2,512]{4,3,2,1,0:T(2,128)(2,1)}, bf16[2,3,6,2,512]{4,3,2,1,0:T(2,128)(2,1)S(1)}, u32[]{:S(2)}, u32[]{:S(2)}) collective-permute-start(bf16[2,3,6,2,512]{4,3,2,1,0:T(2,128)(2,1)} %get-tuple-element.17), channel_id=1, source_target_pairs={{0,504},{8,0},{16,8},{24,16},{32,24},{40,32},{48,40},{56,48},{64,5... | collective-permute-start | bytes 221192 | tf_op jit(solution)/shard_map/ppermute | solution.py:261
  12.7 6.5 %collective-permute-start.1 = (bf16[2,3,6,2,512]{4,3,2,1,0:T(2,128)(2,1)}, bf16[2,3,6,2,512]{4,3,2,1,0:T(2,128)(2,1)S(1)}, u32[]{:S(2)}, u32[]{:S(2)}) collective-permute-start(bf16[2,3,6,2,512]{4,3,2,1,0:T(2,128)(2,1)} %get-tuple-element.18), channel_id=1, source_target_pairs={{0,7},{1,0},{2,1},{3,2},{4,3},{5,4},{6,5},{7,6},{8,15},{9,8},{10,9... | collective-permute-start | bytes 221192 | tf_op jit(solution)/shard_map/ppermute | solution.py:261
  19.2 2.4 %collective-permute-start.2 = (bf16[2,3,6,2,512]{4,3,2,1,0:T(2,128)(2,1)}, bf16[2,3,6,2,512]{4,3,2,1,0:T(2,128)(2,1)S(1)}, u32[]{:S(2)}, u32[]{:S(2)}) collective-permute-start(bf16[2,3,6,2,512]{4,3,2,1,0:T(2,128)(2,1)} %get-tuple-element.19), channel_id=1, source_target_pairs={{0,511},{1,504},{2,505},{3,506},{4,507},{5,508},{6,509},{7,510},{8... | collective-permute-start | bytes 221192 | tf_op jit(solution)/shard_map/ppermute | solution.py:271
  21.6 0.1 pad_add_fusion.place_ref
  21.7 0.0 collective-permute-done.lon_ref
  21.7 0.0 collective-permute-done.1.lat_ref
  21.7 3.3 %collective-permute-done.2.diag_ref = bf16[2,3,6,2,512]{4,3,2,1,0:T(2,128)(2,1)S(1)} collective-permute-done((bf16[2,3,6,2,512]{4,3,2,1,0:T(2,128)(2,1)}, bf16[2,3,6,2,512]{4,3,2,1,0:T(2,128)(2,1)S(1)}, u32[]{:S(2)}, u32[]{:S(2)}) %collective-permute-start.2) | collective-permute-done | bytes 73760 | tf_op jit(solution)/shard_map/ppermute | solution.py:271
  25.0 0.0 copy-start.2
  25.0 0.9 copy-done.2
  25.9 7.3 %shard_map.60 = (bf16[3,6,2,512]{3,2,1,0:T(2,128)(2,1)S(1)}, bf16[3,6,2,512]{3,2,1,0:T(2,128)(2,1)S(1)}, bf16[3,6,2,512]{3,2,1,0:T(2,128)(2,1)S(1)}, bf16[3,6,2,...) custom-call(s32[2]{0:T(128)S(1)} %pad_add_fusion.place_ref, ...), custom_call_target="tpu_custom_call" | custom-call | tf_op jit(solution)/shard_map/pallas_call | solution.py:185
  33.2 3.0 %collective-permute-start.3 = (bf16[8,384,128]{2,1,0:T(8,128)(2,1)}, bf16[8,384,128]{2,1,0:T(8,128)(2,1)S(1)}, u32[]{:S(2)}, u32[]{:S(2)}) collective-permute-start(bf16[8,384,128]{2,1,0:T(8,128)(2,1)} %get-tuple-element.22), channel_id=1, source_target_pairs={{0,8},{8,0},{1,9},{9,1},{2,10},{10,2},{3,11},{11,3},{4,12},{12,4},... | collective-permute-start | bytes 2359304 | tf_op jit(solution)/shard_map/ppermute | solution.py:288
  36.2 2.1 %collective-permute-done.3.taken_ref = bf16[8,384,128]{2,1,0:T(8,128)(2,1)S(1)} collective-permute-done((bf16[8,384,128]{2,1,0:T(8,128)(2,1)}, bf16[8,384,128]{2,1,0:T(8,128)(2,1)S(1)}, u32[]{:S(2)}, u32[]{:S(2)}) %collective-permute-start.3) | collective-permute-done | bytes 786464 | tf_op jit(solution)/shard_map/ppermute | solution.py:288
  38.3 0.0 copy-start
  38.3 1.1 %copy-done = bf16[8,384,128]{2,1,0:T(8,128)(2,1)S(1)} copy-done((bf16[8,384,128]{2,1,0:T(8,128)(2,1)S(1)}, bf16[8,384,128]{2,1,0:T(8,128)(2,1)}, u32[]{:S(2)}) %copy-start) | copy-done | bytes 786456
  39.5 1.1 %shard_map.61 = (bf16[8,384,128]{2,1,0:T(8,128)(2,1)}, bf16[3,6,2,512]{3,2,1,0:T(2,128)(2,1)S(1)}, bf16[3,6,2,512]{3,2,1,0:T(2,128)(2,1)S(1)}, bf16[3,6,2,512]{3,2,1,0:T(2,128)(2,1)S(1)}) custom-call(bf16[8,384,128]{2,1,0:T(8,128)(2,1)S(1)} %copy-done, ...), custom_call_target="tpu_custom_call", output_to_operand_aliasing={{1}: (2, {}), {2}: (3, {}), {3}: (4, {})} | custom-call | tf_op jit(solution)/shard_map/pallas_call | solution.py:210
  40.6 0.0 copy-start.1
  40.6 4.4 %all-to-all-start = ((bf16[8,384,128]{2,1,0:T(8,128)(2,1)}), bf16[8,384,128]{2,1,0:T(8,128)(2,1)S(1)}, u32[]{:S(2)}, u32[]{:S(2)}) async-start(bf16[8,384,128]{2,1,0:T(8,128)(2,1)} %get-tuple-element.29), calls=%async_computation | async-start | bytes 1572864 | tf_op jit(solution)/shard_map/all_to_all | solution.py:290
  44.9 2.0 %collective-permute-start.4 = (bf16[3,6,2,512]{3,2,1,0:T(2,128)(2,1)S(1)}, bf16[3,6,2,512]{3,2,1,0:T(2,128)(2,1)S(1)}, u32[]{:S(2)}, u32[]{:S(2)}) collective-permute-start(bf16[3,6,2,512]{3,2,1,0:T(2,128)(2,1)S(1)} %get-tuple-element.26), channel_id=1, source_target_pairs={{0,8},{8,16},{16,24},{24,32},{32,40},{40,48},{48,56},{56,64},{64,7... | collective-permute-start | bytes 110600 | tf_op jit(solution)/shard_map/ppermute | solution.py:261
  46.9 3.9 %collective-permute-start.5 = (bf16[3,6,2,512]{3,2,1,0:T(2,128)(2,1)S(1)}, bf16[3,6,2,512]{3,2,1,0:T(2,128)(2,1)S(1)}, u32[]{:S(2)}, u32[]{:S(2)}) collective-permute-start(bf16[3,6,2,512]{3,2,1,0:T(2,128)(2,1)S(1)} %get-tuple-element.27), channel_id=1, source_target_pairs={{0,1},{1,2},{2,3},{3,4},{4,5},{5,6},{6,7},{7,0},{8,9},{9,10},{10,1... | collective-permute-start | bytes 110600 | tf_op jit(solution)/shard_map/ppermute | solution.py:261
  50.8 4.4 %collective-permute-start.6 = (bf16[3,6,2,512]{3,2,1,0:T(2,128)(2,1)S(1)}, bf16[3,6,2,512]{3,2,1,0:T(2,128)(2,1)S(1)}, u32[]{:S(2)}, u32[]{:S(2)}) collective-permute-start(bf16[3,6,2,512]{3,2,1,0:T(2,128)(2,1)S(1)} %get-tuple-element.28), channel_id=1, source_target_pairs={{0,9},{1,10},{2,11},{3,12},{4,13},{5,14},{6,15},{7,8},{8,17},{9,18... | collective-permute-start | bytes 110600 | tf_op jit(solution)/shard_map/ppermute | solution.py:271
  55.2 2.9 %collective-permute-done.4.lon_ref = bf16[3,6,2,512]{3,2,1,0:T(2,128)(2,1)S(1)} collective-permute-done((bf16[3,6,2,512]{3,2,1,0:T(2,128)(2,1)S(1)}, bf16[3,6,2,512]{3,2,1,0:T(2,128)(2,1)S(1)}, u32[]{:S(2)}, u32[]{:S(2)}) %collective-permute-start.4) | collective-permute-done | bytes 36896 | tf_op jit(solution)/shard_map/ppermute | solution.py:261
  58.1 1.1 %collective-permute-done.5.lat_ref = bf16[3,6,2,512]{3,2,1,0:T(2,128)(2,1)S(1)} collective-permute-done((bf16[3,6,2,512]{3,2,1,0:T(2,128)(2,1)S(1)}, bf16[3,6,2,512]{3,2,1,0:T(2,128)(2,1)S(1)}, u32[]{:S(2)}, u32[]{:S(2)}) %collective-permute-start.5) | collective-permute-done | bytes 36896 | tf_op jit(solution)/shard_map/ppermute | solution.py:261
  59.2 6.0 %collective-permute-done.6.diag_ref = bf16[3,6,2,512]{3,2,1,0:T(2,128)(2,1)S(1)} collective-permute-done((bf16[3,6,2,512]{3,2,1,0:T(2,128)(2,1)S(1)}, bf16[3,6,2,512]{3,2,1,0:T(2,128)(2,1)S(1)}, u32[]{:S(2)}, u32[]{:S(2)}) %collective-permute-start.6) | collective-permute-done | bytes 36896 | tf_op jit(solution)/shard_map/ppermute | solution.py:271
  65.2 0.0 all-to-all-done.parts_ref
  65.2 0.8 shard_map.62.rows_ref
  66.0 12.0 %all-to-all-start.1 = ((bf16[32,8,192]{2,1,0:T(8,128)(2,1)}), bf16[32,8,192]{2,1,0:T(8,128)(2,1)S(1)}, u32[]{:S(2)}, u32[]{:S(2)}) async-start(bf16[32,8,192]{2,1,0:T(8,128)(2,1)} %shard_map.62.rows_ref), calls=%async_computation.1 | async-start | bytes 262144 | tf_op jit(solution)/shard_map/all_to_all | solution.py:295
  78.1 0.0 copy-done.1
  78.1 0.8 shard_map.63
  78.9 11.7 %all-to-all-done.1 = bf16[32,8,192]{2,1,0:T(8,128)(2,1)S(1)} async-done(((bf16[32,8,192]{2,1,0:T(8,128)(2,1)}), bf16[32,8,192]{2,1,0:T(8,128)(2,1)S(1)}, u32[]{:S(2)}, u32[]{:S(2)}) %all-to-all-start.1) | async-done | bytes 98336 | tf_op jit(solution)/shard_map/all_to_all | solution.py:295
  90.6 0.7 maximum_select_fusion
  (3 shorter events, 0.0 us)
Async XLA Ops:
  10.7 11.0 %collective-permute-start = (bf16[2,3,6,2,512]{4,3,2,1,0:T(2,128)(2,1)}, bf16[2,3,6,2,512]{4,3,2,1,0:T(2,128)(2,1)S(1)}, u32[]{:S(2)}, u32[]{:S(2)}) collective-permute-start(bf16[2,3,6,2,512]{4,3,2,1,0:T(2,128)(2,1)} %get-tuple-element.17), channel_id=1, source_target_pairs={{0,504},{8,0},{16,8},{24,16},{32,24},{40,32},{48,40},{56,48},{64,5... | collective-permute-start | bytes 221192 | tf_op jit(solution)/shard_map/ppermute | solution.py:261
  12.7 9.0 %collective-permute-start.1 = (bf16[2,3,6,2,512]{4,3,2,1,0:T(2,128)(2,1)}, bf16[2,3,6,2,512]{4,3,2,1,0:T(2,128)(2,1)S(1)}, u32[]{:S(2)}, u32[]{:S(2)}) collective-permute-start(bf16[2,3,6,2,512]{4,3,2,1,0:T(2,128)(2,1)} %get-tuple-element.18), channel_id=1, source_target_pairs={{0,7},{1,0},{2,1},{3,2},{4,3},{5,4},{6,5},{7,6},{8,15},{9,8},{10,9... | collective-permute-start | bytes 221192 | tf_op jit(solution)/shard_map/ppermute | solution.py:261
  19.2 5.9 %collective-permute-start.2 = (bf16[2,3,6,2,512]{4,3,2,1,0:T(2,128)(2,1)}, bf16[2,3,6,2,512]{4,3,2,1,0:T(2,128)(2,1)S(1)}, u32[]{:S(2)}, u32[]{:S(2)}) collective-permute-start(bf16[2,3,6,2,512]{4,3,2,1,0:T(2,128)(2,1)} %get-tuple-element.19), channel_id=1, source_target_pairs={{0,511},{1,504},{2,505},{3,506},{4,507},{5,508},{6,509},{7,510},{8... | collective-permute-start | bytes 221192 | tf_op jit(solution)/shard_map/ppermute | solution.py:271
  25.0 0.9 copy-start.2
  33.2 5.1 %collective-permute-start.3 = (bf16[8,384,128]{2,1,0:T(8,128)(2,1)}, bf16[8,384,128]{2,1,0:T(8,128)(2,1)S(1)}, u32[]{:S(2)}, u32[]{:S(2)}) collective-permute-start(bf16[8,384,128]{2,1,0:T(8,128)(2,1)} %get-tuple-element.22), channel_id=1, source_target_pairs={{0,8},{8,0},{1,9},{9,1},{2,10},{10,2},{3,11},{11,3},{4,12},{12,4},... | collective-permute-start | bytes 2359304 | tf_op jit(solution)/shard_map/ppermute | solution.py:288
  38.3 1.1 %copy-start = (bf16[8,384,128]{2,1,0:T(8,128)(2,1)S(1)}, bf16[8,384,128]{2,1,0:T(8,128)(2,1)}, u32[]{:S(2)}) copy-start(bf16[8,384,128]{2,1,0:T(8,128)(2,1)} %get-tuple-element.21.keep_ref) | copy-start | bytes 2359300
  40.6 37.5 %copy-start.1 = (bf16[2,6,12,512]{3,0,2,1:T(2,128)(2,1)S(1)}, bf16[2,6,12,512]{3,0,2,1:T(2,128)(2,1)}, u32[]{:S(2)}) copy-start(bf16[2,6,12,512]{3,0,2,1:T(2,128)(2,1)} %param.5) | copy-start | bytes 442372
  40.6 24.7 %all-to-all-start = ((bf16[8,384,128]{2,1,0:T(8,128)(2,1)}), bf16[8,384,128]{2,1,0:T(8,128)(2,1)S(1)}, u32[]{:S(2)}, u32[]{:S(2)}) async-start(bf16[8,384,128]{2,1,0:T(8,128)(2,1)} %get-tuple-element.29), calls=%async_computation | async-start | bytes 1572864 | tf_op jit(solution)/shard_map/all_to_all | solution.py:290
  44.9 13.2 %collective-permute-start.4 = (bf16[3,6,2,512]{3,2,1,0:T(2,128)(2,1)S(1)}, bf16[3,6,2,512]{3,2,1,0:T(2,128)(2,1)S(1)}, u32[]{:S(2)}, u32[]{:S(2)}) collective-permute-start(bf16[3,6,2,512]{3,2,1,0:T(2,128)(2,1)S(1)} %get-tuple-element.26), channel_id=1, source_target_pairs={{0,8},{8,16},{16,24},{24,32},{32,40},{40,48},{48,56},{56,64},{64,7... | collective-permute-start | bytes 110600 | tf_op jit(solution)/shard_map/ppermute | solution.py:261
  46.9 12.3 %collective-permute-start.5 = (bf16[3,6,2,512]{3,2,1,0:T(2,128)(2,1)S(1)}, bf16[3,6,2,512]{3,2,1,0:T(2,128)(2,1)S(1)}, u32[]{:S(2)}, u32[]{:S(2)}) collective-permute-start(bf16[3,6,2,512]{3,2,1,0:T(2,128)(2,1)S(1)} %get-tuple-element.27), channel_id=1, source_target_pairs={{0,1},{1,2},{2,3},{3,4},{4,5},{5,6},{6,7},{7,0},{8,9},{9,10},{10,1... | collective-permute-start | bytes 110600 | tf_op jit(solution)/shard_map/ppermute | solution.py:261
  50.8 14.4 %collective-permute-start.6 = (bf16[3,6,2,512]{3,2,1,0:T(2,128)(2,1)S(1)}, bf16[3,6,2,512]{3,2,1,0:T(2,128)(2,1)S(1)}, u32[]{:S(2)}, u32[]{:S(2)}) collective-permute-start(bf16[3,6,2,512]{3,2,1,0:T(2,128)(2,1)S(1)} %get-tuple-element.28), channel_id=1, source_target_pairs={{0,9},{1,10},{2,11},{3,12},{4,13},{5,14},{6,15},{7,8},{8,17},{9,18... | collective-permute-start | bytes 110600 | tf_op jit(solution)/shard_map/ppermute | solution.py:271
  66.0 24.6 %all-to-all-start.1 = ((bf16[32,8,192]{2,1,0:T(8,128)(2,1)}), bf16[32,8,192]{2,1,0:T(8,128)(2,1)S(1)}, u32[]{:S(2)}, u32[]{:S(2)}) async-start(bf16[32,8,192]{2,1,0:T(8,128)(2,1)} %shard_map.62.rows_ref), calls=%async_computation.1 | async-start | bytes 262144 | tf_op jit(solution)/shard_map/all_to_all | solution.py:295

commit v3 on v2

--- a/solution.py
+++ b/solution.py
@@ -16,8 +16,9 @@
 GROUP = 8
 LANES = GROUP * HEAD_WIDTH
 SPREAD = GROUP * TOKENS
-VMEM = 60 * 1024 * 1024
-WINDOW_VMEM = 54656 * 1024
+FULL = 60 * 1024 * 1024
+LOAD = 51 * 1024 * 1024
+WINDOW = 32 * 1024 * 1024
 SMALL = pltpu.CompilerParams(vmem_limit_bytes=8 * 1024 * 1024)
 
 EPS = 1e-05
@@ -35,19 +36,27 @@
     return lax.dot_general(a, b, dims, preferred_element_type=F32)
 
 
-def split_kernel(tokens_ref, grads_ref, own_ref, lat_ref, lon_ref, diag_ref, sems):
-    copies = []
-    for ref, rows, side in (
-        (lat_ref, 0, 6), (lon_ref, 3, 0), (diag_ref, 0, 0), (own_ref, 3, 6)
-    ):
-        for array, source in enumerate((tokens_ref, grads_ref)):
-            copies.append(pltpu.make_async_copy(
-                source.at[rows:rows + 3, side:side + 6], ref.at[array], sems.at[len(copies)]
-            ))
-    for copy in copies:
-        copy.start()
-    for copy in copies:
-        copy.wait()
+QUARTERS = ((0, 6), (3, 0), (0, 0), (3, 6))
+
+
+def split_kernel(tokens_ref, grads_ref, *refs):
+    *quarter_refs, hold_ref, in_sems, out_sems = refs
+    loads = [
+        pltpu.make_async_copy(source, hold_ref.at[array], in_sems.at[array])
+        for array, source in enumerate((tokens_ref, grads_ref))
+    ]
+    for load in loads:
+        load.start()
+    stores = []
+    for array, load in enumerate(loads):
+        load.wait()
+        for ref, (row, side) in zip(quarter_refs, QUARTERS):
+            quarter = hold_ref.at[array, row:row + 3, side:side + 6]
+            store = pltpu.make_async_copy(quarter, ref.at[array], out_sems.at[len(stores)])
+            store.start()
+            stores.append(store)
+    for store in stores:
+        store.wait()
 
 
 def split(tokens, grads):
@@ -57,35 +66,44 @@
         out_shape=[jax.ShapeDtypeStruct((2, 3, 6, 2, WIDTH), BF16)] * 4,
         in_specs=[anywhere] * 2,
         out_specs=[anywhere] * 4,
-        scratch_shapes=[pltpu.SemaphoreType.DMA((8,))],
-        compiler_params=pltpu.CompilerParams(vmem_limit_bytes=VMEM),
+        scratch_shapes=[
+            pltpu.VMEM((2,) + tokens.shape, BF16),
+            pltpu.SemaphoreType.DMA((2,)),
+            pltpu.SemaphoreType.DMA((8,)),
+        ],
+        compiler_params=pltpu.CompilerParams(vmem_limit_bytes=FULL),
     )(tokens, grads)
 
 
-def window_kernel(
-    place_ref, own_ref, lon_ref, lat_ref, diag_ref, w_qkv_in, w_proj_in,
-    d_own_ref, d_lon_ref, d_lat_ref, d_diag_ref, keep_ref, send_ref,
-    d_qkv_ref, piece_ref, w_qkv_ref, w_proj_ref, weight_ref, load_sems, store_sems,
-):
+def load_kernel(*refs):
     loads = [
-        (own_ref, piece_ref.at[0]),
-        (lon_ref, piece_ref.at[1]),
-        (lat_ref, piece_ref.at[2]),
-        (diag_ref, piece_ref.at[3]),
-        (w_qkv_in, w_qkv_ref),
-        (w_proj_in, w_proj_ref),
-    ]
-    loads = [
-        pltpu.make_async_copy(source, target, load_sems.at[index])
-        for index, (source, target) in enumerate(loads)
+        pltpu.make_async_copy(refs[index], refs[3 + index], refs[6].at[index])
+        for index in range(3)
     ]
     for load in loads:
         load.start()
-    for load in loads[:4]:
+    for load in loads:
         load.wait()
+
+
+def load(*arrays):
+    return pl.pallas_call(
+        load_kernel,
+        out_shape=[jax.ShapeDtypeStruct(array.shape, array.dtype) for array in arrays],
+        in_specs=[pl.BlockSpec(memory_space=pl.ANY)] * 3,
+        out_specs=[pl.BlockSpec(memory_space=pltpu.VMEM)] * 3,
+        scratch_shapes=[pltpu.SemaphoreType.DMA((3,))],
+        compiler_params=pltpu.CompilerParams(vmem_limit_bytes=LOAD),
+    )(*arrays)
+
+
+def window_kernel(
+    place_ref, own_ref, lon_ref, lat_ref, diag_ref, w_qkv_ref, w_proj_ref,
+    d_own_ref, d_lon_ref, d_lat_ref, d_diag_ref, keep_ref, send_ref, d_qkv_ref,
+):
     pieces = [
-        [piece_ref[quad, array].astype(F32).reshape(PIECE, WIDTH) for array in range(2)]
-        for quad in range(4)
+        [ref[array].astype(F32).reshape(PIECE, WIDTH) for array in range(2)]
+        for ref in (own_ref, lon_ref, lat_ref, diag_ref)
     ]
     values = jnp.concatenate([piece[0] for piece in pieces], axis=0)
     grads = jnp.concatenate([piece[1] for piece in pieces], axis=0).astype(BF16)
@@ -94,10 +112,8 @@
     inv_std = lax.rsqrt(jnp.mean(centred * centred, axis=-1, keepdims=True) + EPS)
     unit = centred * inv_std
     normed = unit.astype(BF16)
-    loads[4].wait()
     w_qkv = w_qkv_ref[...]
     qkv = jnp.dot(normed, w_qkv, preferred_element_type=F32).astype(BF16)
-    loads[5].wait()
     d_att = dot(grads, w_proj_ref[...], NT).astype(BF16)
 
     last = place_ref[0]
@@ -144,26 +160,30 @@
     d_qkv = d_qkv_ref[...]
     left = lax.broadcasted_iota(jnp.int32, (128, 128), 1) < 64
     core = place_ref[1]
-    for pair in range(4):
-        block = dot(normed, d_qkv[:, pair * 384:(pair + 1) * 384], TN).reshape(32, 2, 8, 384)
-        for parity in range(2):
-            half = block[:, parity].reshape(256, 384)
-            middle = half[:, 128:256]
-            turned = pltpu.roll(middle, 64, 1)
-            ref = weight_ref.at[parity]
-            ref[2 * pair, :256, :] = half[:, :128].astype(BF16)
-            ref[2 * pair, 256:, :] = jnp.where(left, middle[:128], turned[128:]).astype(BF16)
-            ref[2 * pair + 1, :256, :] = half[:, 256:].astype(BF16)
-            ref[2 * pair + 1, 256:, :] = jnp.where(left, turned[:128], middle[128:]).astype(BF16)
-
-    def stores(kept):
-        return [
-            pltpu.make_async_copy(weight_ref.at[parity], ref, store_sems.at[index])
-            for index, (parity, ref) in enumerate(((kept, keep_ref), (1 - kept, send_ref)))
-        ]
-
-    for store in stores(core):
-        store.start()
+
+    def write(refs):
+        for pair in range(4):
+            block = dot(normed, d_qkv[:, pair * 384:(pair + 1) * 384], TN).reshape(32, 2, 8, 384)
+            for parity, ref in enumerate(refs):
+                half = block[:, parity].reshape(256, 384)
+                middle = half[:, 128:256]
+                turned = pltpu.roll(middle, 64, 1)
+                folded = (
+                    jnp.where(left, middle[:128], turned[128:]),
+                    jnp.where(left, turned[:128], middle[128:]),
+                )
+                for side in range(2):
+                    ref[2 * pair + side, :256, :] = half[:, 256 * side:256 * side + 128].astype(BF16)
+                    ref[2 * pair + side, 256:, :] = folded[side].astype(BF16)
+
+    @pl.when(core == 0)
+    def _():
+        write((keep_ref, send_ref))
+
+    @pl.when(core == 1)
+    def _():
+        write((send_ref, keep_ref))
+
     d_normed = dot(d_qkv, w_qkv, NT)
     d_inputs = inv_std * (
         d_normed
@@ -174,29 +194,18 @@
         block = d_inputs[index * PIECE:(index + 1) * PIECE]
         ref[...] = block.reshape(3, 6, 2, WIDTH).astype(BF16)
 
-    for store in stores(core):
-        store.wait()
-
 
 def window_pass(place, own, lon, lat, diag, w_qkv, w_proj):
     piece = jax.ShapeDtypeStruct((3, 6, 2, WIDTH), BF16)
     weight = jax.ShapeDtypeStruct((8, 384, 128), BF16)
-    anywhere = pl.BlockSpec(memory_space=pl.ANY)
+    vmem = pl.BlockSpec(memory_space=pltpu.VMEM)
     return pl.pallas_call(
         window_kernel,
         out_shape=[piece] * 4 + [weight] * 2,
-        in_specs=[pl.BlockSpec(memory_space=pltpu.SMEM)] + [anywhere] * 6,
-        out_specs=[pl.BlockSpec(memory_space=pltpu.VMEM)] * 4 + [anywhere] * 2,
-        scratch_shapes=[
-            pltpu.VMEM((TOKENS, 3 * WIDTH), BF16),
-            pltpu.VMEM((4, 2, 3, 6, 2, WIDTH), BF16),
-            pltpu.VMEM(w_qkv.shape, BF16),
-            pltpu.VMEM(w_proj.shape, BF16),
-            pltpu.VMEM((2, 8, 384, 128), BF16),
-            pltpu.SemaphoreType.DMA((6,)),
-            pltpu.SemaphoreType.DMA((2,)),
-        ],
-        compiler_params=pltpu.CompilerParams(vmem_limit_bytes=WINDOW_VMEM),
+        in_specs=[pl.BlockSpec(memory_space=pltpu.SMEM)] + [vmem] * 6,
+        out_specs=[vmem] * 6,
+        scratch_shapes=[pltpu.VMEM((TOKENS, 3 * WIDTH), BF16)],
+        compiler_params=pltpu.CompilerParams(vmem_limit_bytes=WINDOW),
     )(place, own, lon, lat, diag, w_qkv, w_proj)
 
 
@@ -236,7 +245,7 @@
     )(grads, own, lon, lat, diag, rows)
 
 
-def columns_kernel(parts_ref, lon_ref, lat_ref, diag_ref, out_ref):
+def columns_kernel(parts_ref, diag_in, lon_ref, lat_ref, out_ref, diag_out):
     total = parts_ref[0].astype(F32)
     for index in range(1, 8):
         total = total + parts_ref[index].astype(F32)
@@ -246,14 +255,19 @@
     out_ref[16:, :, 128:] = pltpu.roll(rest, 64, 1)[:, :64].reshape(16, 8, 64).astype(BF16)
 
 
-def columns(parts, *grads):
+def columns(parts, diag, lon, lat):
+    vmem = pl.BlockSpec(memory_space=pltpu.VMEM)
+    anywhere = pl.BlockSpec(memory_space=pl.ANY)
     return pl.pallas_call(
         columns_kernel,
-        out_shape=jax.ShapeDtypeStruct((32, 8, 192), BF16),
-        in_specs=[pl.BlockSpec(memory_space=pltpu.VMEM)]
-        + [pl.BlockSpec(memory_space=pl.ANY)] * 3,
+        out_shape=[
+            jax.ShapeDtypeStruct((32, 8, 192), BF16), jax.ShapeDtypeStruct(diag.shape, BF16)
+        ],
+        in_specs=[vmem] + [anywhere] * 3,
+        out_specs=[vmem, anywhere],
+        input_output_aliases={1: 1},
         compiler_params=SMALL,
-    )(parts, *grads)
+    )(parts, diag, lon, lat)
 
 
 def turn(block, axes, distance):
@@ -278,10 +292,11 @@
     ))
     tokens = jnp.transpose(tokens, (1, 2, 0, 3))
     cotangent = jnp.transpose(cotangent, (1, 2, 0, 3))
-    own, to_lat, to_lon, to_diag = split(tokens, cotangent)
+    to_lat, to_lon, to_diag, own = split(tokens, cotangent)
     lat = turn(to_lat, LAT, -1)
     lon = turn(to_lon, LON, -1)
     diag = turn_both(to_diag, -1)
+    own, w_qkv, w_proj = load(own, w_qkv, w_proj)
     d_own, d_lon, d_lat, d_diag, keep, send = window_pass(
         place, own, lon, lat, diag, w_qkv, w_proj
     )
@@ -290,9 +305,9 @@
     by_columns = lax.all_to_all(chip, LAT, 0, 0)
     d_lat = turn(d_lat, LAT, 1)
     d_lon = turn(d_lon, LON, 1)
+    rows, d_diag = columns(by_columns, d_diag, d_lon, d_lat)
+    by_rows = lax.all_to_all(rows, ("zh", "y"), 0, 0)
     d_diag = turn_both(d_diag, 1)
-    rows = columns(by_columns, d_lon, d_lat, d_diag)
-    by_rows = lax.all_to_all(rows, ("zh", "y"), 0, 0)
     d_tokens = join(cotangent, d_own, d_lon, d_lat, d_diag, rows)
     d_weight = jnp.sum(by_rows.astype(F32), axis=0)
     odd = lax.axis_index("x") % 2 == 1

time: 91.9 us -> 77.8 us (0.85)
  Pallas kernels: 20.1 us -> 10.5 us
  waiting for transfers between devices: 27.2 us -> 19.5 us
  starting transfers between devices: 40.5 us -> 43.8 us
    all_to_all x1, waiting for transfers between devices: 11.7 us -> 3.05 us  [per_device(): by_rows = lax.all_to_all(rows, ('zh', 'y'), 0, 0)]
    pallas_call x1, Pallas kernels: 10.1 us -> 1.71 us  [split(): pl.pallas_call(split_kernel, out_shape=[jax.ShapeDtypeStruct((2, 3, 6, 2,...]
    all_to_all x1, starting transfers between devices: 12 us -> 17.4 us  [per_device(): by_rows = lax.all_to_all(rows, ('zh', 'y'), 0, 0)]
    ppermute x4, waiting for transfers between devices: 4.02 us -> 8.18 us  [turn(): lax.ppermute(block, axes, [(i, (i + distance) % count) for i in range(cou...]
    ppermute x2, waiting for transfers between devices: 9.38 us -> 6.38 us  [turn_both(): return lax.ppermute(block, LON + LAT, route)]
    pallas_call x1, Pallas kernels: 7.28 us -> 4.59 us  [window_pass(): pl.pallas_call(window_kernel, out_shape=[piece] * 4 + [weight] * 2, in_sp...]
    ppermute x2, starting transfers between devices: 6.82 us -> 4.37 us  [turn_both(): return lax.ppermute(block, LON + LAT, route)]
    pallas_call x1 -> x2, Pallas kernels: 0.78 us -> 2.28 us  [the longest x1 1.49 us: load(): pl.pallas_call(load_kernel, out_shape=[jax.ShapeDtypeStruct(array.shape,...]
  transfers between devices with their start and end apart: 9 -> 9, of which waited for: 6 -> 5; matrix products, arithmetic and copies ran while one was open for 0% -> 0% of each run, Pallas kernels for 1% -> 3%
where the time goes in v3:
time: 77.8 us; the launch traced here: 77.2 us
  starting transfers between devices  43.8 us (56%)
  waiting for transfers between devices  19.5 us (25%)
  Pallas kernels  10.5 us (13%)
  local copies, waits for them, and re-layouts  1.93 us (2%)
  other arithmetic  0.79 us (1%)
  between operations  0.78 us (1%)
    all_to_all x1, starting transfers between devices, per_device(): by_rows = lax.all_to_all(rows, ('zh', 'y'), 0, 0)  17.4 us
    ppermute x4, starting transfers between devices, turn(): lax.ppermute(block, axes, [(i, (i + distance) % count) for i in range(cou...  14.2 us
    ppermute x4, waiting for transfers between devices, turn(): lax.ppermute(block, axes, [(i, (i + distance) % count) for i in range(cou...  8.18 us
    ppermute x2, waiting for transfers between devices, turn_both(): return lax.ppermute(block, LON + LAT, route)  6.38 us
    all_to_all x1, starting transfers between devices, per_device(): by_columns = lax.all_to_all(chip, LAT, 0, 0)  4.84 us
    pallas_call x1, Pallas kernels, window_pass(): pl.pallas_call(window_kernel, out_shape=[piece] * 4 + [weight] * 2, in_sp...  4.59 us
    ppermute x2, starting transfers between devices, turn_both(): return lax.ppermute(block, LON + LAT, route)  4.37 us
    all_to_all x1, waiting for transfers between devices, per_device(): by_rows = lax.all_to_all(rows, ('zh', 'y'), 0, 0)  3.05 us
  transfers between devices with their start and end apart: 9, of which 5 were waited for; matrix products, arithmetic and copies ran while one was open for 0% of the time, Pallas kernels for 3%

profile of v3, /device:TPU:8, one launch (start us, length us, event | category | flops | bytes accessed | tf_op | source)
XLA Modules:
  0.0 77.2 jit_solution(4082406577239308712)
XLA Ops:
  0.6 1.7 %shard_map.59 = (bf16[2,3,6,2,512]{4,3,2,1,0:T(2,128)(2,1)}, bf16[2,3,6,2,512]{4,3,2,1,0:T(2,128)(2,1)}, bf16[2,3,6,2,512]{4,3,2,1,0:T(2,128)(2,1)}, bf16[2,3,6,2,512]{4,3,2,1,0:T(2,128)(2,1)}) custom-call(bf16[6,12,2,512]{3,2,1,0:T(2,128)(2,1)} %bitcast.8, bf16[6,12,2,512]{3,2,1,0:T(2,128)(2,1)} %bitcast.5), custom_call_target="tpu_custom_call" | custom-call | tf_op jit(solution)/shard_map/pallas_call | solution.py:64
  2.4 1.9 %collective-permute-start = (bf16[2,3,6,2,512]{4,3,2,1,0:T(2,128)(2,1)}, bf16[2,3,6,2,512]{4,3,2,1,0:T(2,128)(2,1)S(1)}, u32[]{:S(2)}, u32[]{:S(2)}) collective-permute-start(bf16[2,3,6,2,512]{4,3,2,1,0:T(2,128)(2,1)} %get-tuple-element.23), channel_id=1, source_target_pairs={{0,504},{8,0},{16,8},{24,16},{32,24},{40,32},{48,40},{56,48},{64,5... | collective-permute-start | bytes 221192 | tf_op jit(solution)/shard_map/ppermute | solution.py:275
  4.3 6.5 %collective-permute-start.1 = (bf16[2,3,6,2,512]{4,3,2,1,0:T(2,128)(2,1)}, bf16[2,3,6,2,512]{4,3,2,1,0:T(2,128)(2,1)S(1)}, u32[]{:S(2)}, u32[]{:S(2)}) collective-permute-start(bf16[2,3,6,2,512]{4,3,2,1,0:T(2,128)(2,1)} %get-tuple-element.24), channel_id=1, source_target_pairs={{0,7},{1,0},{2,1},{3,2},{4,3},{5,4},{6,5},{7,6},{8,15},{9,8},{10,9... | collective-permute-start | bytes 221192 | tf_op jit(solution)/shard_map/ppermute | solution.py:275
  10.8 2.4 %collective-permute-start.2 = (bf16[2,3,6,2,512]{4,3,2,1,0:T(2,128)(2,1)}, bf16[2,3,6,2,512]{4,3,2,1,0:T(2,128)(2,1)S(1)}, u32[]{:S(2)}, u32[]{:S(2)}) collective-permute-start(bf16[2,3,6,2,512]{4,3,2,1,0:T(2,128)(2,1)} %get-tuple-element.25), channel_id=1, source_target_pairs={{0,511},{1,504},{2,505},{3,506},{4,507},{5,508},{6,509},{7,510},{8... | collective-permute-start | bytes 221192 | tf_op jit(solution)/shard_map/ppermute | solution.py:285
  13.2 0.0 copy-start.1
  13.2 1.0 %copy-done.1 = bf16[512,512]{1,0:T(8,128)(2,1)S(1)} copy-done((bf16[512,512]{1,0:T(8,128)(2,1)S(1)}, bf16[512,512]{1,0:T(8,128)(2,1)}, u32[]{:S(2)}) %copy-start.1) | copy-done | bytes 524312
  14.3 0.0 copy-start.2
  14.3 0.9 %copy-done.2 = bf16[2,3,6,2,512]{4,3,2,1,0:T(2,128)(2,1)S(1)} copy-done((bf16[2,3,6,2,512]{4,3,2,1,0:T(2,128)(2,1)S(1)}, bf16[2,3,6,2,512]{4,3,2,1,0:T(2,128)(2,1)}, u32[]{:S(2)}) %copy-start.2) | copy-done | bytes 73752
  15.2 1.5 %shard_map.60 = (bf16[2,3,6,2,512]{4,3,2,1,0:T(2,128)(2,1)S(1)}, bf16[512,1536]{1,0:T(8,128)(2,1)S(1)}, bf16[512,512]{1,0:T(8,128)(2,1)S(1)}) custom-call(bf16[2,3,6,2,512]{4,3,2,1,0:T(2,128)(2,1)S(1)} %copy-done.2, bf16[512,1536]{1,0:T(8,128)(2,1)} %refs_1_.1, bf16[512,512]{1,0:T(8,128)(2,1)S(1)} %copy-done.1), custom_call_target="tpu_custom_call" | custom-call | tf_op jit(solution)/shard_map/pallas_call | solution.py:90
  16.7 0.1 pad_add_fusion.place_ref
  16.7 0.0 collective-permute-done.lon_ref
  16.7 0.0 collective-permute-done.1.lat_ref
  16.7 0.0 collective-permute-done.2.diag_ref
  16.7 4.6 %shard_map.61 = (bf16[3,6,2,512]{3,2,1,0:T(2,128)(2,1)S(1)}, bf16[3,6,2,512]{3,2,1,0:T(2,128)(2,1)S(1)}, bf16[3,6,2,512]{3,2,1,0:T(2,128)(2,1)S(1)}, bf16[3,6,2,...) custom-call(s32[2]{0:T(128)S(1)} %pad_add_fusion.place_ref, ...), custom_call_target="tpu_custom_call" | custom-call | tf_op jit(solution)/shard_map/pallas_call | solution.py:202
  21.3 2.9 %collective-permute-start.3 = (bf16[8,384,128]{2,1,0:T(8,128)(2,1)S(1)}, bf16[8,384,128]{2,1,0:T(8,128)(2,1)S(1)}, u32[]{:S(2)}, u32[]{:S(2)}) collective-permute-start(bf16[8,384,128]{2,1,0:T(8,128)(2,1)S(1)} %get-tuple-element.30), channel_id=1, source_target_pairs={{0,8},{8,0},{1,9},{9,1},{2,10},{10,2},{3,11},{11,3},{4,12},{12,4},... | collective-permute-start | bytes 2359304 | tf_op jit(solution)/shard_map/ppermute | solution.py:303
  24.3 1.9 %collective-permute-done.3.taken_ref = bf16[8,384,128]{2,1,0:T(8,128)(2,1)S(1)} collective-permute-done((bf16[8,384,128]{2,1,0:T(8,128)(2,1)S(1)}, bf16[8,384,128]{2,1,0:T(8,128)(2,1)S(1)}, u32[]{:S(2)}, u32[]{:S(2)}) %collective-permute-start.3) | collective-permute-done | bytes 786464 | tf_op jit(solution)/shard_map/ppermute | solution.py:303
  26.2 1.1 %shard_map.62 = (bf16[8,384,128]{2,1,0:T(8,128)(2,1)}, bf16[3,6,2,512]{3,2,1,0:T(2,128)(2,1)S(1)}, bf16[3,6,2,512]{3,2,1,0:T(2,128)(2,1)S(1)}, bf16[3,6,2,512]{3,2,1,0:T(2,128)(2,1)S(1)}) custom-call(bf16[8,384,128]{2,1,0:T(8,128)(2,1)S(1)} %get-tuple-element.29.keep_ref, ...), custom_call_target="tpu_custom_call", output_to_operand_aliasing={{1}: (2, {}), {2}: (3, {}), {3}: (4, {})} | custom-call | tf_op jit(solution)/shard_map/pallas_call | solution.py:219
  27.2 0.0 copy-start
  27.2 4.8 %all-to-all-start = ((bf16[8,384,128]{2,1,0:T(8,128)(2,1)}), bf16[8,384,128]{2,1,0:T(8,128)(2,1)S(1)}, u32[]{:S(2)}, u32[]{:S(2)}) async-start(bf16[8,384,128]{2,1,0:T(8,128)(2,1)} %get-tuple-element.36), calls=%async_computation | async-start | bytes 1572864 | tf_op jit(solution)/shard_map/all_to_all | solution.py:305
  32.1 1.9 %collective-permute-start.4 = (bf16[3,6,2,512]{3,2,1,0:T(2,128)(2,1)S(1)}, bf16[3,6,2,512]{3,2,1,0:T(2,128)(2,1)S(1)}, u32[]{:S(2)}, u32[]{:S(2)}) collective-permute-start(bf16[3,6,2,512]{3,2,1,0:T(2,128)(2,1)S(1)} %get-tuple-element.34), channel_id=1, source_target_pairs={{0,8},{8,16},{16,24},{24,32},{32,40},{40,48},{48,56},{56,64},{64,7... | collective-permute-start | bytes 110600 | tf_op jit(solution)/shard_map/ppermute | solution.py:275
  34.0 3.9 %collective-permute-start.5 = (bf16[3,6,2,512]{3,2,1,0:T(2,128)(2,1)S(1)}, bf16[3,6,2,512]{3,2,1,0:T(2,128)(2,1)S(1)}, u32[]{:S(2)}, u32[]{:S(2)}) collective-permute-start(bf16[3,6,2,512]{3,2,1,0:T(2,128)(2,1)S(1)} %get-tuple-element.35), channel_id=1, source_target_pairs={{0,1},{1,2},{2,3},{3,4},{4,5},{5,6},{6,7},{7,0},{8,9},{9,10},{10,1... | collective-permute-start | bytes 110600 | tf_op jit(solution)/shard_map/ppermute | solution.py:275
  37.9 6.8 %collective-permute-done.4.lon_ref = bf16[3,6,2,512]{3,2,1,0:T(2,128)(2,1)S(1)} collective-permute-done((bf16[3,6,2,512]{3,2,1,0:T(2,128)(2,1)S(1)}, bf16[3,6,2,512]{3,2,1,0:T(2,128)(2,1)S(1)}, u32[]{:S(2)}, u32[]{:S(2)}) %collective-permute-start.4) | collective-permute-done | bytes 36896 | tf_op jit(solution)/shard_map/ppermute | solution.py:275
  44.8 1.4 %collective-permute-done.5.lat_ref = bf16[3,6,2,512]{3,2,1,0:T(2,128)(2,1)S(1)} collective-permute-done((bf16[3,6,2,512]{3,2,1,0:T(2,128)(2,1)S(1)}, bf16[3,6,2,512]{3,2,1,0:T(2,128)(2,1)S(1)}, u32[]{:S(2)}, u32[]{:S(2)}) %collective-permute-start.5) | collective-permute-done | bytes 36896 | tf_op jit(solution)/shard_map/ppermute | solution.py:275
  46.1 0.0 all-to-all-done.parts_ref
  46.1 0.8 %shard_map.63 = (bf16[32,8,192]{2,1,0:T(8,128)(2,1)}, bf16[3,6,2,512]{3,2,1,0:T(2,128)(2,1)S(1)}) custom-call(bf16[8,384,128]{2,1,0:T(8,128)(2,1)S(1)} %all-to-all-done.parts_ref, bf16[3,6,2,512]{3,2,1,0:T(2,128)(2,1)S(1)} %get-tuple-element.37.diag_in, bf16[3,6,2,512]{3,2,1,0:T(2,128)(2,1)S(1)} %collective-permute-done.4.lon_ref, ...), custom_call_target="tpu_custom_call", output_to_operand_aliasing={{1}: (1, {})} | custom-call | tf_op jit(solution)/shard_map/pallas_call | solution.py:261
  46.9 17.4 %all-to-all-start.1 = ((bf16[32,8,192]{2,1,0:T(8,128)(2,1)}), bf16[32,8,192]{2,1,0:T(8,128)(2,1)S(1)}, u32[]{:S(2)}, u32[]{:S(2)}) async-start(bf16[32,8,192]{2,1,0:T(8,128)(2,1)} %get-tuple-element.39.rows_ref), calls=%async_computation.1 | async-start | bytes 262144 | tf_op jit(solution)/shard_map/all_to_all | solution.py:309
  64.3 1.9 %collective-permute-start.6 = (bf16[3,6,2,512]{3,2,1,0:T(2,128)(2,1)S(1)}, bf16[3,6,2,512]{3,2,1,0:T(2,128)(2,1)S(1)}, u32[]{:S(2)}, u32[]{:S(2)}) collective-permute-start(bf16[3,6,2,512]{3,2,1,0:T(2,128)(2,1)S(1)} %get-tuple-element.38), channel_id=1, source_target_pairs={{0,9},{1,10},{2,11},{3,12},{4,13},{5,14},{6,15},{7,8},{8,17},{9,18... | collective-permute-start | bytes 110600 | tf_op jit(solution)/shard_map/ppermute | solution.py:285
  66.3 6.4 %collective-permute-done.6.diag_ref = bf16[3,6,2,512]{3,2,1,0:T(2,128)(2,1)S(1)} collective-permute-done((bf16[3,6,2,512]{3,2,1,0:T(2,128)(2,1)S(1)}, bf16[3,6,2,512]{3,2,1,0:T(2,128)(2,1)S(1)}, u32[]{:S(2)}, u32[]{:S(2)}) %collective-permute-start.6) | collective-permute-done | bytes 36896 | tf_op jit(solution)/shard_map/ppermute | solution.py:285
  72.7 0.0 copy-done
  72.7 0.8 %shard_map.64 = bf16[6,12,2,512]{3,2,1,0:T(2,128)(2,1)} custom-call(bf16[6,12,2,512]{3,2,1,0:T(2,128)(2,1)S(1)} %bitcast.6, bf16[3,6,2,512]{3,2,1,0:T(2,128)(2,1)S(1)} %get-tuple-element.28.own_ref, bf16[3,6,2,512]{3,2,1,0:T(2,128)(2,1)S(1)} %collective-permute-done.4.lon_ref, bf16[3,6,2,512]{3,2,1,0:T(2,128)(2,1)S(1)} %collective-permute-done.5.lat_ref, ...), custom_call_target="tpu_custom_call" | custom-call | tf_op jit(solution)/shard_map/pallas_call | solution.py:239
  73.4 3.1 %all-to-all-done.1 = bf16[32,8,192]{2,1,0:T(8,128)(2,1)S(1)} async-done(((bf16[32,8,192]{2,1,0:T(8,128)(2,1)}), bf16[32,8,192]{2,1,0:T(8,128)(2,1)S(1)}, u32[]{:S(2)}, u32[]{:S(2)}) %all-to-all-start.1) | async-done | bytes 98336 | tf_op jit(solution)/shard_map/all_to_all | solution.py:309
  76.6 0.7 maximum_select_fusion
  (3 shorter events, 0.0 us)
Async XLA Ops:
  2.4 14.4 %collective-permute-start = (bf16[2,3,6,2,512]{4,3,2,1,0:T(2,128)(2,1)}, bf16[2,3,6,2,512]{4,3,2,1,0:T(2,128)(2,1)S(1)}, u32[]{:S(2)}, u32[]{:S(2)}) collective-permute-start(bf16[2,3,6,2,512]{4,3,2,1,0:T(2,128)(2,1)} %get-tuple-element.23), channel_id=1, source_target_pairs={{0,504},{8,0},{16,8},{24,16},{32,24},{40,32},{48,40},{56,48},{64,5... | collective-permute-start | bytes 221192 | tf_op jit(solution)/shard_map/ppermute | solution.py:275
  4.3 12.5 %collective-permute-start.1 = (bf16[2,3,6,2,512]{4,3,2,1,0:T(2,128)(2,1)}, bf16[2,3,6,2,512]{4,3,2,1,0:T(2,128)(2,1)S(1)}, u32[]{:S(2)}, u32[]{:S(2)}) collective-permute-start(bf16[2,3,6,2,512]{4,3,2,1,0:T(2,128)(2,1)} %get-tuple-element.24), channel_id=1, source_target_pairs={{0,7},{1,0},{2,1},{3,2},{4,3},{5,4},{6,5},{7,6},{8,15},{9,8},{10,9... | collective-permute-start | bytes 221192 | tf_op jit(solution)/shard_map/ppermute | solution.py:275
  10.8 6.0 %collective-permute-start.2 = (bf16[2,3,6,2,512]{4,3,2,1,0:T(2,128)(2,1)}, bf16[2,3,6,2,512]{4,3,2,1,0:T(2,128)(2,1)S(1)}, u32[]{:S(2)}, u32[]{:S(2)}) collective-permute-start(bf16[2,3,6,2,512]{4,3,2,1,0:T(2,128)(2,1)} %get-tuple-element.25), channel_id=1, source_target_pairs={{0,511},{1,504},{2,505},{3,506},{4,507},{5,508},{6,509},{7,510},{8... | collective-permute-start | bytes 221192 | tf_op jit(solution)/shard_map/ppermute | solution.py:285
  13.2 1.0 %copy-start.1 = (bf16[512,512]{1,0:T(8,128)(2,1)S(1)}, bf16[512,512]{1,0:T(8,128)(2,1)}, u32[]{:S(2)}) copy-start(bf16[512,512]{1,0:T(8,128)(2,1)} %refs_2_.1) | copy-start | bytes 1572868
  14.3 0.9 %copy-start.2 = (bf16[2,3,6,2,512]{4,3,2,1,0:T(2,128)(2,1)S(1)}, bf16[2,3,6,2,512]{4,3,2,1,0:T(2,128)(2,1)}, u32[]{:S(2)}) copy-start(bf16[2,3,6,2,512]{4,3,2,1,0:T(2,128)(2,1)} %get-tuple-element.21.refs_0_) | copy-start | bytes 221188
  21.3 4.8 %collective-permute-start.3 = (bf16[8,384,128]{2,1,0:T(8,128)(2,1)S(1)}, bf16[8,384,128]{2,1,0:T(8,128)(2,1)S(1)}, u32[]{:S(2)}, u32[]{:S(2)}) collective-permute-start(bf16[8,384,128]{2,1,0:T(8,128)(2,1)S(1)} %get-tuple-element.30), channel_id=1, source_target_pairs={{0,8},{8,0},{1,9},{9,1},{2,10},{10,2},{3,11},{11,3},{4,12},{12,4},... | collective-permute-start | bytes 2359304 | tf_op jit(solution)/shard_map/ppermute | solution.py:303
  27.2 45.4 %copy-start = (bf16[2,6,12,512]{3,0,2,1:T(2,128)(2,1)S(1)}, bf16[2,6,12,512]{3,0,2,1:T(2,128)(2,1)}, u32[]{:S(2)}) copy-start(bf16[2,6,12,512]{3,0,2,1:T(2,128)(2,1)} %param.5) | copy-start | bytes 442372
  27.2 18.9 %all-to-all-start = ((bf16[8,384,128]{2,1,0:T(8,128)(2,1)}), bf16[8,384,128]{2,1,0:T(8,128)(2,1)S(1)}, u32[]{:S(2)}, u32[]{:S(2)}) async-start(bf16[8,384,128]{2,1,0:T(8,128)(2,1)} %get-tuple-element.36), calls=%async_computation | async-start | bytes 1572864 | tf_op jit(solution)/shard_map/all_to_all | solution.py:305
  32.1 12.7 %collective-permute-start.4 = (bf16[3,6,2,512]{3,2,1,0:T(2,128)(2,1)S(1)}, bf16[3,6,2,512]{3,2,1,0:T(2,128)(2,1)S(1)}, u32[]{:S(2)}, u32[]{:S(2)}) collective-permute-start(bf16[3,6,2,512]{3,2,1,0:T(2,128)(2,1)S(1)} %get-tuple-element.34), channel_id=1, source_target_pairs={{0,8},{8,16},{16,24},{24,32},{32,40},{40,48},{48,56},{56,64},{64,7... | collective-permute-start | bytes 110600 | tf_op jit(solution)/shard_map/ppermute | solution.py:275
  34.0 12.1 %collective-permute-start.5 = (bf16[3,6,2,512]{3,2,1,0:T(2,128)(2,1)S(1)}, bf16[3,6,2,512]{3,2,1,0:T(2,128)(2,1)S(1)}, u32[]{:S(2)}, u32[]{:S(2)}) collective-permute-start(bf16[3,6,2,512]{3,2,1,0:T(2,128)(2,1)S(1)} %get-tuple-element.35), channel_id=1, source_target_pairs={{0,1},{1,2},{2,3},{3,4},{4,5},{5,6},{6,7},{7,0},{8,9},{9,10},{10,1... | collective-permute-start | bytes 110600 | tf_op jit(solution)/shard_map/ppermute | solution.py:275
  46.9 29.6 %all-to-all-start.1 = ((bf16[32,8,192]{2,1,0:T(8,128)(2,1)}), bf16[32,8,192]{2,1,0:T(8,128)(2,1)S(1)}, u32[]{:S(2)}, u32[]{:S(2)}) async-start(bf16[32,8,192]{2,1,0:T(8,128)(2,1)} %get-tuple-element.39.rows_ref), calls=%async_computation.1 | async-start | bytes 262144 | tf_op jit(solution)/shard_map/all_to_all | solution.py:309
  64.3 8.3 %collective-permute-start.6 = (bf16[3,6,2,512]{3,2,1,0:T(2,128)(2,1)S(1)}, bf16[3,6,2,512]{3,2,1,0:T(2,128)(2,1)S(1)}, u32[]{:S(2)}, u32[]{:S(2)}) collective-permute-start(bf16[3,6,2,512]{3,2,1,0:T(2,128)(2,1)S(1)} %get-tuple-element.38), channel_id=1, source_target_pairs={{0,9},{1,10},{2,11},{3,12},{4,13},{5,14},{6,15},{7,8},{8,17},{9,18... | collective-permute-start | bytes 110600 | tf_op jit(solution)/shard_map/ppermute | solution.py:285

commit v4 on v3

--- a/solution.py
+++ b/solution.py
@@ -16,7 +16,7 @@
 GROUP = 8
 LANES = GROUP * HEAD_WIDTH
 SPREAD = GROUP * TOKENS
-FULL = 60 * 1024 * 1024
+FULL = 54880 * 1024
 LOAD = 51 * 1024 * 1024
 WINDOW = 32 * 1024 * 1024
 SMALL = pltpu.CompilerParams(vmem_limit_bytes=8 * 1024 * 1024)
@@ -36,49 +36,37 @@
     return lax.dot_general(a, b, dims, preferred_element_type=F32)
 
 
-QUARTERS = ((0, 6), (3, 0), (0, 0), (3, 6))
+QUARTERS = ((3, 6), (0, 6), (3, 0), (0, 0))
 
 
 def split_kernel(tokens_ref, grads_ref, *refs):
-    *quarter_refs, hold_ref, in_sems, out_sems = refs
-    loads = [
-        pltpu.make_async_copy(source, hold_ref.at[array], in_sems.at[array])
-        for array, source in enumerate((tokens_ref, grads_ref))
-    ]
-    for load in loads:
-        load.start()
-    stores = []
-    for array, load in enumerate(loads):
-        load.wait()
-        for ref, (row, side) in zip(quarter_refs, QUARTERS):
-            quarter = hold_ref.at[array, row:row + 3, side:side + 6]
-            store = pltpu.make_async_copy(quarter, ref.at[array], out_sems.at[len(stores)])
-            store.start()
-            stores.append(store)
-    for store in stores:
-        store.wait()
+    *quarter_refs, sems = refs
+    copies = []
+    for ref, (row, side) in zip(quarter_refs, QUARTERS):
+        for array, source in enumerate((tokens_ref, grads_ref)):
+            quarter = source.at[row:row + 3, side:side + 6]
+            copies.append(pltpu.make_async_copy(quarter, ref.at[array], sems.at[len(copies)]))
+    for copy in copies:
+        copy.start()
+    for copy in copies:
+        copy.wait()
 
 
 def split(tokens, grads):
-    anywhere = pl.BlockSpec(memory_space=pl.ANY)
     return pl.pallas_call(
         split_kernel,
         out_shape=[jax.ShapeDtypeStruct((2, 3, 6, 2, WIDTH), BF16)] * 4,
-        in_specs=[anywhere] * 2,
-        out_specs=[anywhere] * 4,
-        scratch_shapes=[
-            pltpu.VMEM((2,) + tokens.shape, BF16),
-            pltpu.SemaphoreType.DMA((2,)),
-            pltpu.SemaphoreType.DMA((8,)),
-        ],
+        in_specs=[pl.BlockSpec(memory_space=pl.ANY)] * 2,
+        out_specs=[pl.BlockSpec(memory_space=pltpu.VMEM)] * 4,
+        scratch_shapes=[pltpu.SemaphoreType.DMA((8,))],
         compiler_params=pltpu.CompilerParams(vmem_limit_bytes=FULL),
     )(tokens, grads)
 
 
 def load_kernel(*refs):
     loads = [
-        pltpu.make_async_copy(refs[index], refs[3 + index], refs[6].at[index])
-        for index in range(3)
+        pltpu.make_async_copy(refs[index], refs[2 + index], refs[4].at[index])
+        for index in range(2)
     ]
     for load in loads:
         load.start()
@@ -90,16 +78,16 @@
     return pl.pallas_call(
         load_kernel,
         out_shape=[jax.ShapeDtypeStruct(array.shape, array.dtype) for array in arrays],
-        in_specs=[pl.BlockSpec(memory_space=pl.ANY)] * 3,
-        out_specs=[pl.BlockSpec(memory_space=pltpu.VMEM)] * 3,
-        scratch_shapes=[pltpu.SemaphoreType.DMA((3,))],
+        in_specs=[pl.BlockSpec(memory_space=pl.ANY)] * 2,
+        out_specs=[pl.BlockSpec(memory_space=pltpu.VMEM)] * 2,
+        scratch_shapes=[pltpu.SemaphoreType.DMA((2,))],
         compiler_params=pltpu.CompilerParams(vmem_limit_bytes=LOAD),
     )(*arrays)
 
 
 def window_kernel(
-    place_ref, own_ref, lon_ref, lat_ref, diag_ref, w_qkv_ref, w_proj_ref,
-    d_own_ref, d_lon_ref, d_lat_ref, d_diag_ref, keep_ref, send_ref, d_qkv_ref,
+    place_ref, diag_ref, lat_ref, lon_ref, own_ref, w_qkv_ref, w_proj_ref,
+    keep_ref, send_ref, d_qkv_ref, unit_ref, inv_std_ref,
 ):
     pieces = [
         [ref[array].astype(F32).reshape(PIECE, WIDTH) for array in range(2)]
@@ -111,9 +99,10 @@
     centred = values - means
     inv_std = lax.rsqrt(jnp.mean(centred * centred, axis=-1, keepdims=True) + EPS)
     unit = centred * inv_std
+    unit_ref[...] = unit
+    inv_std_ref[...] = jnp.broadcast_to(inv_std, inv_std_ref.shape)
     normed = unit.astype(BF16)
-    w_qkv = w_qkv_ref[...]
-    qkv = jnp.dot(normed, w_qkv, preferred_element_type=F32).astype(BF16)
+    qkv = jnp.dot(normed, w_qkv_ref[...], preferred_element_type=F32).astype(BF16)
     d_att = dot(grads, w_proj_ref[...], NT).astype(BF16)
 
     last = place_ref[0]
@@ -184,68 +173,79 @@
     def _():
         write((send_ref, keep_ref))
 
-    d_normed = dot(d_qkv, w_qkv, NT)
-    d_inputs = inv_std * (
+
+def window_pass(place, diag, lat, lon, own, w_qkv, w_proj):
+    weight = jax.ShapeDtypeStruct((8, 384, 128), BF16)
+    vmem = pl.BlockSpec(memory_space=pltpu.VMEM)
+    return pl.pallas_call(
+        window_kernel,
+        out_shape=[weight] * 2 + [
+            jax.ShapeDtypeStruct((TOKENS, 3 * WIDTH), BF16),
+            jax.ShapeDtypeStruct((TOKENS, WIDTH), F32),
+            jax.ShapeDtypeStruct((TOKENS, 128), F32),
+        ],
+        in_specs=[pl.BlockSpec(memory_space=pltpu.SMEM)] + [vmem] * 6,
+        out_specs=[vmem] * 5,
+        compiler_params=pltpu.CompilerParams(vmem_limit_bytes=WINDOW),
+    )(place, diag, lat, lon, own, w_qkv, w_proj)
+
+
+def inputs_kernel(
+    d_qkv_ref, unit_ref, inv_std_ref, w_qkv_ref, d_own_ref, d_side_ref, d_lat_ref
+):
+    unit = unit_ref[...]
+    d_normed = dot(d_qkv_ref[...], w_qkv_ref[...], NT)
+    d_inputs = inv_std_ref[:, :1] * (
         d_normed
         - jnp.mean(d_normed, axis=-1, keepdims=True)
         - unit * jnp.mean(d_normed * unit, axis=-1, keepdims=True)
     )
-    for index, ref in enumerate((d_own_ref, d_lon_ref, d_lat_ref, d_diag_ref)):
+    d_refs = (d_own_ref, d_side_ref.at[0], d_lat_ref, d_side_ref.at[1])
+    for index, ref in enumerate(d_refs):
         block = d_inputs[index * PIECE:(index + 1) * PIECE]
         ref[...] = block.reshape(3, 6, 2, WIDTH).astype(BF16)
 
 
-def window_pass(place, own, lon, lat, diag, w_qkv, w_proj):
+def inputs_pass(d_qkv, unit, inv_std, w_qkv):
     piece = jax.ShapeDtypeStruct((3, 6, 2, WIDTH), BF16)
-    weight = jax.ShapeDtypeStruct((8, 384, 128), BF16)
-    vmem = pl.BlockSpec(memory_space=pltpu.VMEM)
-    return pl.pallas_call(
-        window_kernel,
-        out_shape=[piece] * 4 + [weight] * 2,
-        in_specs=[pl.BlockSpec(memory_space=pltpu.SMEM)] + [vmem] * 6,
-        out_specs=[vmem] * 6,
-        scratch_shapes=[pltpu.VMEM((TOKENS, 3 * WIDTH), BF16)],
-        compiler_params=pltpu.CompilerParams(vmem_limit_bytes=WINDOW),
-    )(place, own, lon, lat, diag, w_qkv, w_proj)
-
-
-def add_kernel(keep_ref, taken_ref, lon_ref, lat_ref, diag_ref, out_ref, *passed):
+    side = jax.ShapeDtypeStruct((2, 3, 6, 2, WIDTH), BF16)
+    return pl.pallas_call(
+        inputs_kernel, out_shape=[piece, side, piece], compiler_params=SMALL
+    )(d_qkv, unit, inv_std, w_qkv)
+
+
+def add_kernel(keep_ref, taken_ref, side_in, out_ref, side_out):
     out_ref[...] = (keep_ref[...].astype(F32) + taken_ref[...].astype(F32)).astype(BF16)
 
 
-def add(keep, taken, *grads):
+def add(keep, taken, side):
     vmem = pl.BlockSpec(memory_space=pltpu.VMEM)
     anywhere = pl.BlockSpec(memory_space=pl.ANY)
     return pl.pallas_call(
         add_kernel,
-        out_shape=[jax.ShapeDtypeStruct(a.shape, a.dtype) for a in (keep,) + grads],
-        in_specs=[vmem] * 2 + [anywhere] * 3,
-        out_specs=[vmem] + [anywhere] * 3,
-        input_output_aliases={2: 1, 3: 2, 4: 3},
+        out_shape=[jax.ShapeDtypeStruct(a.shape, a.dtype) for a in (keep, side)],
+        in_specs=[vmem] * 2 + [anywhere],
+        out_specs=[vmem, anywhere],
+        input_output_aliases={2: 1},
         compiler_params=SMALL,
-    )(keep, taken, *grads)
-
-
-def join_kernel(grads_ref, own_ref, lon_ref, lat_ref, diag_ref, rows_ref, out_ref):
-    for ref, rows, side in (
-        (diag_ref, 0, 0), (lat_ref, 0, 6), (lon_ref, 3, 0), (own_ref, 3, 6)
+    )(keep, taken, side)
+
+
+def join_kernel(grads_ref, own_ref, side_ref, ahead_ref, out_ref):
+    for ref, row, side in (
+        (ahead_ref.at[1], 3, 6), (side_ref.at[0], 0, 6), (ahead_ref.at[0], 3, 0), (own_ref, 0, 0)
     ):
-        block = grads_ref[rows:rows + 3, side:side + 6].astype(F32)
-        out_ref[rows:rows + 3, side:side + 6] = (block + ref[...].astype(F32)).astype(BF16)
-
-
-def join(grads, own, lon, lat, diag, rows):
-    vmem = pl.BlockSpec(memory_space=pltpu.VMEM)
-    return pl.pallas_call(
-        join_kernel,
-        out_shape=jax.ShapeDtypeStruct(grads.shape, BF16),
-        in_specs=[vmem] * 5 + [pl.BlockSpec(memory_space=pl.ANY)],
-        out_specs=vmem,
-        compiler_params=SMALL,
-    )(grads, own, lon, lat, diag, rows)
-
-
-def columns_kernel(parts_ref, diag_in, lon_ref, lat_ref, out_ref, diag_out):
+        block = grads_ref[row:row + 3, side:side + 6].astype(F32)
+        out_ref[row:row + 3, side:side + 6] = (block + ref[...].astype(F32)).astype(BF16)
+
+
+def join(grads, own, side, ahead):
+    return pl.pallas_call(
+        join_kernel, out_shape=jax.ShapeDtypeStruct(grads.shape, BF16), compiler_params=SMALL
+    )(grads, own, side, ahead)
+
+
+def columns_kernel(parts_ref, lat_in, out_ref, lat_out):
     total = parts_ref[0].astype(F32)
     for index in range(1, 8):
         total = total + parts_ref[index].astype(F32)
@@ -255,19 +255,19 @@
     out_ref[16:, :, 128:] = pltpu.roll(rest, 64, 1)[:, :64].reshape(16, 8, 64).astype(BF16)
 
 
-def columns(parts, diag, lon, lat):
+def columns(parts, lat):
     vmem = pl.BlockSpec(memory_space=pltpu.VMEM)
     anywhere = pl.BlockSpec(memory_space=pl.ANY)
     return pl.pallas_call(
         columns_kernel,
         out_shape=[
-            jax.ShapeDtypeStruct((32, 8, 192), BF16), jax.ShapeDtypeStruct(diag.shape, BF16)
+            jax.ShapeDtypeStruct((32, 8, 192), BF16), jax.ShapeDtypeStruct(lat.shape, BF16)
         ],
-        in_specs=[vmem] + [anywhere] * 3,
+        in_specs=[vmem, anywhere],
         out_specs=[vmem, anywhere],
         input_output_aliases={1: 1},
         compiler_params=SMALL,
-    )(parts, diag, lon, lat)
+    )(parts, lat)
 
 
 def turn(block, axes, distance):
@@ -287,28 +287,26 @@
 
 def per_device(tokens, cotangent, w_qkv, w_proj):
     place = jnp.stack((
-        (lax.axis_index(LAT) == lax.axis_size(LAT) - 1).astype(jnp.int32),
+        (lax.axis_index(LAT) == 0).astype(jnp.int32),
         lax.axis_index("c"),
     ))
     tokens = jnp.transpose(tokens, (1, 2, 0, 3))
     cotangent = jnp.transpose(cotangent, (1, 2, 0, 3))
-    to_lat, to_lon, to_diag, own = split(tokens, cotangent)
-    lat = turn(to_lat, LAT, -1)
-    lon = turn(to_lon, LON, -1)
-    diag = turn_both(to_diag, -1)
-    own, w_qkv, w_proj = load(own, w_qkv, w_proj)
-    d_own, d_lon, d_lat, d_diag, keep, send = window_pass(
-        place, own, lon, lat, diag, w_qkv, w_proj
-    )
+    to_diag, to_lon, to_lat, own = split(tokens, cotangent)
+    diag = turn_both(to_diag, 1)
+    lon = turn(to_lon, LON, 1)
+    lat = turn(to_lat, LAT, 1)
+    w_qkv, w_proj = load(w_qkv, w_proj)
+    keep, send, d_qkv, unit, inv_std = window_pass(place, diag, lat, lon, own, w_qkv, w_proj)
     taken = lax.ppermute(send, "c", [(0, 1), (1, 0)])
-    chip, d_lon, d_lat, d_diag = add(keep, taken, d_lon, d_lat, d_diag)
+    d_own, d_side, d_lat = inputs_pass(d_qkv, unit, inv_std, w_qkv)
+    chip, d_side = add(keep, taken, d_side)
     by_columns = lax.all_to_all(chip, LAT, 0, 0)
-    d_lat = turn(d_lat, LAT, 1)
-    d_lon = turn(d_lon, LON, 1)
-    rows, d_diag = columns(by_columns, d_diag, d_lon, d_lat)
+    d_side = turn(d_side, LON, -1)
+    rows, d_lat = columns(by_columns, d_lat)
     by_rows = lax.all_to_all(rows, ("zh", "y"), 0, 0)
-    d_diag = turn_both(d_diag, 1)
-    d_tokens = join(cotangent, d_own, d_lon, d_lat, d_diag, rows)
+    d_ahead = turn(jnp.stack((d_lat, d_side[1])), LAT, -1)
+    d_tokens = join(cotangent, d_own, d_side, d_ahead)
     d_weight = jnp.sum(by_rows.astype(F32), axis=0)
     odd = lax.axis_index("x") % 2 == 1
     d_weight = jnp.where(odd, jnp.roll(d_weight, 64, axis=1), d_weight)

time: 77.8 us -> 70.5 us (0.906)
  the two profiles are of different devices: /device:TPU:8 before, /device:TPU:6 now
where the time goes in v4:
time: 70.5 us; the launch traced here: 69.3 us
  starting transfers between devices  31.2 us (44%)
  waiting for transfers between devices  25.6 us (36%)
  Pallas kernels  9.65 us (14%)
  local copies, waits for them, and re-layouts  1.07 us (2%)
  other arithmetic  0.89 us (1%)
  between operations  0.79 us (1%)
    ppermute x4, starting transfers between devices, turn(): lax.ppermute(block, axes, [(i, (i + distance) % count) for i in range(cou...  12.4 us
    ppermute x4, waiting for transfers between devices, turn(): lax.ppermute(block, axes, [(i, (i + distance) % count) for i in range(cou...  10.3 us
    all_to_all x1, waiting for transfers between devices, per_device(): by_columns = lax.all_to_all(chip, LAT, 0, 0)  7.69 us
    all_to_all x1, starting transfers between devices, per_device(): by_rows = lax.all_to_all(rows, ('zh', 'y'), 0, 0)  7.03 us
    all_to_all x1, starting transfers between devices, per_device(): by_columns = lax.all_to_all(chip, LAT, 0, 0)  6.29 us
    pallas_call x1, Pallas kernels, window_pass(): pl.pallas_call(window_kernel, out_shape=[weight] * 2 + [jax.ShapeDtypeStr...  3.73 us
    ppermute x1, starting transfers between devices, turn_both(): return lax.ppermute(block, LON + LAT, route)  3.63 us
    ppermute x1, waiting for transfers between devices, turn_both(): return lax.ppermute(block, LON + LAT, route)  3.41 us
  transfers between devices with their start and end apart: 8, of which 6 were waited for; matrix products, arithmetic and copies ran while one was open for 0% of the time, Pallas kernels for 6%

profile of v4, /device:TPU:6, one launch (start us, length us, event | category | flops | bytes accessed | tf_op | source)
XLA Modules:
  0.0 69.3 jit_solution(9565646260156618643)
XLA Ops:
  0.6 1.0 %shard_map.59 = (bf16[2,3,6,2,512]{4,3,2,1,0:T(2,128)(2,1)S(1)}, bf16[2,3,6,2,512]{4,3,2,1,0:T(2,128)(2,1)S(1)}, bf16[2,3,6,2,512]{4,3,2,1,0:T(2,128)(2,1)S(1)}, bf16[2,3,6,2,512]{4,3,2,1,0:T(2,128)(2,1)S(1)}) custom-call(bf16[6,12,2,512]{3,2,1,0:T(2,128)(2,1)} %bitcast.9, bf16[6,12,2,512]{3,2,1,0:T(2,128)(2,1)} %bitcast.6), custom_call_target="tpu_custom_call" | custom-call | tf_op jit(solution)/shard_map/pallas_call | solution.py:56
  1.6 3.6 %collective-permute-start = (bf16[2,3,6,2,512]{4,3,2,1,0:T(2,128)(2,1)S(1)}, bf16[2,3,6,2,512]{4,3,2,1,0:T(2,128)(2,1)S(1)}, u32[]{:S(2)}, u32[]{:S(2)}) collective-permute-start(bf16[2,3,6,2,512]{4,3,2,1,0:T(2,128)(2,1)S(1)} %get-tuple-element.20), channel_id=1, source_target_pairs={{0,9},{1,10},{2,11},{3,12},{4,13},{5,14},{6,15},{7,8},{8,17},{9,18... | collective-permute-start | bytes 221192 | tf_op jit(solution)/shard_map/ppermute | solution.py:285
  5.2 3.4 %collective-permute-start.1 = (bf16[2,3,6,2,512]{4,3,2,1,0:T(2,128)(2,1)S(1)}, bf16[2,3,6,2,512]{4,3,2,1,0:T(2,128)(2,1)S(1)}, u32[]{:S(2)}, u32[]{:S(2)}) collective-permute-start(bf16[2,3,6,2,512]{4,3,2,1,0:T(2,128)(2,1)S(1)} %get-tuple-element.21), channel_id=1, source_target_pairs={{0,1},{1,2},{2,3},{3,4},{4,5},{5,6},{6,7},{7,0},{8,9},{9,10},{10,1... | collective-permute-start | bytes 221192 | tf_op jit(solution)/shard_map/ppermute | solution.py:275
  8.7 3.3 %collective-permute-start.2 = (bf16[2,3,6,2,512]{4,3,2,1,0:T(2,128)(2,1)S(1)}, bf16[2,3,6,2,512]{4,3,2,1,0:T(2,128)(2,1)S(1)}, u32[]{:S(2)}, u32[]{:S(2)}) collective-permute-start(bf16[2,3,6,2,512]{4,3,2,1,0:T(2,128)(2,1)S(1)} %get-tuple-element.22), channel_id=1, source_target_pairs={{0,8},{8,16},{16,24},{24,32},{32,40},{40,48},{48,56},{56,64},{64,7... | collective-permute-start | bytes 221192 | tf_op jit(solution)/shard_map/ppermute | solution.py:275
  12.0 0.0 copy-start.1
  12.0 1.0 %copy-done.1 = bf16[512,512]{1,0:T(8,128)(2,1)S(1)} copy-done((bf16[512,512]{1,0:T(8,128)(2,1)S(1)}, bf16[512,512]{1,0:T(8,128)(2,1)}, u32[]{:S(2)}) %copy-start.1) | copy-done | bytes 524312
  13.0 1.4 %shard_map.60 = (bf16[512,1536]{1,0:T(8,128)(2,1)S(1)}, bf16[512,512]{1,0:T(8,128)(2,1)S(1)}) custom-call(bf16[512,1536]{1,0:T(8,128)(2,1)} %refs_0_.1, bf16[512,512]{1,0:T(8,128)(2,1)S(1)} %copy-done.1), custom_call_target="tpu_custom_call" | custom-call | tf_op jit(solution)/shard_map/pallas_call | solution.py:78
  14.5 0.1 pad_add_fusion.place_ref
  14.5 3.4 %collective-permute-done.diag_ref = bf16[2,3,6,2,512]{4,3,2,1,0:T(2,128)(2,1)S(1)} collective-permute-done((bf16[2,3,6,2,512]{4,3,2,1,0:T(2,128)(2,1)S(1)}, bf16[2,3,6,2,512]{4,3,2,1,0:T(2,128)(2,1)S(1)}, u32[]{:S(2)}, u32[]{:S(2)}) %collective-permute-start) | collective-permute-done | bytes 73760 | tf_op jit(solution)/shard_map/ppermute | solution.py:285
  18.0 0.0 collective-permute-done.1.lat_ref
  18.0 4.0 %collective-permute-done.2.lon_ref = bf16[2,3,6,2,512]{4,3,2,1,0:T(2,128)(2,1)S(1)} collective-permute-done((bf16[2,3,6,2,512]{4,3,2,1,0:T(2,128)(2,1)S(1)}, bf16[2,3,6,2,512]{4,3,2,1,0:T(2,128)(2,1)S(1)}, u32[]{:S(2)}, u32[]{:S(2)}) %collective-permute-start.2) | collective-permute-done | bytes 73760 | tf_op jit(solution)/shard_map/ppermute | solution.py:275
  22.0 3.7 %shard_map.61 = (bf16[8,384,128]{2,1,0:T(8,128)(2,1)S(1)}, bf16[8,384,128]{2,1,0:T(8,128)(2,1)S(1)}, bf16[144,1536]{1,0:T(8,128)(2,1)S(1)}, f32[144,512]{1,0:T(8,128)S(1)}, f32[144,128]{1,0:T(8,128)S(1)}) custom-call(s32[2]{0:T(128)S(1)} %pad_add_fusion.place_ref, bf16[2,3,6,2,512]{4,3,2,1,0:T(2,128)(2,1)S(1)} %collective-permute-done.diag_ref, ...), custom_call_target="tpu_custom_call" | custom-call | tf_op jit(solution)/shard_map/pallas_call | solution.py:180
  25.7 1.9 %collective-permute-start.3 = (bf16[8,384,128]{2,1,0:T(8,128)(2,1)S(1)}, bf16[8,384,128]{2,1,0:T(8,128)(2,1)S(1)}, u32[]{:S(2)}, u32[]{:S(2)}) collective-permute-start(bf16[8,384,128]{2,1,0:T(8,128)(2,1)S(1)} %get-tuple-element.31), channel_id=1, source_target_pairs={{0,8},{8,0},{1,9},{9,1},{2,10},{10,2},{3,11},{11,3},{4,12},{12,4},... | collective-permute-start | bytes 2359304 | tf_op jit(solution)/shard_map/ppermute | solution.py:301
  27.6 0.9 %shard_map.62 = (bf16[3,6,2,512]{3,2,1,0:T(2,128)(2,1)S(1)}, bf16[2,3,6,2,512]{4,3,2,1,0:T(2,128)(2,1)S(1)}, bf16[3,6,2,512]{3,2,1,0:T(2,128)(2,1)S(1)}) custom-call(bf16[144,1536]{1,0:T(8,128)(2,1)S(1)} %get-tuple-element.26.d_qkv_ref, f32[144,512]{1,0:T(8,128)S(1)} %get-tuple-element.27.unit_ref, f32[144,128]{1,0:T(8,128)S(1)} %get-tuple-element.28.inv_std_ref, ...), custom_call_target="tpu_custom_call" | custom-call | tf_op jit(solution)/shard_map/pallas_call | solution.py:212
  28.5 1.4 %collective-permute-done.3.taken_ref = bf16[8,384,128]{2,1,0:T(8,128)(2,1)S(1)} collective-permute-done((bf16[8,384,128]{2,1,0:T(8,128)(2,1)S(1)}, bf16[8,384,128]{2,1,0:T(8,128)(2,1)S(1)}, u32[]{:S(2)}, u32[]{:S(2)}) %collective-permute-start.3) | collective-permute-done | bytes 786464 | tf_op jit(solution)/shard_map/ppermute | solution.py:301
  29.9 1.1 %shard_map.63 = (bf16[8,384,128]{2,1,0:T(8,128)(2,1)}, bf16[2,3,6,2,512]{4,3,2,1,0:T(2,128)(2,1)S(1)}) custom-call(bf16[8,384,128]{2,1,0:T(8,128)(2,1)S(1)} %get-tuple-element.30.keep_ref, bf16[8,384,128]{2,1,0:T(8,128)(2,1)S(1)} %collective-permute-done.3.taken_ref, ...), custom_call_target="tpu_custom_call", output_to_operand_aliasing={{1}: (2, {})} | custom-call | tf_op jit(solution)/shard_map/pallas_call | solution.py:224
  31.0 0.0 copy-start
  31.0 6.3 %all-to-all-start = ((bf16[8,384,128]{2,1,0:T(8,128)(2,1)}), bf16[8,384,128]{2,1,0:T(8,128)(2,1)S(1)}, u32[]{:S(2)}, u32[]{:S(2)}) async-start(bf16[8,384,128]{2,1,0:T(8,128)(2,1)} %get-tuple-element.34), calls=%async_computation | async-start | bytes 1572864 | tf_op jit(solution)/shard_map/all_to_all | solution.py:304
  37.3 2.9 %collective-permute-start.4 = (bf16[2,3,6,2,512]{4,3,2,1,0:T(2,128)(2,1)S(1)}, bf16[2,3,6,2,512]{4,3,2,1,0:T(2,128)(2,1)S(1)}, u32[]{:S(2)}, u32[]{:S(2)}) collective-permute-start(bf16[2,3,6,2,512]{4,3,2,1,0:T(2,128)(2,1)S(1)} %get-tuple-element.33), channel_id=1, source_target_pairs={{0,504},{8,0},{16,8},{24,16},{32,24},{40,32},{48,40},{56,48},{64,5... | collective-permute-start | bytes 221192 | tf_op jit(solution)/shard_map/ppermute | solution.py:275
  40.2 7.7 %all-to-all-done.parts_ref = bf16[8,384,128]{2,1,0:T(8,128)(2,1)S(1)} async-done(((bf16[8,384,128]{2,1,0:T(8,128)(2,1)}), bf16[8,384,128]{2,1,0:T(8,128)(2,1)S(1)}, u32[]{:S(2)}, u32[]{:S(2)}) %all-to-all-start) | async-done | bytes 786464 | tf_op jit(solution)/shard_map/all_to_all | solution.py:304
  47.8 0.8 %shard_map.64 = (bf16[32,8,192]{2,1,0:T(8,128)(2,1)}, bf16[3,6,2,512]{3,2,1,0:T(2,128)(2,1)S(1)}) custom-call(bf16[8,384,128]{2,1,0:T(8,128)(2,1)S(1)} %all-to-all-done.parts_ref, bf16[3,6,2,512]{3,2,1,0:T(2,128)(2,1)S(1)} %get-tuple-element.35.lat_in), custom_call_target="tpu_custom_call", output_to_operand_aliasing={{1}: (1, {})} | custom-call | tf_op jit(solution)/shard_map/pallas_call | solution.py:261
  48.6 7.0 %all-to-all-start.1 = ((bf16[32,8,192]{2,1,0:T(8,128)(2,1)}), bf16[32,8,192]{2,1,0:T(8,128)(2,1)S(1)}, u32[]{:S(2)}, u32[]{:S(2)}) async-start(bf16[32,8,192]{2,1,0:T(8,128)(2,1)} %get-tuple-element.37), calls=%async_computation.1 | async-start | bytes 262144 | tf_op jit(solution)/shard_map/all_to_all | solution.py:307
  55.7 0.0 collective-permute-done.4.side_ref
  55.7 0.1 pad_maximum_fusion
  55.8 2.8 %collective-permute-start.5 = (bf16[2,3,6,2,512]{4,3,2,1,0:T(2,128)(2,1)S(1)}, bf16[2,3,6,2,512]{4,3,2,1,0:T(2,128)(2,1)S(1)}, u32[]{:S(2)}, u32[]{:S(2)}) collective-permute-start(bf16[2,3,6,2,512]{4,3,2,1,0:T(2,128)(2,1)S(1)} %pad_maximum_fusion), channel_id=1, source_target_pairs={{0,7},{1,0},{2,1},{3,2},{4,3},{5,4},{6,5},{7,6},{8,15},{9,8},{10,9... | collective-permute-start | bytes 221192 | tf_op jit(solution)/shard_map/ppermute | solution.py:275
  58.6 6.3 %collective-permute-done.5.ahead_ref = bf16[2,3,6,2,512]{4,3,2,1,0:T(2,128)(2,1)S(1)} collective-permute-done((bf16[2,3,6,2,512]{4,3,2,1,0:T(2,128)(2,1)S(1)}, bf16[2,3,6,2,512]{4,3,2,1,0:T(2,128)(2,1)S(1)}, u32[]{:S(2)}, u32[]{:S(2)}) %collective-permute-start.5) | collective-permute-done | bytes 73760 | tf_op jit(solution)/shard_map/ppermute | solution.py:275
  64.9 0.0 copy-done
  64.9 0.8 %shard_map.65 = bf16[6,12,2,512]{3,2,1,0:T(2,128)(2,1)} custom-call(bf16[6,12,2,512]{3,2,1,0:T(2,128)(2,1)S(1)} %bitcast.7, bf16[3,6,2,512]{3,2,1,0:T(2,128)(2,1)S(1)} %get-tuple-element.29.own_ref, bf16[2,3,6,2,512]{4,3,2,1,0:T(2,128)(2,1)S(1)} %collective-permute-done.4.side_ref, bf16[2,3,6,2,512]{4,3,2,1,0:T(2,128)(2,1)S(1)} %collective-permute-done.5.ahead_ref), custom_call_target="tpu_custom_call" | custom-call | tf_op jit(solution)/shard_map/pallas_call | solution.py:243
  65.7 2.8 %all-to-all-done.1 = bf16[32,8,192]{2,1,0:T(8,128)(2,1)S(1)} async-done(((bf16[32,8,192]{2,1,0:T(8,128)(2,1)}), bf16[32,8,192]{2,1,0:T(8,128)(2,1)S(1)}, u32[]{:S(2)}, u32[]{:S(2)}) %all-to-all-start.1) | async-done | bytes 98336 | tf_op jit(solution)/shard_map/all_to_all | solution.py:307
  68.6 0.7 maximum_select_fusion
  (4 shorter events, 0.1 us)
Async XLA Ops:
  1.6 16.4 %collective-permute-start = (bf16[2,3,6,2,512]{4,3,2,1,0:T(2,128)(2,1)S(1)}, bf16[2,3,6,2,512]{4,3,2,1,0:T(2,128)(2,1)S(1)}, u32[]{:S(2)}, u32[]{:S(2)}) collective-permute-start(bf16[2,3,6,2,512]{4,3,2,1,0:T(2,128)(2,1)S(1)} %get-tuple-element.20), channel_id=1, source_target_pairs={{0,9},{1,10},{2,11},{3,12},{4,13},{5,14},{6,15},{7,8},{8,17},{9,18... | collective-permute-start | bytes 221192 | tf_op jit(solution)/shard_map/ppermute | solution.py:285
  5.2 12.7 %collective-permute-start.1 = (bf16[2,3,6,2,512]{4,3,2,1,0:T(2,128)(2,1)S(1)}, bf16[2,3,6,2,512]{4,3,2,1,0:T(2,128)(2,1)S(1)}, u32[]{:S(2)}, u32[]{:S(2)}) collective-permute-start(bf16[2,3,6,2,512]{4,3,2,1,0:T(2,128)(2,1)S(1)} %get-tuple-element.21), channel_id=1, source_target_pairs={{0,1},{1,2},{2,3},{3,4},{4,5},{5,6},{6,7},{7,0},{8,9},{9,10},{10,1... | collective-permute-start | bytes 221192 | tf_op jit(solution)/shard_map/ppermute | solution.py:275
  8.7 13.3 %collective-permute-start.2 = (bf16[2,3,6,2,512]{4,3,2,1,0:T(2,128)(2,1)S(1)}, bf16[2,3,6,2,512]{4,3,2,1,0:T(2,128)(2,1)S(1)}, u32[]{:S(2)}, u32[]{:S(2)}) collective-permute-start(bf16[2,3,6,2,512]{4,3,2,1,0:T(2,128)(2,1)S(1)} %get-tuple-element.22), channel_id=1, source_target_pairs={{0,8},{8,16},{16,24},{24,32},{32,40},{40,48},{48,56},{56,64},{64,7... | collective-permute-start | bytes 221192 | tf_op jit(solution)/shard_map/ppermute | solution.py:275
  12.0 1.0 %copy-start.1 = (bf16[512,512]{1,0:T(8,128)(2,1)S(1)}, bf16[512,512]{1,0:T(8,128)(2,1)}, u32[]{:S(2)}) copy-start(bf16[512,512]{1,0:T(8,128)(2,1)} %refs_1_.1) | copy-start | bytes 1572868
  25.7 4.2 %collective-permute-start.3 = (bf16[8,384,128]{2,1,0:T(8,128)(2,1)S(1)}, bf16[8,384,128]{2,1,0:T(8,128)(2,1)S(1)}, u32[]{:S(2)}, u32[]{:S(2)}) collective-permute-start(bf16[8,384,128]{2,1,0:T(8,128)(2,1)S(1)} %get-tuple-element.31), channel_id=1, source_target_pairs={{0,8},{8,0},{1,9},{9,1},{2,10},{10,2},{3,11},{11,3},{4,12},{12,4},... | collective-permute-start | bytes 2359304 | tf_op jit(solution)/shard_map/ppermute | solution.py:301
  31.0 33.9 %copy-start = (bf16[2,6,12,512]{3,0,2,1:T(2,128)(2,1)S(1)}, bf16[2,6,12,512]{3,0,2,1:T(2,128)(2,1)}, u32[]{:S(2)}) copy-start(bf16[2,6,12,512]{3,0,2,1:T(2,128)(2,1)} %param.5) | copy-start | bytes 442372
  31.0 16.9 %all-to-all-start = ((bf16[8,384,128]{2,1,0:T(8,128)(2,1)}), bf16[8,384,128]{2,1,0:T(8,128)(2,1)S(1)}, u32[]{:S(2)}, u32[]{:S(2)}) async-start(bf16[8,384,128]{2,1,0:T(8,128)(2,1)} %get-tuple-element.34), calls=%async_computation | async-start | bytes 1572864 | tf_op jit(solution)/shard_map/all_to_all | solution.py:304
  37.3 18.4 %collective-permute-start.4 = (bf16[2,3,6,2,512]{4,3,2,1,0:T(2,128)(2,1)S(1)}, bf16[2,3,6,2,512]{4,3,2,1,0:T(2,128)(2,1)S(1)}, u32[]{:S(2)}, u32[]{:S(2)}) collective-permute-start(bf16[2,3,6,2,512]{4,3,2,1,0:T(2,128)(2,1)S(1)} %get-tuple-element.33), channel_id=1, source_target_pairs={{0,504},{8,0},{16,8},{24,16},{32,24},{40,32},{48,40},{56,48},{64,5... | collective-permute-start | bytes 221192 | tf_op jit(solution)/shard_map/ppermute | solution.py:275
  48.6 19.9 %all-to-all-start.1 = ((bf16[32,8,192]{2,1,0:T(8,128)(2,1)}), bf16[32,8,192]{2,1,0:T(8,128)(2,1)S(1)}, u32[]{:S(2)}, u32[]{:S(2)}) async-start(bf16[32,8,192]{2,1,0:T(8,128)(2,1)} %get-tuple-element.37), calls=%async_computation.1 | async-start | bytes 262144 | tf_op jit(solution)/shard_map/all_to_all | solution.py:307
  55.8 9.1 %collective-permute-start.5 = (bf16[2,3,6,2,512]{4,3,2,1,0:T(2,128)(2,1)S(1)}, bf16[2,3,6,2,512]{4,3,2,1,0:T(2,128)(2,1)S(1)}, u32[]{:S(2)}, u32[]{:S(2)}) collective-permute-start(bf16[2,3,6,2,512]{4,3,2,1,0:T(2,128)(2,1)S(1)} %pad_maximum_fusion), channel_id=1, source_target_pairs={{0,7},{1,0},{2,1},{3,2},{4,3},{5,4},{6,5},{7,6},{8,15},{9,8},{10,9... | collective-permute-start | bytes 221192 | tf_op jit(solution)/shard_map/ppermute | solution.py:275

commit v5 on v4

--- a/solution.py
+++ b/solution.py
@@ -25,6 +25,7 @@
 NEG = -1e30
 LON = ("zh", "y", "c")
 LAT = ("zl", "x")
+LON_ORDER = [31 - i for i in range(32)]
 F32 = jnp.float32
 BF16 = jnp.bfloat16
 
@@ -87,7 +88,7 @@
 
 def window_kernel(
     place_ref, diag_ref, lat_ref, lon_ref, own_ref, w_qkv_ref, w_proj_ref,
-    keep_ref, send_ref, d_qkv_ref, unit_ref, inv_std_ref,
+    send_ref, d_qkv_ref, unit_ref, turned_ref, inv_std_ref,
 ):
     pieces = [
         [ref[array].astype(F32).reshape(PIECE, WIDTH) for array in range(2)]
@@ -100,6 +101,7 @@
     inv_std = lax.rsqrt(jnp.mean(centred * centred, axis=-1, keepdims=True) + EPS)
     unit = centred * inv_std
     unit_ref[...] = unit
+    turned_ref[...] = unit.T.reshape(turned_ref.shape)
     inv_std_ref[...] = jnp.broadcast_to(inv_std, inv_std_ref.shape)
     normed = unit.astype(BF16)
     qkv = jnp.dot(normed, w_qkv_ref[...], preferred_element_type=F32).astype(BF16)
@@ -146,32 +148,26 @@
             start = where * WIDTH + group * LANES
             d_qkv_ref[:, start:start + LANES] = block.astype(BF16)
 
-    d_qkv = d_qkv_ref[...]
+    weight_rows(turned_ref, 1 - place_ref[1], d_qkv_ref, send_ref)
+
+
+def weight_rows(turned_ref, core, d_qkv_ref, out_ref):
+    turned = turned_ref[:, pl.ds(core, 1)].reshape(WIDTH // 2, TOKENS).astype(BF16)
     left = lax.broadcasted_iota(jnp.int32, (128, 128), 1) < 64
-    core = place_ref[1]
-
-    def write(refs):
-        for pair in range(4):
-            block = dot(normed, d_qkv[:, pair * 384:(pair + 1) * 384], TN).reshape(32, 2, 8, 384)
-            for parity, ref in enumerate(refs):
-                half = block[:, parity].reshape(256, 384)
-                middle = half[:, 128:256]
-                turned = pltpu.roll(middle, 64, 1)
-                folded = (
-                    jnp.where(left, middle[:128], turned[128:]),
-                    jnp.where(left, turned[:128], middle[128:]),
-                )
-                for side in range(2):
-                    ref[2 * pair + side, :256, :] = half[:, 256 * side:256 * side + 128].astype(BF16)
-                    ref[2 * pair + side, 256:, :] = folded[side].astype(BF16)
-
-    @pl.when(core == 0)
-    def _():
-        write((keep_ref, send_ref))
-
-    @pl.when(core == 1)
-    def _():
-        write((send_ref, keep_ref))
+    for pair in range(4):
+        columns = d_qkv_ref[:, pair * 384:(pair + 1) * 384]
+        block = jnp.dot(turned, columns, preferred_element_type=F32)
+        middle = block[:, 128:256]
+        swapped = pltpu.roll(middle, 64, 1)
+        folded = (
+            jnp.where(left, middle[:128], swapped[128:]),
+            jnp.where(left, swapped[:128], middle[128:]),
+        )
+        for side in range(2):
+            whole = block[:, 256 * side:256 * side + 128]
+            place = 2 * pair + side
+            out_ref[place, :256, :] = whole.astype(BF16)
+            out_ref[place, 256:, :] = folded[side].astype(BF16)
 
 
 def window_pass(place, diag, lat, lon, own, w_qkv, w_proj):
@@ -179,9 +175,11 @@
     vmem = pl.BlockSpec(memory_space=pltpu.VMEM)
     return pl.pallas_call(
         window_kernel,
-        out_shape=[weight] * 2 + [
+        out_shape=[
+            weight,
             jax.ShapeDtypeStruct((TOKENS, 3 * WIDTH), BF16),
             jax.ShapeDtypeStruct((TOKENS, WIDTH), F32),
+            jax.ShapeDtypeStruct((WIDTH // 16, 2, 8, TOKENS), F32),
             jax.ShapeDtypeStruct((TOKENS, 128), F32),
         ],
         in_specs=[pl.BlockSpec(memory_space=pltpu.SMEM)] + [vmem] * 6,
@@ -191,8 +189,10 @@
 
 
 def inputs_kernel(
-    d_qkv_ref, unit_ref, inv_std_ref, w_qkv_ref, d_own_ref, d_side_ref, d_lat_ref
+    place_ref, d_qkv_ref, unit_ref, turned_ref, inv_std_ref, w_qkv_ref,
+    keep_ref, d_own_ref, d_side_ref, d_lat_ref,
 ):
+    weight_rows(turned_ref, place_ref[1], d_qkv_ref, keep_ref)
     unit = unit_ref[...]
     d_normed = dot(d_qkv_ref[...], w_qkv_ref[...], NT)
     d_inputs = inv_std_ref[:, :1] * (
@@ -206,16 +206,29 @@
         ref[...] = block.reshape(3, 6, 2, WIDTH).astype(BF16)
 
 
-def inputs_pass(d_qkv, unit, inv_std, w_qkv):
+def inputs_pass(place, d_qkv, unit, turned, inv_std, w_qkv):
+    weight = jax.ShapeDtypeStruct((8, 384, 128), BF16)
     piece = jax.ShapeDtypeStruct((3, 6, 2, WIDTH), BF16)
     side = jax.ShapeDtypeStruct((2, 3, 6, 2, WIDTH), BF16)
     return pl.pallas_call(
-        inputs_kernel, out_shape=[piece, side, piece], compiler_params=SMALL
-    )(d_qkv, unit, inv_std, w_qkv)
-
-
-def add_kernel(keep_ref, taken_ref, side_in, out_ref, side_out):
-    out_ref[...] = (keep_ref[...].astype(F32) + taken_ref[...].astype(F32)).astype(BF16)
+        inputs_kernel,
+        out_shape=[weight, piece, side, piece],
+        in_specs=[pl.BlockSpec(memory_space=pltpu.SMEM)]
+        + [pl.BlockSpec(memory_space=pltpu.VMEM)] * 5,
+        compiler_params=SMALL,
+    )(place, d_qkv, unit, turned, inv_std, w_qkv)
+
+
+def add_kernel(keep_ref, taken_ref, side_in, out_ref, side_out, hold_ref, sems):
+    stores = []
+    for index in range(8):
+        total = keep_ref[index].astype(F32) + taken_ref[index].astype(F32)
+        hold_ref[index] = total.astype(BF16)
+        store = pltpu.make_async_copy(hold_ref.at[index], out_ref.at[index], sems.at[index])
+        store.start()
+        stores.append(store)
+    for store in stores:
+        store.wait()
 
 
 def add(keep, taken, side):
@@ -225,8 +238,9 @@
         add_kernel,
         out_shape=[jax.ShapeDtypeStruct(a.shape, a.dtype) for a in (keep, side)],
         in_specs=[vmem] * 2 + [anywhere],
-        out_specs=[vmem, anywhere],
+        out_specs=[anywhere] * 2,
         input_output_aliases={2: 1},
+        scratch_shapes=[pltpu.VMEM(keep.shape, BF16), pltpu.SemaphoreType.DMA((8,))],
         compiler_params=SMALL,
     )(keep, taken, side)
 
@@ -249,10 +263,12 @@
     total = parts_ref[0].astype(F32)
     for index in range(1, 8):
         total = total + parts_ref[index].astype(F32)
-    out_ref[:, :, :128] = total[:256].reshape(32, 8, 128).astype(BF16)
-    rest = total[256:]
-    out_ref[:16, :, 128:] = rest[:, :64].reshape(16, 8, 64).astype(BF16)
-    out_ref[16:, :, 128:] = pltpu.roll(rest, 64, 1)[:, :64].reshape(16, 8, 64).astype(BF16)
+    rests = (total[256:], pltpu.roll(total[256:], 64, 1))
+    for tile in range(32):
+        row, fold = 8 * tile, 256 + 8 * (tile % 16)
+        place = LON_ORDER.index(tile)
+        out_ref[place, :, :128] = total[row:row + 8].astype(BF16)
+        out_ref[place, :, 128:] = rests[tile // 16][fold - 256:fold - 248, :64].astype(BF16)
 
 
 def columns(parts, lat):
@@ -297,14 +313,15 @@
     lon = turn(to_lon, LON, 1)
     lat = turn(to_lat, LAT, 1)
     w_qkv, w_proj = load(w_qkv, w_proj)
-    keep, send, d_qkv, unit, inv_std = window_pass(place, diag, lat, lon, own, w_qkv, w_proj)
+    send, *saved = window_pass(place, diag, lat, lon, own, w_qkv, w_proj)
     taken = lax.ppermute(send, "c", [(0, 1), (1, 0)])
-    d_own, d_side, d_lat = inputs_pass(d_qkv, unit, inv_std, w_qkv)
+    keep, d_own, d_side, d_lat = inputs_pass(place, *saved, w_qkv)
     chip, d_side = add(keep, taken, d_side)
     by_columns = lax.all_to_all(chip, LAT, 0, 0)
     d_side = turn(d_side, LON, -1)
     rows, d_lat = columns(by_columns, d_lat)
-    by_rows = lax.all_to_all(rows, ("zh", "y"), 0, 0)
+    groups = [[2 * tile + core for tile in LON_ORDER] for core in range(2)]
+    by_rows = lax.all_to_all(rows, LON, 0, 0, axis_index_groups=groups)
     d_ahead = turn(jnp.stack((d_lat, d_side[1])), LAT, -1)
     d_tokens = join(cotangent, d_own, d_side, d_ahead)
     d_weight = jnp.sum(by_rows.astype(F32), axis=0)

time: 70.5 us -> 66.9 us (0.949); the launches traced: 69.3 us -> 66.4 us
  waiting for transfers between devices: 25.6 us -> 21.4 us
  starting transfers between devices: 31.2 us -> 32.1 us
    all_to_all x1, waiting for transfers between devices: 2.83 us -> 0.01 us  [per_device(): by_rows = lax.all_to_all(rows, LON, 0, 0, axis_index_groups=groups)]
    all_to_all x1, starting transfers between devices: 7.03 us -> 7.84 us  [per_device(): by_rows = lax.all_to_all(rows, LON, 0, 0, axis_index_groups=groups)]
    ppermute x1, waiting for transfers between devices: 1.38 us -> 0.6 us  [per_device(): taken = lax.ppermute(send, 'c', [(0, 1), (1, 0)])]
  transfers between devices with their start and end apart: 8 -> 8, of which waited for: 6 -> 5; matrix products, arithmetic and copies ran while one was open for 0% -> 0% of each run, Pallas kernels for 6% -> 7%
where the time goes in v5:
time: 66.9 us; the launch traced here: 66.4 us
  starting transfers between devices  32.1 us (48%)
  waiting for transfers between devices  21.4 us (32%)
  Pallas kernels  10.1 us (15%)
  local copies, waits for them, and re-layouts  1.08 us (2%)
  other arithmetic  0.89 us (1%)
  between operations  0.81 us (1%)
    ppermute x4, starting transfers between devices, turn(): lax.ppermute(block, axes, [(i, (i + distance) % count) for i in range(cou...  12.4 us
    ppermute x4, waiting for transfers between devices, turn(): lax.ppermute(block, axes, [(i, (i + distance) % count) for i in range(cou...  9.69 us
    all_to_all x1, starting transfers between devices, per_device(): by_rows = lax.all_to_all(rows, LON, 0, 0, axis_index_groups=groups)  7.84 us
    all_to_all x1, waiting for transfers between devices, per_device(): by_columns = lax.all_to_all(chip, LAT, 0, 0)  7.69 us
    all_to_all x1, starting transfers between devices, per_device(): by_columns = lax.all_to_all(chip, LAT, 0, 0)  6.31 us
    ppermute x1, starting transfers between devices, turn_both(): return lax.ppermute(block, LON + LAT, route)  3.63 us
    pallas_call x1, Pallas kernels, window_pass(): pl.pallas_call(window_kernel, out_shape=[weight, jax.ShapeDtypeStruct((TO...  3.52 us
    ppermute x1, waiting for transfers between devices, turn_both(): return lax.ppermute(block, LON + LAT, route)  3.41 us
  transfers between devices with their start and end apart: 8, of which 5 were waited for; matrix products, arithmetic and copies ran while one was open for 0% of the time, Pallas kernels for 7%

profile of v5, /device:TPU:6, one launch (start us, length us, event | category | flops | bytes accessed | tf_op | source)
XLA Modules:
  0.0 66.4 jit_solution(635049604434119694)
XLA Ops:
  0.6 1.0 %shard_map.59 = (bf16[2,3,6,2,512]{4,3,2,1,0:T(2,128)(2,1)S(1)}, bf16[2,3,6,2,512]{4,3,2,1,0:T(2,128)(2,1)S(1)}, bf16[2,3,6,2,512]{4,3,2,1,0:T(2,128)(2,1)S(1)}, bf16[2,3,6,2,512]{4,3,2,1,0:T(2,128)(2,1)S(1)}) custom-call(bf16[6,12,2,512]{3,2,1,0:T(2,128)(2,1)} %bitcast.9, bf16[6,12,2,512]{3,2,1,0:T(2,128)(2,1)} %bitcast.6), custom_call_target="tpu_custom_call" | custom-call | tf_op jit(solution)/shard_map/pallas_call | solution.py:57
  1.6 3.6 %collective-permute-start = (bf16[2,3,6,2,512]{4,3,2,1,0:T(2,128)(2,1)S(1)}, bf16[2,3,6,2,512]{4,3,2,1,0:T(2,128)(2,1)S(1)}, u32[]{:S(2)}, u32[]{:S(2)}) collective-permute-start(bf16[2,3,6,2,512]{4,3,2,1,0:T(2,128)(2,1)S(1)} %get-tuple-element.21), channel_id=1, source_target_pairs={{0,9},{1,10},{2,11},{3,12},{4,13},{5,14},{6,15},{7,8},{8,17},{9,18... | collective-permute-start | bytes 221192 | tf_op jit(solution)/shard_map/ppermute | solution.py:301
  5.2 3.4 %collective-permute-start.1 = (bf16[2,3,6,2,512]{4,3,2,1,0:T(2,128)(2,1)S(1)}, bf16[2,3,6,2,512]{4,3,2,1,0:T(2,128)(2,1)S(1)}, u32[]{:S(2)}, u32[]{:S(2)}) collective-permute-start(bf16[2,3,6,2,512]{4,3,2,1,0:T(2,128)(2,1)S(1)} %get-tuple-element.22), channel_id=1, source_target_pairs={{0,1},{1,2},{2,3},{3,4},{4,5},{5,6},{6,7},{7,0},{8,9},{9,10},{10,1... | collective-permute-start | bytes 221192 | tf_op jit(solution)/shard_map/ppermute | solution.py:291
  8.7 3.3 %collective-permute-start.2 = (bf16[2,3,6,2,512]{4,3,2,1,0:T(2,128)(2,1)S(1)}, bf16[2,3,6,2,512]{4,3,2,1,0:T(2,128)(2,1)S(1)}, u32[]{:S(2)}, u32[]{:S(2)}) collective-permute-start(bf16[2,3,6,2,512]{4,3,2,1,0:T(2,128)(2,1)S(1)} %get-tuple-element.23), channel_id=1, source_target_pairs={{0,8},{8,16},{16,24},{24,32},{32,40},{40,48},{48,56},{56,64},{64,7... | collective-permute-start | bytes 221192 | tf_op jit(solution)/shard_map/ppermute | solution.py:291
  12.0 0.0 copy-start.1
  12.0 1.0 %copy-done.1 = bf16[512,512]{1,0:T(8,128)(2,1)S(1)} copy-done((bf16[512,512]{1,0:T(8,128)(2,1)S(1)}, bf16[512,512]{1,0:T(8,128)(2,1)}, u32[]{:S(2)}) %copy-start.1) | copy-done | bytes 524312
  13.0 1.4 %shard_map.60 = (bf16[512,1536]{1,0:T(8,128)(2,1)S(1)}, bf16[512,512]{1,0:T(8,128)(2,1)S(1)}) custom-call(bf16[512,1536]{1,0:T(8,128)(2,1)} %refs_0_.1, bf16[512,512]{1,0:T(8,128)(2,1)S(1)} %copy-done.1), custom_call_target="tpu_custom_call" | custom-call | tf_op jit(solution)/shard_map/pallas_call | solution.py:79
  14.5 0.1 pad_add_fusion.place_ref
  14.5 3.4 %collective-permute-done.diag_ref = bf16[2,3,6,2,512]{4,3,2,1,0:T(2,128)(2,1)S(1)} collective-permute-done((bf16[2,3,6,2,512]{4,3,2,1,0:T(2,128)(2,1)S(1)}, bf16[2,3,6,2,512]{4,3,2,1,0:T(2,128)(2,1)S(1)}, u32[]{:S(2)}, u32[]{:S(2)}) %collective-permute-start) | collective-permute-done | bytes 73760 | tf_op jit(solution)/shard_map/ppermute | solution.py:301
  18.0 0.0 collective-permute-done.1.lat_ref
  18.0 4.0 %collective-permute-done.2.lon_ref = bf16[2,3,6,2,512]{4,3,2,1,0:T(2,128)(2,1)S(1)} collective-permute-done((bf16[2,3,6,2,512]{4,3,2,1,0:T(2,128)(2,1)S(1)}, bf16[2,3,6,2,512]{4,3,2,1,0:T(2,128)(2,1)S(1)}, u32[]{:S(2)}, u32[]{:S(2)}) %collective-permute-start.2) | collective-permute-done | bytes 73760 | tf_op jit(solution)/shard_map/ppermute | solution.py:291
  22.0 3.5 %shard_map.61 = (bf16[8,384,128]{2,1,0:T(8,128)(2,1)S(1)}, bf16[144,1536]{1,0:T(8,128)(2,1)S(1)}, f32[144,512]{1,0:T(8,128)S(1)}, f32[32,2,8,144]{3,2,1,0:T(8,128)S(1)}, f32[144,128]{1,0:T(8,128)S(1)}) custom-call(s32[2]{0:T(128)S(1)} %pad_add_fusion.place_ref, bf16[2,3,6,2,512]{4,3,2,1,0:T(2,128)(2,1)S(1)} %collective-permute-done.diag_ref, ...), custom_call_target="tpu_custom_call" | custom-call | tf_op jit(solution)/shard_map/pallas_call | solution.py:176
  25.5 1.9 %collective-permute-start.3 = (bf16[8,384,128]{2,1,0:T(8,128)(2,1)S(1)}, bf16[8,384,128]{2,1,0:T(8,128)(2,1)S(1)}, u32[]{:S(2)}, u32[]{:S(2)}) collective-permute-start(bf16[8,384,128]{2,1,0:T(8,128)(2,1)S(1)} %get-tuple-element.33), channel_id=1, source_target_pairs={{0,8},{8,0},{1,9},{9,1},{2,10},{10,2},{3,11},{11,3},{4,12},{12,4},... | collective-permute-start | bytes 2359304 | tf_op jit(solution)/shard_map/ppermute | solution.py:317
  27.4 1.6 %shard_map.62 = (bf16[8,384,128]{2,1,0:T(8,128)(2,1)S(1)}, bf16[3,6,2,512]{3,2,1,0:T(2,128)(2,1)S(1)}, bf16[2,3,6,2,512]{4,3,2,1,0:T(2,128)(2,1)S(1)}, bf16[3,6,2,512]{3,2,1,0:T(2,128)(2,1)S(1)}) custom-call(s32[2]{0:T(128)S(1)} %pad_add_fusion.place_ref, bf16[144,1536]{1,0:T(8,128)(2,1)S(1)} %get-tuple-element.27.d_qkv_ref, ...), custom_call_target="tpu_custom_call" | custom-call | tf_op jit(solution)/shard_map/pallas_call | solution.py:213
  29.1 0.6 collective-permute-done.3.taken_ref
  29.7 1.0 %shard_map.63 = (bf16[8,384,128]{2,1,0:T(8,128)(2,1)}, bf16[2,3,6,2,512]{4,3,2,1,0:T(2,128)(2,1)S(1)}) custom-call(bf16[8,384,128]{2,1,0:T(8,128)(2,1)S(1)} %get-tuple-element.32.keep_ref, bf16[8,384,128]{2,1,0:T(8,128)(2,1)S(1)} %collective-permute-done.3.taken_ref, ...), custom_call_target="tpu_custom_call", output_to_operand_aliasing={{1}: (2, {})} | custom-call | tf_op jit(solution)/shard_map/pallas_call | solution.py:237
  30.7 0.0 copy-start
  30.7 6.3 %all-to-all-start = ((bf16[8,384,128]{2,1,0:T(8,128)(2,1)}), bf16[8,384,128]{2,1,0:T(8,128)(2,1)S(1)}, u32[]{:S(2)}, u32[]{:S(2)}) async-start(bf16[8,384,128]{2,1,0:T(8,128)(2,1)} %get-tuple-element.36), calls=%async_computation | async-start | bytes 1572864 | tf_op jit(solution)/shard_map/all_to_all | solution.py:320
  37.0 2.9 %collective-permute-start.4 = (bf16[2,3,6,2,512]{4,3,2,1,0:T(2,128)(2,1)S(1)}, bf16[2,3,6,2,512]{4,3,2,1,0:T(2,128)(2,1)S(1)}, u32[]{:S(2)}, u32[]{:S(2)}) collective-permute-start(bf16[2,3,6,2,512]{4,3,2,1,0:T(2,128)(2,1)S(1)} %get-tuple-element.35), channel_id=1, source_target_pairs={{0,504},{8,0},{16,8},{24,16},{32,24},{40,32},{48,40},{56,48},{64,5... | collective-permute-start | bytes 221192 | tf_op jit(solution)/shard_map/ppermute | solution.py:291
  39.9 7.7 %all-to-all-done.parts_ref = bf16[8,384,128]{2,1,0:T(8,128)(2,1)S(1)} async-done(((bf16[8,384,128]{2,1,0:T(8,128)(2,1)}), bf16[8,384,128]{2,1,0:T(8,128)(2,1)S(1)}, u32[]{:S(2)}, u32[]{:S(2)}) %all-to-all-start) | async-done | bytes 786464 | tf_op jit(solution)/shard_map/all_to_all | solution.py:320
  47.6 0.8 %shard_map.64 = (bf16[32,8,192]{2,1,0:T(8,128)(2,1)}, bf16[3,6,2,512]{3,2,1,0:T(2,128)(2,1)S(1)}) custom-call(bf16[8,384,128]{2,1,0:T(8,128)(2,1)S(1)} %all-to-all-done.parts_ref, bf16[3,6,2,512]{3,2,1,0:T(2,128)(2,1)S(1)} %get-tuple-element.37.lat_in), custom_call_target="tpu_custom_call", output_to_operand_aliasing={{1}: (1, {})} | custom-call | tf_op jit(solution)/shard_map/pallas_call | solution.py:277
  48.4 7.8 %all-to-all-start.1 = ((bf16[32,8,192]{2,1,0:T(8,128)(2,1)}), bf16[32,8,192]{2,1,0:T(8,128)(2,1)S(1)}, u32[]{:S(2)}, u32[]{:S(2)}) async-start(bf16[32,8,192]{2,1,0:T(8,128)(2,1)} %get-tuple-element.39), calls=%async_computation.1 | async-start | bytes 262144 | tf_op jit(solution)/shard_map/all_to_all | solution.py:324
  56.2 0.0 collective-permute-done.4.side_ref
  56.3 0.1 pad_maximum_fusion
  56.4 2.8 %collective-permute-start.5 = (bf16[2,3,6,2,512]{4,3,2,1,0:T(2,128)(2,1)S(1)}, bf16[2,3,6,2,512]{4,3,2,1,0:T(2,128)(2,1)S(1)}, u32[]{:S(2)}, u32[]{:S(2)}) collective-permute-start(bf16[2,3,6,2,512]{4,3,2,1,0:T(2,128)(2,1)S(1)} %pad_maximum_fusion), channel_id=1, source_target_pairs={{0,7},{1,0},{2,1},{3,2},{4,3},{5,4},{6,5},{7,6},{8,15},{9,8},{10,9... | collective-permute-start | bytes 221192 | tf_op jit(solution)/shard_map/ppermute | solution.py:291
  59.2 5.7 %collective-permute-done.5.ahead_ref = bf16[2,3,6,2,512]{4,3,2,1,0:T(2,128)(2,1)S(1)} collective-permute-done((bf16[2,3,6,2,512]{4,3,2,1,0:T(2,128)(2,1)S(1)}, bf16[2,3,6,2,512]{4,3,2,1,0:T(2,128)(2,1)S(1)}, u32[]{:S(2)}, u32[]{:S(2)}) %collective-permute-start.5) | collective-permute-done | bytes 73760 | tf_op jit(solution)/shard_map/ppermute | solution.py:291
  64.9 0.0 copy-done
  64.9 0.8 %shard_map.65 = bf16[6,12,2,512]{3,2,1,0:T(2,128)(2,1)} custom-call(bf16[6,12,2,512]{3,2,1,0:T(2,128)(2,1)S(1)} %bitcast.7, bf16[3,6,2,512]{3,2,1,0:T(2,128)(2,1)S(1)} %get-tuple-element.31.own_ref, bf16[2,3,6,2,512]{4,3,2,1,0:T(2,128)(2,1)S(1)} %collective-permute-done.4.side_ref, bf16[2,3,6,2,512]{4,3,2,1,0:T(2,128)(2,1)S(1)} %collective-permute-done.5.ahead_ref), custom_call_target="tpu_custom_call" | custom-call | tf_op jit(solution)/shard_map/pallas_call | solution.py:257
  65.7 0.0 all-to-all-done.1
  65.7 0.7 %maximum_select_fusion = f32[8,192]{1,0:T(8,128)} fusion(f32[8,192]{1,0:T(8,128)S(1)} %convert_reduce_fusion, f32[8,128]{1,0:T(8,128)S(1)} %slice.16, f32[8,64]{1,0:T(8,128)S(1)} %slice.15, pred[]{:T(512)S(6)} %eq.9), kind=kLoop, calls=%fused_computation.2 | loop fusion | flops 3072 | bytes 18433 | tf_op jit(solution)/shard_map/jit(_where)/select_n | solution.py:329
  (4 shorter events, 0.1 us)
Async XLA Ops:
  1.6 16.4 %collective-permute-start = (bf16[2,3,6,2,512]{4,3,2,1,0:T(2,128)(2,1)S(1)}, bf16[2,3,6,2,512]{4,3,2,1,0:T(2,128)(2,1)S(1)}, u32[]{:S(2)}, u32[]{:S(2)}) collective-permute-start(bf16[2,3,6,2,512]{4,3,2,1,0:T(2,128)(2,1)S(1)} %get-tuple-element.21), channel_id=1, source_target_pairs={{0,9},{1,10},{2,11},{3,12},{4,13},{5,14},{6,15},{7,8},{8,17},{9,18... | collective-permute-start | bytes 221192 | tf_op jit(solution)/shard_map/ppermute | solution.py:301
  5.2 12.7 %collective-permute-start.1 = (bf16[2,3,6,2,512]{4,3,2,1,0:T(2,128)(2,1)S(1)}, bf16[2,3,6,2,512]{4,3,2,1,0:T(2,128)(2,1)S(1)}, u32[]{:S(2)}, u32[]{:S(2)}) collective-permute-start(bf16[2,3,6,2,512]{4,3,2,1,0:T(2,128)(2,1)S(1)} %get-tuple-element.22), channel_id=1, source_target_pairs={{0,1},{1,2},{2,3},{3,4},{4,5},{5,6},{6,7},{7,0},{8,9},{9,10},{10,1... | collective-permute-start | bytes 221192 | tf_op jit(solution)/shard_map/ppermute | solution.py:291
  8.7 13.3 %collective-permute-start.2 = (bf16[2,3,6,2,512]{4,3,2,1,0:T(2,128)(2,1)S(1)}, bf16[2,3,6,2,512]{4,3,2,1,0:T(2,128)(2,1)S(1)}, u32[]{:S(2)}, u32[]{:S(2)}) collective-permute-start(bf16[2,3,6,2,512]{4,3,2,1,0:T(2,128)(2,1)S(1)} %get-tuple-element.23), channel_id=1, source_target_pairs={{0,8},{8,16},{16,24},{24,32},{32,40},{40,48},{48,56},{56,64},{64,7... | collective-permute-start | bytes 221192 | tf_op jit(solution)/shard_map/ppermute | solution.py:291
  12.0 1.0 %copy-start.1 = (bf16[512,512]{1,0:T(8,128)(2,1)S(1)}, bf16[512,512]{1,0:T(8,128)(2,1)}, u32[]{:S(2)}) copy-start(bf16[512,512]{1,0:T(8,128)(2,1)} %refs_1_.1) | copy-start | bytes 1572868
  25.5 4.2 %collective-permute-start.3 = (bf16[8,384,128]{2,1,0:T(8,128)(2,1)S(1)}, bf16[8,384,128]{2,1,0:T(8,128)(2,1)S(1)}, u32[]{:S(2)}, u32[]{:S(2)}) collective-permute-start(bf16[8,384,128]{2,1,0:T(8,128)(2,1)S(1)} %get-tuple-element.33), channel_id=1, source_target_pairs={{0,8},{8,0},{1,9},{9,1},{2,10},{10,2},{3,11},{11,3},{4,12},{12,4},... | collective-permute-start | bytes 2359304 | tf_op jit(solution)/shard_map/ppermute | solution.py:317
  30.7 34.2 %copy-start = (bf16[2,6,12,512]{3,0,2,1:T(2,128)(2,1)S(1)}, bf16[2,6,12,512]{3,0,2,1:T(2,128)(2,1)}, u32[]{:S(2)}) copy-start(bf16[2,6,12,512]{3,0,2,1:T(2,128)(2,1)} %param.5) | copy-start | bytes 442372
  30.7 16.9 %all-to-all-start = ((bf16[8,384,128]{2,1,0:T(8,128)(2,1)}), bf16[8,384,128]{2,1,0:T(8,128)(2,1)S(1)}, u32[]{:S(2)}, u32[]{:S(2)}) async-start(bf16[8,384,128]{2,1,0:T(8,128)(2,1)} %get-tuple-element.36), calls=%async_computation | async-start | bytes 1572864 | tf_op jit(solution)/shard_map/all_to_all | solution.py:320
  37.0 19.2 %collective-permute-start.4 = (bf16[2,3,6,2,512]{4,3,2,1,0:T(2,128)(2,1)S(1)}, bf16[2,3,6,2,512]{4,3,2,1,0:T(2,128)(2,1)S(1)}, u32[]{:S(2)}, u32[]{:S(2)}) collective-permute-start(bf16[2,3,6,2,512]{4,3,2,1,0:T(2,128)(2,1)S(1)} %get-tuple-element.35), channel_id=1, source_target_pairs={{0,504},{8,0},{16,8},{24,16},{32,24},{40,32},{48,40},{56,48},{64,5... | collective-permute-start | bytes 221192 | tf_op jit(solution)/shard_map/ppermute | solution.py:291
  48.4 17.3 %all-to-all-start.1 = ((bf16[32,8,192]{2,1,0:T(8,128)(2,1)}), bf16[32,8,192]{2,1,0:T(8,128)(2,1)S(1)}, u32[]{:S(2)}, u32[]{:S(2)}) async-start(bf16[32,8,192]{2,1,0:T(8,128)(2,1)} %get-tuple-element.39), calls=%async_computation.1 | async-start | bytes 262144 | tf_op jit(solution)/shard_map/all_to_all | solution.py:324
  56.4 8.5 %collective-permute-start.5 = (bf16[2,3,6,2,512]{4,3,2,1,0:T(2,128)(2,1)S(1)}, bf16[2,3,6,2,512]{4,3,2,1,0:T(2,128)(2,1)S(1)}, u32[]{:S(2)}, u32[]{:S(2)}) collective-permute-start(bf16[2,3,6,2,512]{4,3,2,1,0:T(2,128)(2,1)S(1)} %pad_maximum_fusion), channel_id=1, source_target_pairs={{0,7},{1,0},{2,1},{3,2},{4,3},{5,4},{6,5},{7,6},{8,15},{9,8},{10,9... | collective-permute-start | bytes 221192 | tf_op jit(solution)/shard_map/ppermute | solution.py:291

commit v6 on v5

--- a/solution.py
+++ b/solution.py
@@ -87,7 +87,7 @@
 
 
 def window_kernel(
-    place_ref, diag_ref, lat_ref, lon_ref, own_ref, w_qkv_ref, w_proj_ref,
+    diag_ref, lat_ref, lon_ref, own_ref, w_qkv_ref, w_proj_ref,
     send_ref, d_qkv_ref, unit_ref, turned_ref, inv_std_ref,
 ):
     pieces = [
@@ -107,7 +107,7 @@
     qkv = jnp.dot(normed, w_qkv_ref[...], preferred_element_type=F32).astype(BF16)
     d_att = dot(grads, w_proj_ref[...], NT).astype(BF16)
 
-    last = place_ref[0]
+    last = (lax.axis_index(LAT) == 0).astype(jnp.int32)
 
     def region(index):
         quad = index // PIECE
@@ -148,7 +148,7 @@
             start = where * WIDTH + group * LANES
             d_qkv_ref[:, start:start + LANES] = block.astype(BF16)
 
-    weight_rows(turned_ref, 1 - place_ref[1], d_qkv_ref, send_ref)
+    weight_rows(turned_ref, 1 - lax.axis_index("c"), d_qkv_ref, send_ref)
 
 
 def weight_rows(turned_ref, core, d_qkv_ref, out_ref):
@@ -170,7 +170,7 @@
             out_ref[place, 256:, :] = folded[side].astype(BF16)
 
 
-def window_pass(place, diag, lat, lon, own, w_qkv, w_proj):
+def window_pass(diag, lat, lon, own, w_qkv, w_proj):
     weight = jax.ShapeDtypeStruct((8, 384, 128), BF16)
     vmem = pl.BlockSpec(memory_space=pltpu.VMEM)
     return pl.pallas_call(
@@ -182,17 +182,17 @@
             jax.ShapeDtypeStruct((WIDTH // 16, 2, 8, TOKENS), F32),
             jax.ShapeDtypeStruct((TOKENS, 128), F32),
         ],
-        in_specs=[pl.BlockSpec(memory_space=pltpu.SMEM)] + [vmem] * 6,
+        in_specs=[vmem] * 6,
         out_specs=[vmem] * 5,
         compiler_params=pltpu.CompilerParams(vmem_limit_bytes=WINDOW),
-    )(place, diag, lat, lon, own, w_qkv, w_proj)
+    )(diag, lat, lon, own, w_qkv, w_proj)
 
 
 def inputs_kernel(
-    place_ref, d_qkv_ref, unit_ref, turned_ref, inv_std_ref, w_qkv_ref,
+    d_qkv_ref, unit_ref, turned_ref, inv_std_ref, w_qkv_ref,
     keep_ref, d_own_ref, d_side_ref, d_lat_ref,
 ):
-    weight_rows(turned_ref, place_ref[1], d_qkv_ref, keep_ref)
+    weight_rows(turned_ref, lax.axis_index("c"), d_qkv_ref, keep_ref)
     unit = unit_ref[...]
     d_normed = dot(d_qkv_ref[...], w_qkv_ref[...], NT)
     d_inputs = inv_std_ref[:, :1] * (
@@ -206,17 +206,15 @@
         ref[...] = block.reshape(3, 6, 2, WIDTH).astype(BF16)
 
 
-def inputs_pass(place, d_qkv, unit, turned, inv_std, w_qkv):
+def inputs_pass(d_qkv, unit, turned, inv_std, w_qkv):
     weight = jax.ShapeDtypeStruct((8, 384, 128), BF16)
     piece = jax.ShapeDtypeStruct((3, 6, 2, WIDTH), BF16)
     side = jax.ShapeDtypeStruct((2, 3, 6, 2, WIDTH), BF16)
     return pl.pallas_call(
         inputs_kernel,
         out_shape=[weight, piece, side, piece],
-        in_specs=[pl.BlockSpec(memory_space=pltpu.SMEM)]
-        + [pl.BlockSpec(memory_space=pltpu.VMEM)] * 5,
         compiler_params=SMALL,
-    )(place, d_qkv, unit, turned, inv_std, w_qkv)
+    )(d_qkv, unit, turned, inv_std, w_qkv)
 
 
 def add_kernel(keep_ref, taken_ref, side_in, out_ref, side_out, hold_ref, sems):
@@ -245,18 +243,36 @@
     )(keep, taken, side)
 
 
-def join_kernel(grads_ref, own_ref, side_ref, ahead_ref, out_ref):
+def finish_kernel(
+    grads_ref, own_ref, side_ref, ahead_ref, rows_ref, d_tokens_ref, d_weight_ref
+):
     for ref, row, side in (
         (ahead_ref.at[1], 3, 6), (side_ref.at[0], 0, 6), (ahead_ref.at[0], 3, 0), (own_ref, 0, 0)
     ):
         block = grads_ref[row:row + 3, side:side + 6].astype(F32)
-        out_ref[row:row + 3, side:side + 6] = (block + ref[...].astype(F32)).astype(BF16)
-
-
-def join(grads, own, side, ahead):
-    return pl.pallas_call(
-        join_kernel, out_shape=jax.ShapeDtypeStruct(grads.shape, BF16), compiler_params=SMALL
-    )(grads, own, side, ahead)
+        d_tokens_ref[row:row + 3, side:side + 6] = (block + ref[...].astype(F32)).astype(BF16)
+    total = jnp.sum(rows_ref[...].astype(F32), axis=0)
+
+    odd = lax.axis_index("x") % 2
+
+    @pl.when(odd == 0)
+    def _():
+        d_weight_ref[...] = total
+
+    @pl.when(odd == 1)
+    def _():
+        d_weight_ref[:, :64] = total[:, 128:]
+        d_weight_ref[:, 64:] = total[:, :128]
+
+
+def finish(grads, own, side, ahead, rows):
+    return pl.pallas_call(
+        finish_kernel,
+        out_shape=[
+            jax.ShapeDtypeStruct(grads.shape, BF16), jax.ShapeDtypeStruct(rows.shape[1:], F32)
+        ],
+        compiler_params=SMALL,
+    )(grads, own, side, ahead, rows)
 
 
 def columns_kernel(parts_ref, lat_in, out_ref, lat_out):
@@ -302,10 +318,6 @@
 
 
 def per_device(tokens, cotangent, w_qkv, w_proj):
-    place = jnp.stack((
-        (lax.axis_index(LAT) == 0).astype(jnp.int32),
-        lax.axis_index("c"),
-    ))
     tokens = jnp.transpose(tokens, (1, 2, 0, 3))
     cotangent = jnp.transpose(cotangent, (1, 2, 0, 3))
     to_diag, to_lon, to_lat, own = split(tokens, cotangent)
@@ -313,9 +325,9 @@
     lon = turn(to_lon, LON, 1)
     lat = turn(to_lat, LAT, 1)
     w_qkv, w_proj = load(w_qkv, w_proj)
-    send, *saved = window_pass(place, diag, lat, lon, own, w_qkv, w_proj)
+    send, *saved = window_pass(diag, lat, lon, own, w_qkv, w_proj)
     taken = lax.ppermute(send, "c", [(0, 1), (1, 0)])
-    keep, d_own, d_side, d_lat = inputs_pass(place, *saved, w_qkv)
+    keep, d_own, d_side, d_lat = inputs_pass(*saved, w_qkv)
     chip, d_side = add(keep, taken, d_side)
     by_columns = lax.all_to_all(chip, LAT, 0, 0)
     d_side = turn(d_side, LON, -1)
@@ -323,10 +335,7 @@
     groups = [[2 * tile + core for tile in LON_ORDER] for core in range(2)]
     by_rows = lax.all_to_all(rows, LON, 0, 0, axis_index_groups=groups)
     d_ahead = turn(jnp.stack((d_lat, d_side[1])), LAT, -1)
-    d_tokens = join(cotangent, d_own, d_side, d_ahead)
-    d_weight = jnp.sum(by_rows.astype(F32), axis=0)
-    odd = lax.axis_index("x") % 2 == 1
-    d_weight = jnp.where(odd, jnp.roll(d_weight, 64, axis=1), d_weight)
+    d_tokens, d_weight = finish(cotangent, d_own, d_side, d_ahead, by_rows)
     return (jnp.transpose(d_tokens, (2, 0, 1, 3)), d_weight)
 
 

time: 66.9 us -> 65.7 us (0.982)
  Pallas kernels: 10.1 us -> 9.11 us
  other arithmetic: 0.89 us -> 0.1 us
  waiting for transfers between devices: 21.4 us -> 22.1 us
    select_n x1 -> x0, other arithmetic: 0.67 us -> none  [per_device(): d_weight = jnp.where(odd, jnp.roll(d_weight, 64, axis=1), d_weight)]
  transfers between devices with their start and end apart: 8 -> 8, of which waited for: 5 -> 5; matrix products, arithmetic and copies ran while one was open for 0% -> 0% of each run, Pallas kernels for 7% -> 5%
where the time goes in v6:
time: 65.7 us; the launch traced here: 65.2 us
  starting transfers between devices  32.1 us (49%)
  waiting for transfers between devices  22.1 us (34%)
  Pallas kernels  9.11 us (14%)
  local copies, waits for them, and re-layouts  1.07 us (2%)
  between operations  0.76 us (1%)
    ppermute x4, starting transfers between devices, turn(): lax.ppermute(block, axes, [(i, (i + distance) % count) for i in range(cou...  12.4 us
    ppermute x4, waiting for transfers between devices, turn(): lax.ppermute(block, axes, [(i, (i + distance) % count) for i in range(cou...  9.7 us
    all_to_all x1, starting transfers between devices, per_device(): by_rows = lax.all_to_all(rows, LON, 0, 0, axis_index_groups=groups)  7.83 us
    all_to_all x1, waiting for transfers between devices, per_device(): by_columns = lax.all_to_all(chip, LAT, 0, 0)  7.69 us
    all_to_all x1, starting transfers between devices, per_device(): by_columns = lax.all_to_all(chip, LAT, 0, 0)  6.31 us
    ppermute x1, starting transfers between devices, turn_both(): return lax.ppermute(block, LON + LAT, route)  3.63 us
    ppermute x1, waiting for transfers between devices, turn_both(): return lax.ppermute(block, LON + LAT, route)  3.5 us
    pallas_call x1, Pallas kernels, window_pass(): pl.pallas_call(window_kernel, out_shape=[weight, jax.ShapeDtypeStruct((TO...  2.98 us
  transfers between devices with their start and end apart: 8, of which 5 were waited for; matrix products, arithmetic and copies ran while one was open for 0% of the time, Pallas kernels for 5%

profile of v6, /device:TPU:6, one launch (start us, length us, event | category | flops | bytes accessed | tf_op | source)
XLA Modules:
  0.0 65.2 jit_solution(420240994899147293)
XLA Ops:
  0.6 1.0 %shard_map.59 = (bf16[2,3,6,2,512]{4,3,2,1,0:T(2,128)(2,1)S(1)}, bf16[2,3,6,2,512]{4,3,2,1,0:T(2,128)(2,1)S(1)}, bf16[2,3,6,2,512]{4,3,2,1,0:T(2,128)(2,1)S(1)}, bf16[2,3,6,2,512]{4,3,2,1,0:T(2,128)(2,1)S(1)}) custom-call(bf16[6,12,2,512]{3,2,1,0:T(2,128)(2,1)} %bitcast.7, bf16[6,12,2,512]{3,2,1,0:T(2,128)(2,1)} %bitcast.4), custom_call_target="tpu_custom_call" | custom-call | tf_op jit(solution)/shard_map/pallas_call | solution.py:57
  1.6 3.6 %collective-permute-start = (bf16[2,3,6,2,512]{4,3,2,1,0:T(2,128)(2,1)S(1)}, bf16[2,3,6,2,512]{4,3,2,1,0:T(2,128)(2,1)S(1)}, u32[]{:S(2)}, u32[]{:S(2)}) collective-permute-start(bf16[2,3,6,2,512]{4,3,2,1,0:T(2,128)(2,1)S(1)} %get-tuple-element.23), channel_id=1, source_target_pairs={{0,9},{1,10},{2,11},{3,12},{4,13},{5,14},{6,15},{7,8},{8,17},{9,18... | collective-permute-start | bytes 221192 | tf_op jit(solution)/shard_map/ppermute | solution.py:317
  5.2 3.4 %collective-permute-start.1 = (bf16[2,3,6,2,512]{4,3,2,1,0:T(2,128)(2,1)S(1)}, bf16[2,3,6,2,512]{4,3,2,1,0:T(2,128)(2,1)S(1)}, u32[]{:S(2)}, u32[]{:S(2)}) collective-permute-start(bf16[2,3,6,2,512]{4,3,2,1,0:T(2,128)(2,1)S(1)} %get-tuple-element.24), channel_id=1, source_target_pairs={{0,1},{1,2},{2,3},{3,4},{4,5},{5,6},{6,7},{7,0},{8,9},{9,10},{10,1... | collective-permute-start | bytes 221192 | tf_op jit(solution)/shard_map/ppermute | solution.py:307
  8.7 3.3 %collective-permute-start.2 = (bf16[2,3,6,2,512]{4,3,2,1,0:T(2,128)(2,1)S(1)}, bf16[2,3,6,2,512]{4,3,2,1,0:T(2,128)(2,1)S(1)}, u32[]{:S(2)}, u32[]{:S(2)}) collective-permute-start(bf16[2,3,6,2,512]{4,3,2,1,0:T(2,128)(2,1)S(1)} %get-tuple-element.25), channel_id=1, source_target_pairs={{0,8},{8,16},{16,24},{24,32},{32,40},{40,48},{48,56},{56,64},{64,7... | collective-permute-start | bytes 221192 | tf_op jit(solution)/shard_map/ppermute | solution.py:307
  12.0 0.0 copy-start.1
  12.0 1.0 %copy-done.1 = bf16[512,512]{1,0:T(8,128)(2,1)S(1)} copy-done((bf16[512,512]{1,0:T(8,128)(2,1)S(1)}, bf16[512,512]{1,0:T(8,128)(2,1)}, u32[]{:S(2)}) %copy-start.1) | copy-done | bytes 524312
  13.0 1.4 %shard_map.60 = (bf16[512,1536]{1,0:T(8,128)(2,1)S(1)}, bf16[512,512]{1,0:T(8,128)(2,1)S(1)}) custom-call(bf16[512,1536]{1,0:T(8,128)(2,1)} %refs_0_.1, bf16[512,512]{1,0:T(8,128)(2,1)S(1)} %copy-done.1), custom_call_target="tpu_custom_call" | custom-call | tf_op jit(solution)/shard_map/pallas_call | solution.py:79
  14.5 3.5 %collective-permute-done.diag_ref = bf16[2,3,6,2,512]{4,3,2,1,0:T(2,128)(2,1)S(1)} collective-permute-done((bf16[2,3,6,2,512]{4,3,2,1,0:T(2,128)(2,1)S(1)}, bf16[2,3,6,2,512]{4,3,2,1,0:T(2,128)(2,1)S(1)}, u32[]{:S(2)}, u32[]{:S(2)}) %collective-permute-start) | collective-permute-done | bytes 73760 | tf_op jit(solution)/shard_map/ppermute | solution.py:317
  18.0 0.0 collective-permute-done.1.lat_ref
  18.0 4.0 %collective-permute-done.2.lon_ref = bf16[2,3,6,2,512]{4,3,2,1,0:T(2,128)(2,1)S(1)} collective-permute-done((bf16[2,3,6,2,512]{4,3,2,1,0:T(2,128)(2,1)S(1)}, bf16[2,3,6,2,512]{4,3,2,1,0:T(2,128)(2,1)S(1)}, u32[]{:S(2)}, u32[]{:S(2)}) %collective-permute-start.2) | collective-permute-done | bytes 73760 | tf_op jit(solution)/shard_map/ppermute | solution.py:307
  22.0 3.0 %shard_map.61 = (bf16[8,384,128]{2,1,0:T(8,128)(2,1)S(1)}, bf16[144,1536]{1,0:T(8,128)(2,1)S(1)}, f32[144,512]{1,0:T(8,128)S(1)}, f32[32,2,8,144]{3,2,1,0:T(8,128)S(1)}, f32[144,128]{1,0:T(8,128)S(1)}) custom-call(bf16[2,3,6,2,512]{4,3,2,1,0:T(2,128)(2,1)S(1)} %collective-permute-done.diag_ref, ...), custom_call_target="tpu_custom_call" | custom-call | tf_op jit(solution)/shard_map/pallas_call | solution.py:176
  25.0 1.9 %collective-permute-start.3 = (bf16[8,384,128]{2,1,0:T(8,128)(2,1)S(1)}, bf16[8,384,128]{2,1,0:T(8,128)(2,1)S(1)}, u32[]{:S(2)}, u32[]{:S(2)}) collective-permute-start(bf16[8,384,128]{2,1,0:T(8,128)(2,1)S(1)} %get-tuple-element.35), channel_id=1, source_target_pairs={{0,8},{8,0},{1,9},{9,1},{2,10},{10,2},{3,11},{11,3},{4,12},{12,4},... | collective-permute-start | bytes 2359304 | tf_op jit(solution)/shard_map/ppermute | solution.py:329
  26.9 1.1 %shard_map.62 = (bf16[8,384,128]{2,1,0:T(8,128)(2,1)S(1)}, bf16[3,6,2,512]{3,2,1,0:T(2,128)(2,1)S(1)}, bf16[2,3,6,2,512]{4,3,2,1,0:T(2,128)(2,1)S(1)}, bf16[3,6,2,512]{3,2,1,0:T(2,128)(2,1)S(1)}) custom-call(bf16[144,1536]{1,0:T(8,128)(2,1)S(1)} %get-tuple-element.29.d_qkv_ref, f32[144,512]{1,0:T(8,128)S(1)} %get-tuple-element.30.unit_ref, ...), custom_call_target="tpu_custom_call" | custom-call | tf_op jit(solution)/shard_map/pallas_call | solution.py:213
  28.0 1.2 %collective-permute-done.3.taken_ref = bf16[8,384,128]{2,1,0:T(8,128)(2,1)S(1)} collective-permute-done((bf16[8,384,128]{2,1,0:T(8,128)(2,1)S(1)}, bf16[8,384,128]{2,1,0:T(8,128)(2,1)S(1)}, u32[]{:S(2)}, u32[]{:S(2)}) %collective-permute-start.3) | collective-permute-done | bytes 786464 | tf_op jit(solution)/shard_map/ppermute | solution.py:329
  29.1 1.0 %shard_map.63 = (bf16[8,384,128]{2,1,0:T(8,128)(2,1)}, bf16[2,3,6,2,512]{4,3,2,1,0:T(2,128)(2,1)S(1)}) custom-call(bf16[8,384,128]{2,1,0:T(8,128)(2,1)S(1)} %get-tuple-element.34.keep_ref, bf16[8,384,128]{2,1,0:T(8,128)(2,1)S(1)} %collective-permute-done.3.taken_ref, ...), custom_call_target="tpu_custom_call", output_to_operand_aliasing={{1}: (2, {})} | custom-call | tf_op jit(solution)/shard_map/pallas_call | solution.py:235
  30.1 0.0 copy-start
  30.1 6.3 %all-to-all-start = ((bf16[8,384,128]{2,1,0:T(8,128)(2,1)}), bf16[8,384,128]{2,1,0:T(8,128)(2,1)S(1)}, u32[]{:S(2)}, u32[]{:S(2)}) async-start(bf16[8,384,128]{2,1,0:T(8,128)(2,1)} %get-tuple-element.38), calls=%async_computation | async-start | bytes 1572864 | tf_op jit(solution)/shard_map/all_to_all | solution.py:332
  36.5 2.9 %collective-permute-start.4 = (bf16[2,3,6,2,512]{4,3,2,1,0:T(2,128)(2,1)S(1)}, bf16[2,3,6,2,512]{4,3,2,1,0:T(2,128)(2,1)S(1)}, u32[]{:S(2)}, u32[]{:S(2)}) collective-permute-start(bf16[2,3,6,2,512]{4,3,2,1,0:T(2,128)(2,1)S(1)} %get-tuple-element.37), channel_id=1, source_target_pairs={{0,504},{8,0},{16,8},{24,16},{32,24},{40,32},{48,40},{56,48},{64,5... | collective-permute-start | bytes 221192 | tf_op jit(solution)/shard_map/ppermute | solution.py:307
  39.3 7.7 %all-to-all-done.parts_ref = bf16[8,384,128]{2,1,0:T(8,128)(2,1)S(1)} async-done(((bf16[8,384,128]{2,1,0:T(8,128)(2,1)}), bf16[8,384,128]{2,1,0:T(8,128)(2,1)S(1)}, u32[]{:S(2)}, u32[]{:S(2)}) %all-to-all-start) | async-done | bytes 786464 | tf_op jit(solution)/shard_map/all_to_all | solution.py:332
  47.0 0.8 %shard_map.64 = (bf16[32,8,192]{2,1,0:T(8,128)(2,1)}, bf16[3,6,2,512]{3,2,1,0:T(2,128)(2,1)S(1)}) custom-call(bf16[8,384,128]{2,1,0:T(8,128)(2,1)S(1)} %all-to-all-done.parts_ref, bf16[3,6,2,512]{3,2,1,0:T(2,128)(2,1)S(1)} %get-tuple-element.39.lat_in), custom_call_target="tpu_custom_call", output_to_operand_aliasing={{1}: (1, {})} | custom-call | tf_op jit(solution)/shard_map/pallas_call | solution.py:293
  47.8 7.8 %all-to-all-start.1 = ((bf16[32,8,192]{2,1,0:T(8,128)(2,1)}), bf16[32,8,192]{2,1,0:T(8,128)(2,1)S(1)}, u32[]{:S(2)}, u32[]{:S(2)}) async-start(bf16[32,8,192]{2,1,0:T(8,128)(2,1)} %get-tuple-element.41), calls=%async_computation.1 | async-start | bytes 262144 | tf_op jit(solution)/shard_map/all_to_all | solution.py:336
  55.6 0.0 collective-permute-done.4.side_ref
  55.7 0.1 pad_maximum_fusion
  55.8 2.8 %collective-permute-start.5 = (bf16[2,3,6,2,512]{4,3,2,1,0:T(2,128)(2,1)S(1)}, bf16[2,3,6,2,512]{4,3,2,1,0:T(2,128)(2,1)S(1)}, u32[]{:S(2)}, u32[]{:S(2)}) collective-permute-start(bf16[2,3,6,2,512]{4,3,2,1,0:T(2,128)(2,1)S(1)} %pad_maximum_fusion), channel_id=1, source_target_pairs={{0,7},{1,0},{2,1},{3,2},{4,3},{5,4},{6,5},{7,6},{8,15},{9,8},{10,9... | collective-permute-start | bytes 221192 | tf_op jit(solution)/shard_map/ppermute | solution.py:307
  58.6 5.7 %collective-permute-done.5.ahead_ref = bf16[2,3,6,2,512]{4,3,2,1,0:T(2,128)(2,1)S(1)} collective-permute-done((bf16[2,3,6,2,512]{4,3,2,1,0:T(2,128)(2,1)S(1)}, bf16[2,3,6,2,512]{4,3,2,1,0:T(2,128)(2,1)S(1)}, u32[]{:S(2)}, u32[]{:S(2)}) %collective-permute-start.5) | collective-permute-done | bytes 73760 | tf_op jit(solution)/shard_map/ppermute | solution.py:307
  64.3 0.0 all-to-all-done.1.rows_ref
  64.3 0.0 copy-done
  64.3 0.9 %shard_map.65 = (bf16[6,12,2,512]{3,2,1,0:T(2,128)(2,1)}, f32[8,192]{1,0:T(8,128)}) custom-call(bf16[6,12,2,512]{3,2,1,0:T(2,128)(2,1)S(1)} %bitcast.5, bf16[3,6,2,512]{3,2,1,0:T(2,128)(2,1)S(1)} %get-tuple-element.33.own_ref, bf16[2,3,6,2,512]{4,3,2,1,0:T(2,128)(2,1)S(1)} %collective-permute-done.4.side_ref, ...), custom_call_target="tpu_custom_call" | custom-call | tf_op jit(solution)/shard_map/pallas_call | solution.py:269
  (1 shorter events, 0.0 us)
Async XLA Ops:
  1.6 16.4 %collective-permute-start = (bf16[2,3,6,2,512]{4,3,2,1,0:T(2,128)(2,1)S(1)}, bf16[2,3,6,2,512]{4,3,2,1,0:T(2,128)(2,1)S(1)}, u32[]{:S(2)}, u32[]{:S(2)}) collective-permute-start(bf16[2,3,6,2,512]{4,3,2,1,0:T(2,128)(2,1)S(1)} %get-tuple-element.23), channel_id=1, source_target_pairs={{0,9},{1,10},{2,11},{3,12},{4,13},{5,14},{6,15},{7,8},{8,17},{9,18... | collective-permute-start | bytes 221192 | tf_op jit(solution)/shard_map/ppermute | solution.py:317
  5.2 12.7 %collective-permute-start.1 = (bf16[2,3,6,2,512]{4,3,2,1,0:T(2,128)(2,1)S(1)}, bf16[2,3,6,2,512]{4,3,2,1,0:T(2,128)(2,1)S(1)}, u32[]{:S(2)}, u32[]{:S(2)}) collective-permute-start(bf16[2,3,6,2,512]{4,3,2,1,0:T(2,128)(2,1)S(1)} %get-tuple-element.24), channel_id=1, source_target_pairs={{0,1},{1,2},{2,3},{3,4},{4,5},{5,6},{6,7},{7,0},{8,9},{9,10},{10,1... | collective-permute-start | bytes 221192 | tf_op jit(solution)/shard_map/ppermute | solution.py:307
  8.7 13.3 %collective-permute-start.2 = (bf16[2,3,6,2,512]{4,3,2,1,0:T(2,128)(2,1)S(1)}, bf16[2,3,6,2,512]{4,3,2,1,0:T(2,128)(2,1)S(1)}, u32[]{:S(2)}, u32[]{:S(2)}) collective-permute-start(bf16[2,3,6,2,512]{4,3,2,1,0:T(2,128)(2,1)S(1)} %get-tuple-element.25), channel_id=1, source_target_pairs={{0,8},{8,16},{16,24},{24,32},{32,40},{40,48},{48,56},{56,64},{64,7... | collective-permute-start | bytes 221192 | tf_op jit(solution)/shard_map/ppermute | solution.py:307
  12.0 1.0 %copy-start.1 = (bf16[512,512]{1,0:T(8,128)(2,1)S(1)}, bf16[512,512]{1,0:T(8,128)(2,1)}, u32[]{:S(2)}) copy-start(bf16[512,512]{1,0:T(8,128)(2,1)} %refs_1_.1) | copy-start | bytes 1572868
  25.0 4.2 %collective-permute-start.3 = (bf16[8,384,128]{2,1,0:T(8,128)(2,1)S(1)}, bf16[8,384,128]{2,1,0:T(8,128)(2,1)S(1)}, u32[]{:S(2)}, u32[]{:S(2)}) collective-permute-start(bf16[8,384,128]{2,1,0:T(8,128)(2,1)S(1)} %get-tuple-element.35), channel_id=1, source_target_pairs={{0,8},{8,0},{1,9},{9,1},{2,10},{10,2},{3,11},{11,3},{4,12},{12,4},... | collective-permute-start | bytes 2359304 | tf_op jit(solution)/shard_map/ppermute | solution.py:329
  30.1 34.2 %copy-start = (bf16[2,6,12,512]{3,0,2,1:T(2,128)(2,1)S(1)}, bf16[2,6,12,512]{3,0,2,1:T(2,128)(2,1)}, u32[]{:S(2)}) copy-start(bf16[2,6,12,512]{3,0,2,1:T(2,128)(2,1)} %param.5) | copy-start | bytes 442372
  30.1 16.9 %all-to-all-start = ((bf16[8,384,128]{2,1,0:T(8,128)(2,1)}), bf16[8,384,128]{2,1,0:T(8,128)(2,1)S(1)}, u32[]{:S(2)}, u32[]{:S(2)}) async-start(bf16[8,384,128]{2,1,0:T(8,128)(2,1)} %get-tuple-element.38), calls=%async_computation | async-start | bytes 1572864 | tf_op jit(solution)/shard_map/all_to_all | solution.py:332
  36.5 19.2 %collective-permute-start.4 = (bf16[2,3,6,2,512]{4,3,2,1,0:T(2,128)(2,1)S(1)}, bf16[2,3,6,2,512]{4,3,2,1,0:T(2,128)(2,1)S(1)}, u32[]{:S(2)}, u32[]{:S(2)}) collective-permute-start(bf16[2,3,6,2,512]{4,3,2,1,0:T(2,128)(2,1)S(1)} %get-tuple-element.37), channel_id=1, source_target_pairs={{0,504},{8,0},{16,8},{24,16},{32,24},{40,32},{48,40},{56,48},{64,5... | collective-permute-start | bytes 221192 | tf_op jit(solution)/shard_map/ppermute | solution.py:307
  47.8 16.5 %all-to-all-start.1 = ((bf16[32,8,192]{2,1,0:T(8,128)(2,1)}), bf16[32,8,192]{2,1,0:T(8,128)(2,1)S(1)}, u32[]{:S(2)}, u32[]{:S(2)}) async-start(bf16[32,8,192]{2,1,0:T(8,128)(2,1)} %get-tuple-element.41), calls=%async_computation.1 | async-start | bytes 262144 | tf_op jit(solution)/shard_map/all_to_all | solution.py:336
  55.8 8.5 %collective-permute-start.5 = (bf16[2,3,6,2,512]{4,3,2,1,0:T(2,128)(2,1)S(1)}, bf16[2,3,6,2,512]{4,3,2,1,0:T(2,128)(2,1)S(1)}, u32[]{:S(2)}, u32[]{:S(2)}) collective-permute-start(bf16[2,3,6,2,512]{4,3,2,1,0:T(2,128)(2,1)S(1)} %pad_maximum_fusion), channel_id=1, source_target_pairs={{0,7},{1,0},{2,1},{3,2},{4,3},{5,4},{6,5},{7,6},{8,15},{9,8},{10,9... | collective-permute-start | bytes 221192 | tf_op jit(solution)/shard_map/ppermute | solution.py:307

commit v7 on v6

--- a/solution.py
+++ b/solution.py
@@ -88,7 +88,7 @@
 
 def window_kernel(
     diag_ref, lat_ref, lon_ref, own_ref, w_qkv_ref, w_proj_ref,
-    send_ref, d_qkv_ref, unit_ref, turned_ref, inv_std_ref,
+    factors_ref, unit_ref, inv_std_ref,
 ):
     pieces = [
         [ref[array].astype(F32).reshape(PIECE, WIDTH) for array in range(2)]
@@ -101,9 +101,9 @@
     inv_std = lax.rsqrt(jnp.mean(centred * centred, axis=-1, keepdims=True) + EPS)
     unit = centred * inv_std
     unit_ref[...] = unit
-    turned_ref[...] = unit.T.reshape(turned_ref.shape)
     inv_std_ref[...] = jnp.broadcast_to(inv_std, inv_std_ref.shape)
     normed = unit.astype(BF16)
+    factors_ref[:, 3 * WIDTH:] = normed
     qkv = jnp.dot(normed, w_qkv_ref[...], preferred_element_type=F32).astype(BF16)
     d_att = dot(grads, w_proj_ref[...], NT).astype(BF16)
 
@@ -139,62 +139,53 @@
         inner = jnp.sum(probs * d_probs, axis=0, keepdims=True)
         d_scores = (probs * (d_probs - inner) * scaling).astype(BF16)
         d_keys = jnp.dot(d_scores, queries_spread, preferred_element_type=F32)
-        d_queries_spread = dot(d_scores, keys, TN)
-        d_queries = jnp.zeros((TOKENS, LANES), F32)
-        for head in range(GROUP):
-            rows = d_queries_spread[head * TOKENS:(head + 1) * TOKENS]
-            d_queries = jnp.where(column_head == head, rows, d_queries)
+        turned = dot(keys, d_scores, TN)
+        d_queries = jnp.concatenate([
+            turned[head * HEAD_WIDTH:(head + 1) * HEAD_WIDTH, head * TOKENS:(head + 1) * TOKENS]
+            for head in range(GROUP)
+        ], axis=0).T
         for where, block in ((0, d_queries), (1, d_keys), (2, d_vals)):
             start = where * WIDTH + group * LANES
-            d_qkv_ref[:, start:start + LANES] = block.astype(BF16)
-
-    weight_rows(turned_ref, 1 - lax.axis_index("c"), d_qkv_ref, send_ref)
-
-
-def weight_rows(turned_ref, core, d_qkv_ref, out_ref):
-    turned = turned_ref[:, pl.ds(core, 1)].reshape(WIDTH // 2, TOKENS).astype(BF16)
+            factors_ref[:, start:start + LANES] = block.astype(BF16)
+
+
+def weight_rows(unit, turned_ref, factors_ref):
+    turned_ref[...] = unit.T.reshape(turned_ref.shape)
+    turned = turned_ref[:, pl.ds(lax.axis_index("c"), 1)].reshape(WIDTH // 2, TOKENS).astype(BF16)
     left = lax.broadcasted_iota(jnp.int32, (128, 128), 1) < 64
     for pair in range(4):
-        columns = d_qkv_ref[:, pair * 384:(pair + 1) * 384]
+        columns = factors_ref[:, pair * 384:(pair + 1) * 384]
         block = jnp.dot(turned, columns, preferred_element_type=F32)
         middle = block[:, 128:256]
         swapped = pltpu.roll(middle, 64, 1)
-        folded = (
-            jnp.where(left, middle[:128], swapped[128:]),
-            jnp.where(left, swapped[:128], middle[128:]),
-        )
-        for side in range(2):
-            whole = block[:, 256 * side:256 * side + 128]
-            place = 2 * pair + side
-            out_ref[place, :256, :] = whole.astype(BF16)
-            out_ref[place, 256:, :] = folded[side].astype(BF16)
+        yield 2 * pair, block[:, :128], jnp.where(left, middle[:128], swapped[128:])
+        yield 2 * pair + 1, block[:, 256:], jnp.where(left, swapped[:128], middle[128:])
+
+
+TURNED = (WIDTH // 16, 2, 8, TOKENS)
 
 
 def window_pass(diag, lat, lon, own, w_qkv, w_proj):
-    weight = jax.ShapeDtypeStruct((8, 384, 128), BF16)
-    vmem = pl.BlockSpec(memory_space=pltpu.VMEM)
     return pl.pallas_call(
         window_kernel,
         out_shape=[
-            weight,
-            jax.ShapeDtypeStruct((TOKENS, 3 * WIDTH), BF16),
+            jax.ShapeDtypeStruct((TOKENS, 4 * WIDTH), BF16),
             jax.ShapeDtypeStruct((TOKENS, WIDTH), F32),
-            jax.ShapeDtypeStruct((WIDTH // 16, 2, 8, TOKENS), F32),
             jax.ShapeDtypeStruct((TOKENS, 128), F32),
         ],
-        in_specs=[vmem] * 6,
-        out_specs=[vmem] * 5,
         compiler_params=pltpu.CompilerParams(vmem_limit_bytes=WINDOW),
     )(diag, lat, lon, own, w_qkv, w_proj)
 
 
 def inputs_kernel(
-    d_qkv_ref, unit_ref, turned_ref, inv_std_ref, w_qkv_ref,
-    keep_ref, d_own_ref, d_side_ref, d_lat_ref,
+    factors_ref, unit_ref, inv_std_ref, w_qkv_ref,
+    keep_ref, d_own_ref, d_side_ref, d_lat_ref, turned_ref,
 ):
-    weight_rows(turned_ref, lax.axis_index("c"), d_qkv_ref, keep_ref)
     unit = unit_ref[...]
-    d_normed = dot(d_qkv_ref[...], w_qkv_ref[...], NT)
+    for index, whole, folded in weight_rows(unit, turned_ref, factors_ref):
+        keep_ref[index, :256, :] = whole
+        keep_ref[index, 256:, :] = folded
+    d_normed = dot(factors_ref[:, :3 * WIDTH], w_qkv_ref[...], NT)
     d_inputs = inv_std_ref[:, :1] * (
         d_normed
         - jnp.mean(d_normed, axis=-1, keepdims=True)
@@ -206,22 +197,24 @@
         ref[...] = block.reshape(3, 6, 2, WIDTH).astype(BF16)
 
 
-def inputs_pass(d_qkv, unit, turned, inv_std, w_qkv):
-    weight = jax.ShapeDtypeStruct((8, 384, 128), BF16)
+def inputs_pass(factors, unit, inv_std, w_qkv):
+    weight = jax.ShapeDtypeStruct((8, 384, 128), F32)
     piece = jax.ShapeDtypeStruct((3, 6, 2, WIDTH), BF16)
     side = jax.ShapeDtypeStruct((2, 3, 6, 2, WIDTH), BF16)
     return pl.pallas_call(
         inputs_kernel,
         out_shape=[weight, piece, side, piece],
+        scratch_shapes=[pltpu.VMEM(TURNED, F32)],
         compiler_params=SMALL,
-    )(d_qkv, unit, turned, inv_std, w_qkv)
-
-
-def add_kernel(keep_ref, taken_ref, side_in, out_ref, side_out, hold_ref, sems):
+    )(factors, unit, inv_std, w_qkv)
+
+
+def add_kernel(keep_ref, taken_ref, side_in, out_ref, side_out, hold_ref, turned_ref, sems):
     stores = []
-    for index in range(8):
-        total = keep_ref[index].astype(F32) + taken_ref[index].astype(F32)
-        hold_ref[index] = total.astype(BF16)
+    unit = taken_ref[:, 3 * WIDTH:].astype(F32)
+    for index, whole, folded in weight_rows(unit, turned_ref, taken_ref):
+        hold_ref[index, :256, :] = (keep_ref[index, :256, :] + whole).astype(BF16)
+        hold_ref[index, 256:, :] = (keep_ref[index, 256:, :] + folded).astype(BF16)
         store = pltpu.make_async_copy(hold_ref.at[index], out_ref.at[index], sems.at[index])
         store.start()
         stores.append(store)
@@ -234,11 +227,17 @@
     anywhere = pl.BlockSpec(memory_space=pl.ANY)
     return pl.pallas_call(
         add_kernel,
-        out_shape=[jax.ShapeDtypeStruct(a.shape, a.dtype) for a in (keep, side)],
+        out_shape=[
+            jax.ShapeDtypeStruct(keep.shape, BF16), jax.ShapeDtypeStruct(side.shape, BF16)
+        ],
         in_specs=[vmem] * 2 + [anywhere],
         out_specs=[anywhere] * 2,
         input_output_aliases={2: 1},
-        scratch_shapes=[pltpu.VMEM(keep.shape, BF16), pltpu.SemaphoreType.DMA((8,))],
+        scratch_shapes=[
+            pltpu.VMEM(keep.shape, BF16),
+            pltpu.VMEM(TURNED, F32),
+            pltpu.SemaphoreType.DMA((8,)),
+        ],
         compiler_params=SMALL,
     )(keep, taken, side)
 
@@ -325,9 +324,9 @@
     lon = turn(to_lon, LON, 1)
     lat = turn(to_lat, LAT, 1)
     w_qkv, w_proj = load(w_qkv, w_proj)
-    send, *saved = window_pass(diag, lat, lon, own, w_qkv, w_proj)
-    taken = lax.ppermute(send, "c", [(0, 1), (1, 0)])
-    keep, d_own, d_side, d_lat = inputs_pass(*saved, w_qkv)
+    factors, unit, inv_std = window_pass(diag, lat, lon, own, w_qkv, w_proj)
+    taken = lax.ppermute(factors, "c", [(0, 1), (1, 0)])
+    keep, d_own, d_side, d_lat = inputs_pass(factors, unit, inv_std, w_qkv)
     chip, d_side = add(keep, taken, d_side)
     by_columns = lax.all_to_all(chip, LAT, 0, 0)
     d_side = turn(d_side, LON, -1)

time: 65.7 us -> 65.4 us (level)
  no operation moved by 1% of the time
where the time goes in v7:
time: 65.4 us; the launch traced here: 64.8 us
  starting transfers between devices  32.1 us (49%)
  waiting for transfers between devices  21.6 us (33%)
  Pallas kernels  9.18 us (14%)
  local copies, waits for them, and re-layouts  1.07 us (2%)
  between operations  0.77 us (1%)
    ppermute x4, starting transfers between devices, turn(): lax.ppermute(block, axes, [(i, (i + distance) % count) for i in range(cou...  12.4 us
    ppermute x4, waiting for transfers between devices, turn(): lax.ppermute(block, axes, [(i, (i + distance) % count) for i in range(cou...  9.7 us
    all_to_all x1, starting transfers between devices, per_device(): by_rows = lax.all_to_all(rows, LON, 0, 0, axis_index_groups=groups)  7.83 us
    all_to_all x1, waiting for transfers between devices, per_device(): by_columns = lax.all_to_all(chip, LAT, 0, 0)  7.69 us
    all_to_all x1, starting transfers between devices, per_device(): by_columns = lax.all_to_all(chip, LAT, 0, 0)  6.31 us
    ppermute x1, starting transfers between devices, turn_both(): return lax.ppermute(block, LON + LAT, route)  3.63 us
    ppermute x1, waiting for transfers between devices, turn_both(): return lax.ppermute(block, LON + LAT, route)  3.5 us
    pallas_call x1, Pallas kernels, window_pass(): pl.pallas_call(window_kernel, out_shape=[jax.ShapeDtypeStruct((TOKENS, 4...  2.47 us
  transfers between devices with their start and end apart: 8, of which 5 were waited for; matrix products, arithmetic and copies ran while one was open for 0% of the time, Pallas kernels for 5%

profile of v7, /device:TPU:6, one launch (start us, length us, event | category | flops | bytes accessed | tf_op | source)
XLA Modules:
  0.0 64.8 jit_solution(13925383511156508742)
XLA Ops:
  0.6 1.0 %shard_map.59 = (bf16[2,3,6,2,512]{4,3,2,1,0:T(2,128)(2,1)S(1)}, bf16[2,3,6,2,512]{4,3,2,1,0:T(2,128)(2,1)S(1)}, bf16[2,3,6,2,512]{4,3,2,1,0:T(2,128)(2,1)S(1)}, bf16[2,3,6,2,512]{4,3,2,1,0:T(2,128)(2,1)S(1)}) custom-call(bf16[6,12,2,512]{3,2,1,0:T(2,128)(2,1)} %bitcast.7, bf16[6,12,2,512]{3,2,1,0:T(2,128)(2,1)} %bitcast.4), custom_call_target="tpu_custom_call" | custom-call | tf_op jit(solution)/shard_map/pallas_call | solution.py:57
  1.6 3.6 %collective-permute-start = (bf16[2,3,6,2,512]{4,3,2,1,0:T(2,128)(2,1)S(1)}, bf16[2,3,6,2,512]{4,3,2,1,0:T(2,128)(2,1)S(1)}, u32[]{:S(2)}, u32[]{:S(2)}) collective-permute-start(bf16[2,3,6,2,512]{4,3,2,1,0:T(2,128)(2,1)S(1)} %get-tuple-element.21), channel_id=1, source_target_pairs={{0,9},{1,10},{2,11},{3,12},{4,13},{5,14},{6,15},{7,8},{8,17},{9,18... | collective-permute-start | bytes 221192 | tf_op jit(solution)/shard_map/ppermute | solution.py:316
  5.2 3.4 %collective-permute-start.1 = (bf16[2,3,6,2,512]{4,3,2,1,0:T(2,128)(2,1)S(1)}, bf16[2,3,6,2,512]{4,3,2,1,0:T(2,128)(2,1)S(1)}, u32[]{:S(2)}, u32[]{:S(2)}) collective-permute-start(bf16[2,3,6,2,512]{4,3,2,1,0:T(2,128)(2,1)S(1)} %get-tuple-element.22), channel_id=1, source_target_pairs={{0,1},{1,2},{2,3},{3,4},{4,5},{5,6},{6,7},{7,0},{8,9},{9,10},{10,1... | collective-permute-start | bytes 221192 | tf_op jit(solution)/shard_map/ppermute | solution.py:306
  8.7 3.3 %collective-permute-start.2 = (bf16[2,3,6,2,512]{4,3,2,1,0:T(2,128)(2,1)S(1)}, bf16[2,3,6,2,512]{4,3,2,1,0:T(2,128)(2,1)S(1)}, u32[]{:S(2)}, u32[]{:S(2)}) collective-permute-start(bf16[2,3,6,2,512]{4,3,2,1,0:T(2,128)(2,1)S(1)} %get-tuple-element.23), channel_id=1, source_target_pairs={{0,8},{8,16},{16,24},{24,32},{32,40},{40,48},{48,56},{56,64},{64,7... | collective-permute-start | bytes 221192 | tf_op jit(solution)/shard_map/ppermute | solution.py:306
  12.0 0.0 copy-start.1
  12.0 1.0 %copy-done.1 = bf16[512,512]{1,0:T(8,128)(2,1)S(1)} copy-done((bf16[512,512]{1,0:T(8,128)(2,1)S(1)}, bf16[512,512]{1,0:T(8,128)(2,1)}, u32[]{:S(2)}) %copy-start.1) | copy-done | bytes 524312
  13.0 1.4 %shard_map.60 = (bf16[512,1536]{1,0:T(8,128)(2,1)S(1)}, bf16[512,512]{1,0:T(8,128)(2,1)S(1)}) custom-call(bf16[512,1536]{1,0:T(8,128)(2,1)} %refs_0_.1, bf16[512,512]{1,0:T(8,128)(2,1)S(1)} %copy-done.1), custom_call_target="tpu_custom_call" | custom-call | tf_op jit(solution)/shard_map/pallas_call | solution.py:79
  14.5 3.5 %collective-permute-done.diag_ref = bf16[2,3,6,2,512]{4,3,2,1,0:T(2,128)(2,1)S(1)} collective-permute-done((bf16[2,3,6,2,512]{4,3,2,1,0:T(2,128)(2,1)S(1)}, bf16[2,3,6,2,512]{4,3,2,1,0:T(2,128)(2,1)S(1)}, u32[]{:S(2)}, u32[]{:S(2)}) %collective-permute-start) | collective-permute-done | bytes 73760 | tf_op jit(solution)/shard_map/ppermute | solution.py:316
  18.0 0.0 collective-permute-done.1.lat_ref
  18.0 4.0 %collective-permute-done.2.lon_ref = bf16[2,3,6,2,512]{4,3,2,1,0:T(2,128)(2,1)S(1)} collective-permute-done((bf16[2,3,6,2,512]{4,3,2,1,0:T(2,128)(2,1)S(1)}, bf16[2,3,6,2,512]{4,3,2,1,0:T(2,128)(2,1)S(1)}, u32[]{:S(2)}, u32[]{:S(2)}) %collective-permute-start.2) | collective-permute-done | bytes 73760 | tf_op jit(solution)/shard_map/ppermute | solution.py:306
  22.0 2.5 %shard_map.61 = (bf16[144,2048]{1,0:T(8,128)(2,1)S(1)}, f32[144,512]{1,0:T(8,128)S(1)}, f32[144,128]{1,0:T(8,128)S(1)}) custom-call(bf16[2,3,6,2,512]{4,3,2,1,0:T(2,128)(2,1)S(1)} %collective-permute-done.diag_ref, bf16[2,3,6,2,512]{4,3,2,1,0:T(2,128)(2,1)S(1)} %collective-permute-done.1.lat_ref, ...), custom_call_target="tpu_custom_call" | custom-call | tf_op jit(solution)/shard_map/pallas_call | solution.py:169
  24.5 1.9 %collective-permute-start.3 = (bf16[144,2048]{1,0:T(8,128)(2,1)S(1)}, bf16[144,2048]{1,0:T(8,128)(2,1)S(1)}, u32[]{:S(2)}, u32[]{:S(2)}) collective-permute-start(bf16[144,2048]{1,0:T(8,128)(2,1)S(1)} %get-tuple-element.27.factors_ref), channel_id=1, source_target_pairs={{0,8},{8,0},{1,9},{9,1},{2,10},{10,2},{3,11},{11,3},{4,12},{12,4},... | collective-permute-start | bytes 1769480 | tf_op jit(solution)/shard_map/ppermute | solution.py:328
  26.4 1.3 %shard_map.62 = (f32[8,384,128]{2,1,0:T(8,128)S(1)}, bf16[3,6,2,512]{3,2,1,0:T(2,128)(2,1)S(1)}, bf16[2,3,6,2,512]{4,3,2,1,0:T(2,128)(2,1)S(1)}, bf16[3,6,2,512]{3,2,1,0:T(2,128)(2,1)S(1)}) custom-call(bf16[144,2048]{1,0:T(8,128)(2,1)S(1)} %get-tuple-element.27.factors_ref, f32[144,512]{1,0:T(8,128)S(1)} %get-tuple-element.28.unit_ref, ...), custom_call_target="tpu_custom_call" | custom-call | tf_op jit(solution)/shard_map/pallas_call | solution.py:204
  27.7 0.7 %collective-permute-done.3.taken_ref = bf16[144,2048]{1,0:T(8,128)(2,1)S(1)} collective-permute-done((bf16[144,2048]{1,0:T(8,128)(2,1)S(1)}, bf16[144,2048]{1,0:T(8,128)(2,1)S(1)}, u32[]{:S(2)}, u32[]{:S(2)}) %collective-permute-start.3) | collective-permute-done | bytes 589856 | tf_op jit(solution)/shard_map/ppermute | solution.py:328
  28.4 1.4 %shard_map.63 = (bf16[8,384,128]{2,1,0:T(8,128)(2,1)}, bf16[2,3,6,2,512]{4,3,2,1,0:T(2,128)(2,1)S(1)}) custom-call(f32[8,384,128]{2,1,0:T(8,128)S(1)} %get-tuple-element.31.keep_ref, bf16[144,2048]{1,0:T(8,128)(2,1)S(1)} %collective-permute-done.3.taken_ref, bf16[2,3,6,2,512]{4,3,2,1,0:T(2,128)(2,1)S(1)} %get-tuple-element.32.side_in), custom_call_target="tpu_custom_call", output_to_operand_aliasing={{1}: (2, {})} | custom-call | tf_op jit(solution)/shard_map/pallas_call | solution.py:228
  29.7 0.0 copy-start
  29.7 6.3 %all-to-all-start = ((bf16[8,384,128]{2,1,0:T(8,128)(2,1)}), bf16[8,384,128]{2,1,0:T(8,128)(2,1)S(1)}, u32[]{:S(2)}, u32[]{:S(2)}) async-start(bf16[8,384,128]{2,1,0:T(8,128)(2,1)} %get-tuple-element.34), calls=%async_computation | async-start | bytes 1572864 | tf_op jit(solution)/shard_map/all_to_all | solution.py:331
  36.1 2.9 %collective-permute-start.4 = (bf16[2,3,6,2,512]{4,3,2,1,0:T(2,128)(2,1)S(1)}, bf16[2,3,6,2,512]{4,3,2,1,0:T(2,128)(2,1)S(1)}, u32[]{:S(2)}, u32[]{:S(2)}) collective-permute-start(bf16[2,3,6,2,512]{4,3,2,1,0:T(2,128)(2,1)S(1)} %get-tuple-element.33), channel_id=1, source_target_pairs={{0,504},{8,0},{16,8},{24,16},{32,24},{40,32},{48,40},{56,48},{64,5... | collective-permute-start | bytes 221192 | tf_op jit(solution)/shard_map/ppermute | solution.py:306
  38.9 7.7 %all-to-all-done.parts_ref = bf16[8,384,128]{2,1,0:T(8,128)(2,1)S(1)} async-done(((bf16[8,384,128]{2,1,0:T(8,128)(2,1)}), bf16[8,384,128]{2,1,0:T(8,128)(2,1)S(1)}, u32[]{:S(2)}, u32[]{:S(2)}) %all-to-all-start) | async-done | bytes 786464 | tf_op jit(solution)/shard_map/all_to_all | solution.py:331
  46.6 0.8 %shard_map.64 = (bf16[32,8,192]{2,1,0:T(8,128)(2,1)}, bf16[3,6,2,512]{3,2,1,0:T(2,128)(2,1)S(1)}) custom-call(bf16[8,384,128]{2,1,0:T(8,128)(2,1)S(1)} %all-to-all-done.parts_ref, bf16[3,6,2,512]{3,2,1,0:T(2,128)(2,1)S(1)} %get-tuple-element.35.lat_in), custom_call_target="tpu_custom_call", output_to_operand_aliasing={{1}: (1, {})} | custom-call | tf_op jit(solution)/shard_map/pallas_call | solution.py:292
  47.4 7.8 %all-to-all-start.1 = ((bf16[32,8,192]{2,1,0:T(8,128)(2,1)}), bf16[32,8,192]{2,1,0:T(8,128)(2,1)S(1)}, u32[]{:S(2)}, u32[]{:S(2)}) async-start(bf16[32,8,192]{2,1,0:T(8,128)(2,1)} %get-tuple-element.37), calls=%async_computation.1 | async-start | bytes 262144 | tf_op jit(solution)/shard_map/all_to_all | solution.py:335
  55.3 0.0 collective-permute-done.4.side_ref
  55.3 0.1 pad_maximum_fusion
  55.4 2.8 %collective-permute-start.5 = (bf16[2,3,6,2,512]{4,3,2,1,0:T(2,128)(2,1)S(1)}, bf16[2,3,6,2,512]{4,3,2,1,0:T(2,128)(2,1)S(1)}, u32[]{:S(2)}, u32[]{:S(2)}) collective-permute-start(bf16[2,3,6,2,512]{4,3,2,1,0:T(2,128)(2,1)S(1)} %pad_maximum_fusion), channel_id=1, source_target_pairs={{0,7},{1,0},{2,1},{3,2},{4,3},{5,4},{6,5},{7,6},{8,15},{9,8},{10,9... | collective-permute-start | bytes 221192 | tf_op jit(solution)/shard_map/ppermute | solution.py:306
  58.2 5.7 %collective-permute-done.5.ahead_ref = bf16[2,3,6,2,512]{4,3,2,1,0:T(2,128)(2,1)S(1)} collective-permute-done((bf16[2,3,6,2,512]{4,3,2,1,0:T(2,128)(2,1)S(1)}, bf16[2,3,6,2,512]{4,3,2,1,0:T(2,128)(2,1)S(1)}, u32[]{:S(2)}, u32[]{:S(2)}) %collective-permute-start.5) | collective-permute-done | bytes 73760 | tf_op jit(solution)/shard_map/ppermute | solution.py:306
  63.9 0.0 all-to-all-done.1.rows_ref
  63.9 0.0 copy-done
  63.9 0.9 %shard_map.65 = (bf16[6,12,2,512]{3,2,1,0:T(2,128)(2,1)}, f32[8,192]{1,0:T(8,128)}) custom-call(bf16[6,12,2,512]{3,2,1,0:T(2,128)(2,1)S(1)} %bitcast.5, bf16[3,6,2,512]{3,2,1,0:T(2,128)(2,1)S(1)} %get-tuple-element.30.own_ref, bf16[2,3,6,2,512]{4,3,2,1,0:T(2,128)(2,1)S(1)} %collective-permute-done.4.side_ref, ...), custom_call_target="tpu_custom_call" | custom-call | tf_op jit(solution)/shard_map/pallas_call | solution.py:268
  (1 shorter events, 0.0 us)
Async XLA Ops:
  1.6 16.4 %collective-permute-start = (bf16[2,3,6,2,512]{4,3,2,1,0:T(2,128)(2,1)S(1)}, bf16[2,3,6,2,512]{4,3,2,1,0:T(2,128)(2,1)S(1)}, u32[]{:S(2)}, u32[]{:S(2)}) collective-permute-start(bf16[2,3,6,2,512]{4,3,2,1,0:T(2,128)(2,1)S(1)} %get-tuple-element.21), channel_id=1, source_target_pairs={{0,9},{1,10},{2,11},{3,12},{4,13},{5,14},{6,15},{7,8},{8,17},{9,18... | collective-permute-start | bytes 221192 | tf_op jit(solution)/shard_map/ppermute | solution.py:316
  5.2 12.7 %collective-permute-start.1 = (bf16[2,3,6,2,512]{4,3,2,1,0:T(2,128)(2,1)S(1)}, bf16[2,3,6,2,512]{4,3,2,1,0:T(2,128)(2,1)S(1)}, u32[]{:S(2)}, u32[]{:S(2)}) collective-permute-start(bf16[2,3,6,2,512]{4,3,2,1,0:T(2,128)(2,1)S(1)} %get-tuple-element.22), channel_id=1, source_target_pairs={{0,1},{1,2},{2,3},{3,4},{4,5},{5,6},{6,7},{7,0},{8,9},{9,10},{10,1... | collective-permute-start | bytes 221192 | tf_op jit(solution)/shard_map/ppermute | solution.py:306
  8.7 13.3 %collective-permute-start.2 = (bf16[2,3,6,2,512]{4,3,2,1,0:T(2,128)(2,1)S(1)}, bf16[2,3,6,2,512]{4,3,2,1,0:T(2,128)(2,1)S(1)}, u32[]{:S(2)}, u32[]{:S(2)}) collective-permute-start(bf16[2,3,6,2,512]{4,3,2,1,0:T(2,128)(2,1)S(1)} %get-tuple-element.23), channel_id=1, source_target_pairs={{0,8},{8,16},{16,24},{24,32},{32,40},{40,48},{48,56},{56,64},{64,7... | collective-permute-start | bytes 221192 | tf_op jit(solution)/shard_map/ppermute | solution.py:306
  12.0 1.0 %copy-start.1 = (bf16[512,512]{1,0:T(8,128)(2,1)S(1)}, bf16[512,512]{1,0:T(8,128)(2,1)}, u32[]{:S(2)}) copy-start(bf16[512,512]{1,0:T(8,128)(2,1)} %refs_1_.1) | copy-start | bytes 1572868
  24.5 3.9 %collective-permute-start.3 = (bf16[144,2048]{1,0:T(8,128)(2,1)S(1)}, bf16[144,2048]{1,0:T(8,128)(2,1)S(1)}, u32[]{:S(2)}, u32[]{:S(2)}) collective-permute-start(bf16[144,2048]{1,0:T(8,128)(2,1)S(1)} %get-tuple-element.27.factors_ref), channel_id=1, source_target_pairs={{0,8},{8,0},{1,9},{9,1},{2,10},{10,2},{3,11},{11,3},{4,12},{12,4},... | collective-permute-start | bytes 1769480 | tf_op jit(solution)/shard_map/ppermute | solution.py:328
  29.7 34.2 %copy-start = (bf16[2,6,12,512]{3,0,2,1:T(2,128)(2,1)S(1)}, bf16[2,6,12,512]{3,0,2,1:T(2,128)(2,1)}, u32[]{:S(2)}) copy-start(bf16[2,6,12,512]{3,0,2,1:T(2,128)(2,1)} %param.5) | copy-start | bytes 442372
  29.7 16.9 %all-to-all-start = ((bf16[8,384,128]{2,1,0:T(8,128)(2,1)}), bf16[8,384,128]{2,1,0:T(8,128)(2,1)S(1)}, u32[]{:S(2)}, u32[]{:S(2)}) async-start(bf16[8,384,128]{2,1,0:T(8,128)(2,1)} %get-tuple-element.34), calls=%async_computation | async-start | bytes 1572864 | tf_op jit(solution)/shard_map/all_to_all | solution.py:331
  36.1 19.2 %collective-permute-start.4 = (bf16[2,3,6,2,512]{4,3,2,1,0:T(2,128)(2,1)S(1)}, bf16[2,3,6,2,512]{4,3,2,1,0:T(2,128)(2,1)S(1)}, u32[]{:S(2)}, u32[]{:S(2)}) collective-permute-start(bf16[2,3,6,2,512]{4,3,2,1,0:T(2,128)(2,1)S(1)} %get-tuple-element.33), channel_id=1, source_target_pairs={{0,504},{8,0},{16,8},{24,16},{32,24},{40,32},{48,40},{56,48},{64,5... | collective-permute-start | bytes 221192 | tf_op jit(solution)/shard_map/ppermute | solution.py:306
  47.4 16.5 %all-to-all-start.1 = ((bf16[32,8,192]{2,1,0:T(8,128)(2,1)}), bf16[32,8,192]{2,1,0:T(8,128)(2,1)S(1)}, u32[]{:S(2)}, u32[]{:S(2)}) async-start(bf16[32,8,192]{2,1,0:T(8,128)(2,1)} %get-tuple-element.37), calls=%async_computation.1 | async-start | bytes 262144 | tf_op jit(solution)/shard_map/all_to_all | solution.py:335
  55.4 8.5 %collective-permute-start.5 = (bf16[2,3,6,2,512]{4,3,2,1,0:T(2,128)(2,1)S(1)}, bf16[2,3,6,2,512]{4,3,2,1,0:T(2,128)(2,1)S(1)}, u32[]{:S(2)}, u32[]{:S(2)}) collective-permute-start(bf16[2,3,6,2,512]{4,3,2,1,0:T(2,128)(2,1)S(1)} %pad_maximum_fusion), channel_id=1, source_target_pairs={{0,7},{1,0},{2,1},{3,2},{4,3},{5,4},{6,5},{7,6},{8,15},{9,8},{10,9... | collective-permute-start | bytes 221192 | tf_op jit(solution)/shard_map/ppermute | solution.py:306

commit v8 on v7

--- a/solution.py
+++ b/solution.py
@@ -103,7 +103,7 @@
     unit_ref[...] = unit
     inv_std_ref[...] = jnp.broadcast_to(inv_std, inv_std_ref.shape)
     normed = unit.astype(BF16)
-    factors_ref[:, 3 * WIDTH:] = normed
+    factors_ref[:, 3 * WIDTH:] = owned(normed, 1 - lax.axis_index("c")).astype(BF16)
     qkv = jnp.dot(normed, w_qkv_ref[...], preferred_element_type=F32).astype(BF16)
     d_att = dot(grads, w_proj_ref[...], NT).astype(BF16)
 
@@ -149,9 +149,15 @@
             factors_ref[:, start:start + LANES] = block.astype(BF16)
 
 
-def weight_rows(unit, turned_ref, factors_ref):
-    turned_ref[...] = unit.T.reshape(turned_ref.shape)
-    turned = turned_ref[:, pl.ds(lax.axis_index("c"), 1)].reshape(WIDTH // 2, TOKENS).astype(BF16)
+def owned(normed, core):
+    feature = lax.broadcasted_iota(jnp.int32, (WIDTH, WIDTH // 2), 0)
+    place = lax.broadcasted_iota(jnp.int32, (WIDTH, WIDTH // 2), 1)
+    chosen = feature == place // 8 * 16 + core * 8 + place % 8
+    return jnp.dot(normed, chosen.astype(F32).astype(BF16), preferred_element_type=F32)
+
+
+def weight_rows(features, factors_ref):
+    turned = features.T.astype(BF16)
     left = lax.broadcasted_iota(jnp.int32, (128, 128), 1) < 64
     for pair in range(4):
         columns = factors_ref[:, pair * 384:(pair + 1) * 384]
@@ -162,14 +168,11 @@
         yield 2 * pair + 1, block[:, 256:], jnp.where(left, swapped[:128], middle[128:])
 
 
-TURNED = (WIDTH // 16, 2, 8, TOKENS)
-
-
 def window_pass(diag, lat, lon, own, w_qkv, w_proj):
     return pl.pallas_call(
         window_kernel,
         out_shape=[
-            jax.ShapeDtypeStruct((TOKENS, 4 * WIDTH), BF16),
+            jax.ShapeDtypeStruct((TOKENS, 3 * WIDTH + WIDTH // 2), BF16),
             jax.ShapeDtypeStruct((TOKENS, WIDTH), F32),
             jax.ShapeDtypeStruct((TOKENS, 128), F32),
         ],
@@ -179,10 +182,11 @@
 
 def inputs_kernel(
     factors_ref, unit_ref, inv_std_ref, w_qkv_ref,
-    keep_ref, d_own_ref, d_side_ref, d_lat_ref, turned_ref,
+    keep_ref, d_own_ref, d_side_ref, d_lat_ref,
 ):
     unit = unit_ref[...]
-    for index, whole, folded in weight_rows(unit, turned_ref, factors_ref):
+    features = owned(unit.astype(BF16), lax.axis_index("c"))
+    for index, whole, folded in weight_rows(features, factors_ref):
         keep_ref[index, :256, :] = whole
         keep_ref[index, 256:, :] = folded
     d_normed = dot(factors_ref[:, :3 * WIDTH], w_qkv_ref[...], NT)
@@ -204,15 +208,14 @@
     return pl.pallas_call(
         inputs_kernel,
         out_shape=[weight, piece, side, piece],
-        scratch_shapes=[pltpu.VMEM(TURNED, F32)],
         compiler_params=SMALL,
     )(factors, unit, inv_std, w_qkv)
 
 
-def add_kernel(keep_ref, taken_ref, side_in, out_ref, side_out, hold_ref, turned_ref, sems):
+def add_kernel(keep_ref, taken_ref, side_in, out_ref, side_out, hold_ref, sems):
     stores = []
-    unit = taken_ref[:, 3 * WIDTH:].astype(F32)
-    for index, whole, folded in weight_rows(unit, turned_ref, taken_ref):
+    features = taken_ref[:, 3 * WIDTH:].astype(F32)
+    for index, whole, folded in weight_rows(features, taken_ref):
         hold_ref[index, :256, :] = (keep_ref[index, :256, :] + whole).astype(BF16)
         hold_ref[index, 256:, :] = (keep_ref[index, 256:, :] + folded).astype(BF16)
         store = pltpu.make_async_copy(hold_ref.at[index], out_ref.at[index], sems.at[index])
@@ -235,7 +238,6 @@
         input_output_aliases={2: 1},
         scratch_shapes=[
             pltpu.VMEM(keep.shape, BF16),
-            pltpu.VMEM(TURNED, F32),
             pltpu.SemaphoreType.DMA((8,)),
         ],
         compiler_params=SMALL,

time: 65.4 us -> 65.2 us (level)
  transfers between devices with their start and end apart: 8 -> 8, of which waited for: 5 -> 5; matrix products, arithmetic and copies ran while one was open for 0% -> 0% of each run, Pallas kernels for 5% -> 6%
where the time goes in v8:
time: 65.2 us; the launch traced here: 64.6 us
  starting transfers between devices  32.1 us (49%)
  waiting for transfers between devices  21.4 us (33%)
  Pallas kernels  9.26 us (14%)
  local copies, waits for them, and re-layouts  1.07 us (2%)
  between operations  0.77 us (1%)
    ppermute x4, starting transfers between devices, turn(): lax.ppermute(block, axes, [(i, (i + distance) % count) for i in range(cou...  12.4 us
    ppermute x4, waiting for transfers between devices, turn(): lax.ppermute(block, axes, [(i, (i + distance) % count) for i in range(cou...  9.7 us
    all_to_all x1, starting transfers between devices, per_device(): by_rows = lax.all_to_all(rows, LON, 0, 0, axis_index_groups=groups)  7.83 us
    all_to_all x1, waiting for transfers between devices, per_device(): by_columns = lax.all_to_all(chip, LAT, 0, 0)  7.69 us
    all_to_all x1, starting transfers between devices, per_device(): by_columns = lax.all_to_all(chip, LAT, 0, 0)  6.3 us
    ppermute x1, starting transfers between devices, turn_both(): return lax.ppermute(block, LON + LAT, route)  3.63 us
    ppermute x1, waiting for transfers between devices, turn_both(): return lax.ppermute(block, LON + LAT, route)  3.5 us
    pallas_call x1, Pallas kernels, window_pass(): pl.pallas_call(window_kernel, out_shape=[jax.ShapeDtypeStruct((TOKENS, 3...  2.47 us
  transfers between devices with their start and end apart: 8, of which 5 were waited for; matrix products, arithmetic and copies ran while one was open for 0% of the time, Pallas kernels for 6%

profile of v8, /device:TPU:6, one launch (start us, length us, event | category | flops | bytes accessed | tf_op | source)
XLA Modules:
  0.0 64.6 jit_solution(2123577555896536680)
XLA Ops:
  0.6 1.0 %shard_map.59 = (bf16[2,3,6,2,512]{4,3,2,1,0:T(2,128)(2,1)S(1)}, bf16[2,3,6,2,512]{4,3,2,1,0:T(2,128)(2,1)S(1)}, bf16[2,3,6,2,512]{4,3,2,1,0:T(2,128)(2,1)S(1)}, bf16[2,3,6,2,512]{4,3,2,1,0:T(2,128)(2,1)S(1)}) custom-call(bf16[6,12,2,512]{3,2,1,0:T(2,128)(2,1)} %bitcast.7, bf16[6,12,2,512]{3,2,1,0:T(2,128)(2,1)} %bitcast.4), custom_call_target="tpu_custom_call" | custom-call | tf_op jit(solution)/shard_map/pallas_call | solution.py:57
  1.6 3.6 %collective-permute-start = (bf16[2,3,6,2,512]{4,3,2,1,0:T(2,128)(2,1)S(1)}, bf16[2,3,6,2,512]{4,3,2,1,0:T(2,128)(2,1)S(1)}, u32[]{:S(2)}, u32[]{:S(2)}) collective-permute-start(bf16[2,3,6,2,512]{4,3,2,1,0:T(2,128)(2,1)S(1)} %get-tuple-element.21), channel_id=1, source_target_pairs={{0,9},{1,10},{2,11},{3,12},{4,13},{5,14},{6,15},{7,8},{8,17},{9,18... | collective-permute-start | bytes 221192 | tf_op jit(solution)/shard_map/ppermute | solution.py:318
  5.2 3.4 %collective-permute-start.1 = (bf16[2,3,6,2,512]{4,3,2,1,0:T(2,128)(2,1)S(1)}, bf16[2,3,6,2,512]{4,3,2,1,0:T(2,128)(2,1)S(1)}, u32[]{:S(2)}, u32[]{:S(2)}) collective-permute-start(bf16[2,3,6,2,512]{4,3,2,1,0:T(2,128)(2,1)S(1)} %get-tuple-element.22), channel_id=1, source_target_pairs={{0,1},{1,2},{2,3},{3,4},{4,5},{5,6},{6,7},{7,0},{8,9},{9,10},{10,1... | collective-permute-start | bytes 221192 | tf_op jit(solution)/shard_map/ppermute | solution.py:308
  8.7 3.3 %collective-permute-start.2 = (bf16[2,3,6,2,512]{4,3,2,1,0:T(2,128)(2,1)S(1)}, bf16[2,3,6,2,512]{4,3,2,1,0:T(2,128)(2,1)S(1)}, u32[]{:S(2)}, u32[]{:S(2)}) collective-permute-start(bf16[2,3,6,2,512]{4,3,2,1,0:T(2,128)(2,1)S(1)} %get-tuple-element.23), channel_id=1, source_target_pairs={{0,8},{8,16},{16,24},{24,32},{32,40},{40,48},{48,56},{56,64},{64,7... | collective-permute-start | bytes 221192 | tf_op jit(solution)/shard_map/ppermute | solution.py:308
  12.0 0.0 copy-start.1
  12.0 1.0 %copy-done.1 = bf16[512,512]{1,0:T(8,128)(2,1)S(1)} copy-done((bf16[512,512]{1,0:T(8,128)(2,1)S(1)}, bf16[512,512]{1,0:T(8,128)(2,1)}, u32[]{:S(2)}) %copy-start.1) | copy-done | bytes 524312
  13.0 1.4 %shard_map.60 = (bf16[512,1536]{1,0:T(8,128)(2,1)S(1)}, bf16[512,512]{1,0:T(8,128)(2,1)S(1)}) custom-call(bf16[512,1536]{1,0:T(8,128)(2,1)} %refs_0_.1, bf16[512,512]{1,0:T(8,128)(2,1)S(1)} %copy-done.1), custom_call_target="tpu_custom_call" | custom-call | tf_op jit(solution)/shard_map/pallas_call | solution.py:79
  14.5 3.5 %collective-permute-done.diag_ref = bf16[2,3,6,2,512]{4,3,2,1,0:T(2,128)(2,1)S(1)} collective-permute-done((bf16[2,3,6,2,512]{4,3,2,1,0:T(2,128)(2,1)S(1)}, bf16[2,3,6,2,512]{4,3,2,1,0:T(2,128)(2,1)S(1)}, u32[]{:S(2)}, u32[]{:S(2)}) %collective-permute-start) | collective-permute-done | bytes 73760 | tf_op jit(solution)/shard_map/ppermute | solution.py:318
  18.0 0.0 collective-permute-done.1.lat_ref
  18.0 4.0 %collective-permute-done.2.lon_ref = bf16[2,3,6,2,512]{4,3,2,1,0:T(2,128)(2,1)S(1)} collective-permute-done((bf16[2,3,6,2,512]{4,3,2,1,0:T(2,128)(2,1)S(1)}, bf16[2,3,6,2,512]{4,3,2,1,0:T(2,128)(2,1)S(1)}, u32[]{:S(2)}, u32[]{:S(2)}) %collective-permute-start.2) | collective-permute-done | bytes 73760 | tf_op jit(solution)/shard_map/ppermute | solution.py:308
  22.0 2.5 %shard_map.61 = (bf16[144,1792]{1,0:T(8,128)(2,1)S(1)}, f32[144,512]{1,0:T(8,128)S(1)}, f32[144,128]{1,0:T(8,128)S(1)}) custom-call(bf16[2,3,6,2,512]{4,3,2,1,0:T(2,128)(2,1)S(1)} %collective-permute-done.diag_ref, bf16[2,3,6,2,512]{4,3,2,1,0:T(2,128)(2,1)S(1)} %collective-permute-done.1.lat_ref, ...), custom_call_target="tpu_custom_call" | custom-call | tf_op jit(solution)/shard_map/pallas_call | solution.py:172
  24.5 1.9 %collective-permute-start.3 = (bf16[144,1792]{1,0:T(8,128)(2,1)S(1)}, bf16[144,1792]{1,0:T(8,128)(2,1)S(1)}, u32[]{:S(2)}, u32[]{:S(2)}) collective-permute-start(bf16[144,1792]{1,0:T(8,128)(2,1)S(1)} %get-tuple-element.27.factors_ref), channel_id=1, source_target_pairs={{0,8},{8,0},{1,9},{9,1},{2,10},{10,2},{3,11},{11,3},{4,12},{12,4},... | collective-permute-start | bytes 1548296 | tf_op jit(solution)/shard_map/ppermute | solution.py:330
  26.4 1.4 %shard_map.62 = (f32[8,384,128]{2,1,0:T(8,128)S(1)}, bf16[3,6,2,512]{3,2,1,0:T(2,128)(2,1)S(1)}, bf16[2,3,6,2,512]{4,3,2,1,0:T(2,128)(2,1)S(1)}, bf16[3,6,2,512]{3,2,1,0:T(2,128)(2,1)S(1)}) custom-call(bf16[144,1792]{1,0:T(8,128)(2,1)S(1)} %get-tuple-element.27.factors_ref, f32[144,512]{1,0:T(8,128)S(1)} %get-tuple-element.28.unit_ref, ...), custom_call_target="tpu_custom_call" | custom-call | tf_op jit(solution)/shard_map/pallas_call | solution.py:208
  27.8 0.5 collective-permute-done.3.taken_ref
  28.3 1.3 %shard_map.63 = (bf16[8,384,128]{2,1,0:T(8,128)(2,1)}, bf16[2,3,6,2,512]{4,3,2,1,0:T(2,128)(2,1)S(1)}) custom-call(f32[8,384,128]{2,1,0:T(8,128)S(1)} %get-tuple-element.31.keep_ref, bf16[144,1792]{1,0:T(8,128)(2,1)S(1)} %collective-permute-done.3.taken_ref, bf16[2,3,6,2,512]{4,3,2,1,0:T(2,128)(2,1)S(1)} %get-tuple-element.32.side_in), custom_call_target="tpu_custom_call", output_to_operand_aliasing={{1}: (2, {})} | custom-call | tf_op jit(solution)/shard_map/pallas_call | solution.py:231
  29.6 0.0 copy-start
  29.6 6.3 %all-to-all-start = ((bf16[8,384,128]{2,1,0:T(8,128)(2,1)}), bf16[8,384,128]{2,1,0:T(8,128)(2,1)S(1)}, u32[]{:S(2)}, u32[]{:S(2)}) async-start(bf16[8,384,128]{2,1,0:T(8,128)(2,1)} %get-tuple-element.34), calls=%async_computation | async-start | bytes 1572864 | tf_op jit(solution)/shard_map/all_to_all | solution.py:333
  35.9 2.9 %collective-permute-start.4 = (bf16[2,3,6,2,512]{4,3,2,1,0:T(2,128)(2,1)S(1)}, bf16[2,3,6,2,512]{4,3,2,1,0:T(2,128)(2,1)S(1)}, u32[]{:S(2)}, u32[]{:S(2)}) collective-permute-start(bf16[2,3,6,2,512]{4,3,2,1,0:T(2,128)(2,1)S(1)} %get-tuple-element.33), channel_id=1, source_target_pairs={{0,504},{8,0},{16,8},{24,16},{32,24},{40,32},{48,40},{56,48},{64,5... | collective-permute-start | bytes 221192 | tf_op jit(solution)/shard_map/ppermute | solution.py:308
  38.8 7.7 %all-to-all-done.parts_ref = bf16[8,384,128]{2,1,0:T(8,128)(2,1)S(1)} async-done(((bf16[8,384,128]{2,1,0:T(8,128)(2,1)}), bf16[8,384,128]{2,1,0:T(8,128)(2,1)S(1)}, u32[]{:S(2)}, u32[]{:S(2)}) %all-to-all-start) | async-done | bytes 786464 | tf_op jit(solution)/shard_map/all_to_all | solution.py:333
  46.5 0.8 %shard_map.64 = (bf16[32,8,192]{2,1,0:T(8,128)(2,1)}, bf16[3,6,2,512]{3,2,1,0:T(2,128)(2,1)S(1)}) custom-call(bf16[8,384,128]{2,1,0:T(8,128)(2,1)S(1)} %all-to-all-done.parts_ref, bf16[3,6,2,512]{3,2,1,0:T(2,128)(2,1)S(1)} %get-tuple-element.35.lat_in), custom_call_target="tpu_custom_call", output_to_operand_aliasing={{1}: (1, {})} | custom-call | tf_op jit(solution)/shard_map/pallas_call | solution.py:294
  47.3 7.8 %all-to-all-start.1 = ((bf16[32,8,192]{2,1,0:T(8,128)(2,1)}), bf16[32,8,192]{2,1,0:T(8,128)(2,1)S(1)}, u32[]{:S(2)}, u32[]{:S(2)}) async-start(bf16[32,8,192]{2,1,0:T(8,128)(2,1)} %get-tuple-element.37), calls=%async_computation.1 | async-start | bytes 262144 | tf_op jit(solution)/shard_map/all_to_all | solution.py:337
  55.1 0.0 collective-permute-done.4.side_ref
  55.1 0.1 pad_maximum_fusion
  55.2 2.8 %collective-permute-start.5 = (bf16[2,3,6,2,512]{4,3,2,1,0:T(2,128)(2,1)S(1)}, bf16[2,3,6,2,512]{4,3,2,1,0:T(2,128)(2,1)S(1)}, u32[]{:S(2)}, u32[]{:S(2)}) collective-permute-start(bf16[2,3,6,2,512]{4,3,2,1,0:T(2,128)(2,1)S(1)} %pad_maximum_fusion), channel_id=1, source_target_pairs={{0,7},{1,0},{2,1},{3,2},{4,3},{5,4},{6,5},{7,6},{8,15},{9,8},{10,9... | collective-permute-start | bytes 221192 | tf_op jit(solution)/shard_map/ppermute | solution.py:308
  58.1 5.7 %collective-permute-done.5.ahead_ref = bf16[2,3,6,2,512]{4,3,2,1,0:T(2,128)(2,1)S(1)} collective-permute-done((bf16[2,3,6,2,512]{4,3,2,1,0:T(2,128)(2,1)S(1)}, bf16[2,3,6,2,512]{4,3,2,1,0:T(2,128)(2,1)S(1)}, u32[]{:S(2)}, u32[]{:S(2)}) %collective-permute-start.5) | collective-permute-done | bytes 73760 | tf_op jit(solution)/shard_map/ppermute | solution.py:308
  63.7 0.0 all-to-all-done.1.rows_ref
  63.7 0.0 copy-done
  63.7 0.9 %shard_map.65 = (bf16[6,12,2,512]{3,2,1,0:T(2,128)(2,1)}, f32[8,192]{1,0:T(8,128)}) custom-call(bf16[6,12,2,512]{3,2,1,0:T(2,128)(2,1)S(1)} %bitcast.5, bf16[3,6,2,512]{3,2,1,0:T(2,128)(2,1)S(1)} %get-tuple-element.30.own_ref, bf16[2,3,6,2,512]{4,3,2,1,0:T(2,128)(2,1)S(1)} %collective-permute-done.4.side_ref, ...), custom_call_target="tpu_custom_call" | custom-call | tf_op jit(solution)/shard_map/pallas_call | solution.py:270
  (1 shorter events, 0.0 us)
Async XLA Ops:
  1.6 16.4 %collective-permute-start = (bf16[2,3,6,2,512]{4,3,2,1,0:T(2,128)(2,1)S(1)}, bf16[2,3,6,2,512]{4,3,2,1,0:T(2,128)(2,1)S(1)}, u32[]{:S(2)}, u32[]{:S(2)}) collective-permute-start(bf16[2,3,6,2,512]{4,3,2,1,0:T(2,128)(2,1)S(1)} %get-tuple-element.21), channel_id=1, source_target_pairs={{0,9},{1,10},{2,11},{3,12},{4,13},{5,14},{6,15},{7,8},{8,17},{9,18... | collective-permute-start | bytes 221192 | tf_op jit(solution)/shard_map/ppermute | solution.py:318
  5.2 12.7 %collective-permute-start.1 = (bf16[2,3,6,2,512]{4,3,2,1,0:T(2,128)(2,1)S(1)}, bf16[2,3,6,2,512]{4,3,2,1,0:T(2,128)(2,1)S(1)}, u32[]{:S(2)}, u32[]{:S(2)}) collective-permute-start(bf16[2,3,6,2,512]{4,3,2,1,0:T(2,128)(2,1)S(1)} %get-tuple-element.22), channel_id=1, source_target_pairs={{0,1},{1,2},{2,3},{3,4},{4,5},{5,6},{6,7},{7,0},{8,9},{9,10},{10,1... | collective-permute-start | bytes 221192 | tf_op jit(solution)/shard_map/ppermute | solution.py:308
  8.7 13.3 %collective-permute-start.2 = (bf16[2,3,6,2,512]{4,3,2,1,0:T(2,128)(2,1)S(1)}, bf16[2,3,6,2,512]{4,3,2,1,0:T(2,128)(2,1)S(1)}, u32[]{:S(2)}, u32[]{:S(2)}) collective-permute-start(bf16[2,3,6,2,512]{4,3,2,1,0:T(2,128)(2,1)S(1)} %get-tuple-element.23), channel_id=1, source_target_pairs={{0,8},{8,16},{16,24},{24,32},{32,40},{40,48},{48,56},{56,64},{64,7... | collective-permute-start | bytes 221192 | tf_op jit(solution)/shard_map/ppermute | solution.py:308
  12.0 1.0 %copy-start.1 = (bf16[512,512]{1,0:T(8,128)(2,1)S(1)}, bf16[512,512]{1,0:T(8,128)(2,1)}, u32[]{:S(2)}) copy-start(bf16[512,512]{1,0:T(8,128)(2,1)} %refs_1_.1) | copy-start | bytes 1572868
  24.5 3.8 %collective-permute-start.3 = (bf16[144,1792]{1,0:T(8,128)(2,1)S(1)}, bf16[144,1792]{1,0:T(8,128)(2,1)S(1)}, u32[]{:S(2)}, u32[]{:S(2)}) collective-permute-start(bf16[144,1792]{1,0:T(8,128)(2,1)S(1)} %get-tuple-element.27.factors_ref), channel_id=1, source_target_pairs={{0,8},{8,0},{1,9},{9,1},{2,10},{10,2},{3,11},{11,3},{4,12},{12,4},... | collective-permute-start | bytes 1548296 | tf_op jit(solution)/shard_map/ppermute | solution.py:330
  29.6 34.2 %copy-start = (bf16[2,6,12,512]{3,0,2,1:T(2,128)(2,1)S(1)}, bf16[2,6,12,512]{3,0,2,1:T(2,128)(2,1)}, u32[]{:S(2)}) copy-start(bf16[2,6,12,512]{3,0,2,1:T(2,128)(2,1)} %param.5) | copy-start | bytes 442372
  29.6 16.9 %all-to-all-start = ((bf16[8,384,128]{2,1,0:T(8,128)(2,1)}), bf16[8,384,128]{2,1,0:T(8,128)(2,1)S(1)}, u32[]{:S(2)}, u32[]{:S(2)}) async-start(bf16[8,384,128]{2,1,0:T(8,128)(2,1)} %get-tuple-element.34), calls=%async_computation | async-start | bytes 1572864 | tf_op jit(solution)/shard_map/all_to_all | solution.py:333
  35.9 19.2 %collective-permute-start.4 = (bf16[2,3,6,2,512]{4,3,2,1,0:T(2,128)(2,1)S(1)}, bf16[2,3,6,2,512]{4,3,2,1,0:T(2,128)(2,1)S(1)}, u32[]{:S(2)}, u32[]{:S(2)}) collective-permute-start(bf16[2,3,6,2,512]{4,3,2,1,0:T(2,128)(2,1)S(1)} %get-tuple-element.33), channel_id=1, source_target_pairs={{0,504},{8,0},{16,8},{24,16},{32,24},{40,32},{48,40},{56,48},{64,5... | collective-permute-start | bytes 221192 | tf_op jit(solution)/shard_map/ppermute | solution.py:308
  47.3 16.5 %all-to-all-start.1 = ((bf16[32,8,192]{2,1,0:T(8,128)(2,1)}), bf16[32,8,192]{2,1,0:T(8,128)(2,1)S(1)}, u32[]{:S(2)}, u32[]{:S(2)}) async-start(bf16[32,8,192]{2,1,0:T(8,128)(2,1)} %get-tuple-element.37), calls=%async_computation.1 | async-start | bytes 262144 | tf_op jit(solution)/shard_map/all_to_all | solution.py:337
  55.2 8.5 %collective-permute-start.5 = (bf16[2,3,6,2,512]{4,3,2,1,0:T(2,128)(2,1)S(1)}, bf16[2,3,6,2,512]{4,3,2,1,0:T(2,128)(2,1)S(1)}, u32[]{:S(2)}, u32[]{:S(2)}) collective-permute-start(bf16[2,3,6,2,512]{4,3,2,1,0:T(2,128)(2,1)S(1)} %pad_maximum_fusion), channel_id=1, source_target_pairs={{0,7},{1,0},{2,1},{3,2},{4,3},{5,4},{6,5},{7,6},{8,15},{9,8},{10,9... | collective-permute-start | bytes 221192 | tf_op jit(solution)/shard_map/ppermute | solution.py:308

commit v9 on v8

--- a/solution.py
+++ b/solution.py
@@ -276,7 +276,7 @@
     )(grads, own, side, ahead, rows)
 
 
-def columns_kernel(parts_ref, lat_in, out_ref, lat_out):
+def columns_kernel(parts_ref, out_ref):
     total = parts_ref[0].astype(F32)
     for index in range(1, 8):
         total = total + parts_ref[index].astype(F32)
@@ -288,19 +288,12 @@
         out_ref[place, :, 128:] = rests[tile // 16][fold - 256:fold - 248, :64].astype(BF16)
 
 
-def columns(parts, lat):
-    vmem = pl.BlockSpec(memory_space=pltpu.VMEM)
-    anywhere = pl.BlockSpec(memory_space=pl.ANY)
+def columns(parts):
     return pl.pallas_call(
         columns_kernel,
-        out_shape=[
-            jax.ShapeDtypeStruct((32, 8, 192), BF16), jax.ShapeDtypeStruct(lat.shape, BF16)
-        ],
-        in_specs=[vmem, anywhere],
-        out_specs=[vmem, anywhere],
-        input_output_aliases={1: 1},
+        out_shape=jax.ShapeDtypeStruct((32, 8, 192), BF16),
         compiler_params=SMALL,
-    )(parts, lat)
+    )(parts)
 
 
 def turn(block, axes, distance):
@@ -332,7 +325,7 @@
     chip, d_side = add(keep, taken, d_side)
     by_columns = lax.all_to_all(chip, LAT, 0, 0)
     d_side = turn(d_side, LON, -1)
-    rows, d_lat = columns(by_columns, d_lat)
+    rows = columns(by_columns)
     groups = [[2 * tile + core for tile in LON_ORDER] for core in range(2)]
     by_rows = lax.all_to_all(rows, LON, 0, 0, axis_index_groups=groups)
     d_ahead = turn(jnp.stack((d_lat, d_side[1])), LAT, -1)

time: 65.2 us -> 65.2 us (level)
  no operation moved by 1% of the time
where the time goes in v9:
time: 65.2 us; the launch traced here: 64.6 us
  starting transfers between devices  32.1 us (49%)
  waiting for transfers between devices  21.4 us (33%)
  Pallas kernels  9.26 us (14%)
  local copies, waits for them, and re-layouts  1.07 us (2%)
  between operations  0.77 us (1%)
    ppermute x4, starting transfers between devices, turn(): lax.ppermute(block, axes, [(i, (i + distance) % count) for i in range(cou...  12.4 us
    ppermute x4, waiting for transfers between devices, turn(): lax.ppermute(block, axes, [(i, (i + distance) % count) for i in range(cou...  9.7 us
    all_to_all x1, starting transfers between devices, per_device(): by_rows = lax.all_to_all(rows, LON, 0, 0, axis_index_groups=groups)  7.83 us
    all_to_all x1, waiting for transfers between devices, per_device(): by_columns = lax.all_to_all(chip, LAT, 0, 0)  7.69 us
    all_to_all x1, starting transfers between devices, per_device(): by_columns = lax.all_to_all(chip, LAT, 0, 0)  6.3 us
    ppermute x1, starting transfers between devices, turn_both(): return lax.ppermute(block, LON + LAT, route)  3.63 us
    ppermute x1, waiting for transfers between devices, turn_both(): return lax.ppermute(block, LON + LAT, route)  3.5 us
    pallas_call x1, Pallas kernels, window_pass(): pl.pallas_call(window_kernel, out_shape=[jax.ShapeDtypeStruct((TOKENS, 3...  2.47 us
  transfers between devices with their start and end apart: 8, of which 5 were waited for; matrix products, arithmetic and copies ran while one was open for 0% of the time, Pallas kernels for 6%

profile of v9, /device:TPU:6, one launch (start us, length us, event | category | flops | bytes accessed | tf_op | source)
XLA Modules:
  0.0 64.6 jit_solution(12349725288057206590)
XLA Ops:
  0.6 1.0 %shard_map.59 = (bf16[2,3,6,2,512]{4,3,2,1,0:T(2,128)(2,1)S(1)}, bf16[2,3,6,2,512]{4,3,2,1,0:T(2,128)(2,1)S(1)}, bf16[2,3,6,2,512]{4,3,2,1,0:T(2,128)(2,1)S(1)}, bf16[2,3,6,2,512]{4,3,2,1,0:T(2,128)(2,1)S(1)}) custom-call(bf16[6,12,2,512]{3,2,1,0:T(2,128)(2,1)} %bitcast.7, bf16[6,12,2,512]{3,2,1,0:T(2,128)(2,1)} %bitcast.4), custom_call_target="tpu_custom_call" | custom-call | tf_op jit(solution)/shard_map/pallas_call | solution.py:57
  1.6 3.6 %collective-permute-start = (bf16[2,3,6,2,512]{4,3,2,1,0:T(2,128)(2,1)S(1)}, bf16[2,3,6,2,512]{4,3,2,1,0:T(2,128)(2,1)S(1)}, u32[]{:S(2)}, u32[]{:S(2)}) collective-permute-start(bf16[2,3,6,2,512]{4,3,2,1,0:T(2,128)(2,1)S(1)} %get-tuple-element.19), channel_id=1, source_target_pairs={{0,9},{1,10},{2,11},{3,12},{4,13},{5,14},{6,15},{7,8},{8,17},{9,18... | collective-permute-start | bytes 221192 | tf_op jit(solution)/shard_map/ppermute | solution.py:311
  5.2 3.4 %collective-permute-start.1 = (bf16[2,3,6,2,512]{4,3,2,1,0:T(2,128)(2,1)S(1)}, bf16[2,3,6,2,512]{4,3,2,1,0:T(2,128)(2,1)S(1)}, u32[]{:S(2)}, u32[]{:S(2)}) collective-permute-start(bf16[2,3,6,2,512]{4,3,2,1,0:T(2,128)(2,1)S(1)} %get-tuple-element.20), channel_id=1, source_target_pairs={{0,1},{1,2},{2,3},{3,4},{4,5},{5,6},{6,7},{7,0},{8,9},{9,10},{10,1... | collective-permute-start | bytes 221192 | tf_op jit(solution)/shard_map/ppermute | solution.py:301
  8.7 3.3 %collective-permute-start.2 = (bf16[2,3,6,2,512]{4,3,2,1,0:T(2,128)(2,1)S(1)}, bf16[2,3,6,2,512]{4,3,2,1,0:T(2,128)(2,1)S(1)}, u32[]{:S(2)}, u32[]{:S(2)}) collective-permute-start(bf16[2,3,6,2,512]{4,3,2,1,0:T(2,128)(2,1)S(1)} %get-tuple-element.21), channel_id=1, source_target_pairs={{0,8},{8,16},{16,24},{24,32},{32,40},{40,48},{48,56},{56,64},{64,7... | collective-permute-start | bytes 221192 | tf_op jit(solution)/shard_map/ppermute | solution.py:301
  12.0 0.0 copy-start.1
  12.0 1.0 %copy-done.1 = bf16[512,512]{1,0:T(8,128)(2,1)S(1)} copy-done((bf16[512,512]{1,0:T(8,128)(2,1)S(1)}, bf16[512,512]{1,0:T(8,128)(2,1)}, u32[]{:S(2)}) %copy-start.1) | copy-done | bytes 524312
  13.0 1.4 %shard_map.60 = (bf16[512,1536]{1,0:T(8,128)(2,1)S(1)}, bf16[512,512]{1,0:T(8,128)(2,1)S(1)}) custom-call(bf16[512,1536]{1,0:T(8,128)(2,1)} %refs_0_.1, bf16[512,512]{1,0:T(8,128)(2,1)S(1)} %copy-done.1), custom_call_target="tpu_custom_call" | custom-call | tf_op jit(solution)/shard_map/pallas_call | solution.py:79
  14.5 3.5 %collective-permute-done.diag_ref = bf16[2,3,6,2,512]{4,3,2,1,0:T(2,128)(2,1)S(1)} collective-permute-done((bf16[2,3,6,2,512]{4,3,2,1,0:T(2,128)(2,1)S(1)}, bf16[2,3,6,2,512]{4,3,2,1,0:T(2,128)(2,1)S(1)}, u32[]{:S(2)}, u32[]{:S(2)}) %collective-permute-start) | collective-permute-done | bytes 73760 | tf_op jit(solution)/shard_map/ppermute | solution.py:311
  18.0 0.0 collective-permute-done.1.lat_ref
  18.0 4.0 %collective-permute-done.2.lon_ref = bf16[2,3,6,2,512]{4,3,2,1,0:T(2,128)(2,1)S(1)} collective-permute-done((bf16[2,3,6,2,512]{4,3,2,1,0:T(2,128)(2,1)S(1)}, bf16[2,3,6,2,512]{4,3,2,1,0:T(2,128)(2,1)S(1)}, u32[]{:S(2)}, u32[]{:S(2)}) %collective-permute-start.2) | collective-permute-done | bytes 73760 | tf_op jit(solution)/shard_map/ppermute | solution.py:301
  22.0 2.5 %shard_map.61 = (bf16[144,1792]{1,0:T(8,128)(2,1)S(1)}, f32[144,512]{1,0:T(8,128)S(1)}, f32[144,128]{1,0:T(8,128)S(1)}) custom-call(bf16[2,3,6,2,512]{4,3,2,1,0:T(2,128)(2,1)S(1)} %collective-permute-done.diag_ref, bf16[2,3,6,2,512]{4,3,2,1,0:T(2,128)(2,1)S(1)} %collective-permute-done.1.lat_ref, ...), custom_call_target="tpu_custom_call" | custom-call | tf_op jit(solution)/shard_map/pallas_call | solution.py:172
  24.5 1.9 %collective-permute-start.3 = (bf16[144,1792]{1,0:T(8,128)(2,1)S(1)}, bf16[144,1792]{1,0:T(8,128)(2,1)S(1)}, u32[]{:S(2)}, u32[]{:S(2)}) collective-permute-start(bf16[144,1792]{1,0:T(8,128)(2,1)S(1)} %get-tuple-element.25.factors_ref), channel_id=1, source_target_pairs={{0,8},{8,0},{1,9},{9,1},{2,10},{10,2},{3,11},{11,3},{4,12},{12,4},... | collective-permute-start | bytes 1548296 | tf_op jit(solution)/shard_map/ppermute | solution.py:323
  26.4 1.4 %shard_map.62 = (f32[8,384,128]{2,1,0:T(8,128)S(1)}, bf16[3,6,2,512]{3,2,1,0:T(2,128)(2,1)S(1)}, bf16[2,3,6,2,512]{4,3,2,1,0:T(2,128)(2,1)S(1)}, bf16[3,6,2,512]{3,2,1,0:T(2,128)(2,1)S(1)}) custom-call(bf16[144,1792]{1,0:T(8,128)(2,1)S(1)} %get-tuple-element.25.factors_ref, f32[144,512]{1,0:T(8,128)S(1)} %get-tuple-element.26.unit_ref, ...), custom_call_target="tpu_custom_call" | custom-call | tf_op jit(solution)/shard_map/pallas_call | solution.py:208
  27.8 0.5 collective-permute-done.3.taken_ref
  28.3 1.3 %shard_map.63 = (bf16[8,384,128]{2,1,0:T(8,128)(2,1)}, bf16[2,3,6,2,512]{4,3,2,1,0:T(2,128)(2,1)S(1)}) custom-call(f32[8,384,128]{2,1,0:T(8,128)S(1)} %get-tuple-element.29.keep_ref, bf16[144,1792]{1,0:T(8,128)(2,1)S(1)} %collective-permute-done.3.taken_ref, bf16[2,3,6,2,512]{4,3,2,1,0:T(2,128)(2,1)S(1)} %get-tuple-element.30.side_in), custom_call_target="tpu_custom_call", output_to_operand_aliasing={{1}: (2, {})} | custom-call | tf_op jit(solution)/shard_map/pallas_call | solution.py:231
  29.6 0.0 copy-start
  29.6 6.3 %all-to-all-start = ((bf16[8,384,128]{2,1,0:T(8,128)(2,1)}), bf16[8,384,128]{2,1,0:T(8,128)(2,1)S(1)}, u32[]{:S(2)}, u32[]{:S(2)}) async-start(bf16[8,384,128]{2,1,0:T(8,128)(2,1)} %get-tuple-element.33), calls=%async_computation | async-start | bytes 1572864 | tf_op jit(solution)/shard_map/all_to_all | solution.py:326
  35.9 2.9 %collective-permute-start.4 = (bf16[2,3,6,2,512]{4,3,2,1,0:T(2,128)(2,1)S(1)}, bf16[2,3,6,2,512]{4,3,2,1,0:T(2,128)(2,1)S(1)}, u32[]{:S(2)}, u32[]{:S(2)}) collective-permute-start(bf16[2,3,6,2,512]{4,3,2,1,0:T(2,128)(2,1)S(1)} %get-tuple-element.31), channel_id=1, source_target_pairs={{0,504},{8,0},{16,8},{24,16},{32,24},{40,32},{48,40},{56,48},{64,5... | collective-permute-start | bytes 221192 | tf_op jit(solution)/shard_map/ppermute | solution.py:301
  38.8 7.7 %all-to-all-done.parts_ref = bf16[8,384,128]{2,1,0:T(8,128)(2,1)S(1)} async-done(((bf16[8,384,128]{2,1,0:T(8,128)(2,1)}), bf16[8,384,128]{2,1,0:T(8,128)(2,1)S(1)}, u32[]{:S(2)}, u32[]{:S(2)}) %all-to-all-start) | async-done | bytes 786464 | tf_op jit(solution)/shard_map/all_to_all | solution.py:326
  46.5 0.8 %shard_map.64 = bf16[32,8,192]{2,1,0:T(8,128)(2,1)} custom-call(bf16[8,384,128]{2,1,0:T(8,128)(2,1)S(1)} %all-to-all-done.parts_ref), custom_call_target="tpu_custom_call" | custom-call | tf_op jit(solution)/shard_map/pallas_call | solution.py:292
  47.3 7.8 %all-to-all-start.1 = ((bf16[32,8,192]{2,1,0:T(8,128)(2,1)}), bf16[32,8,192]{2,1,0:T(8,128)(2,1)S(1)}, u32[]{:S(2)}, u32[]{:S(2)}) async-start(bf16[32,8,192]{2,1,0:T(8,128)(2,1)} %shard_map.64), calls=%async_computation.1 | async-start | bytes 262144 | tf_op jit(solution)/shard_map/all_to_all | solution.py:330
  55.1 0.0 collective-permute-done.4.side_ref
  55.1 0.1 pad_maximum_fusion
  55.3 2.8 %collective-permute-start.5 = (bf16[2,3,6,2,512]{4,3,2,1,0:T(2,128)(2,1)S(1)}, bf16[2,3,6,2,512]{4,3,2,1,0:T(2,128)(2,1)S(1)}, u32[]{:S(2)}, u32[]{:S(2)}) collective-permute-start(bf16[2,3,6,2,512]{4,3,2,1,0:T(2,128)(2,1)S(1)} %pad_maximum_fusion), channel_id=1, source_target_pairs={{0,7},{1,0},{2,1},{3,2},{4,3},{5,4},{6,5},{7,6},{8,15},{9,8},{10,9... | collective-permute-start | bytes 221192 | tf_op jit(solution)/shard_map/ppermute | solution.py:301
  58.1 5.7 %collective-permute-done.5.ahead_ref = bf16[2,3,6,2,512]{4,3,2,1,0:T(2,128)(2,1)S(1)} collective-permute-done((bf16[2,3,6,2,512]{4,3,2,1,0:T(2,128)(2,1)S(1)}, bf16[2,3,6,2,512]{4,3,2,1,0:T(2,128)(2,1)S(1)}, u32[]{:S(2)}, u32[]{:S(2)}) %collective-permute-start.5) | collective-permute-done | bytes 73760 | tf_op jit(solution)/shard_map/ppermute | solution.py:301
  63.7 0.0 all-to-all-done.1.rows_ref
  63.7 0.0 copy-done
  63.7 0.9 %shard_map.65 = (bf16[6,12,2,512]{3,2,1,0:T(2,128)(2,1)}, f32[8,192]{1,0:T(8,128)}) custom-call(bf16[6,12,2,512]{3,2,1,0:T(2,128)(2,1)S(1)} %bitcast.5, bf16[3,6,2,512]{3,2,1,0:T(2,128)(2,1)S(1)} %get-tuple-element.28.own_ref, bf16[2,3,6,2,512]{4,3,2,1,0:T(2,128)(2,1)S(1)} %collective-permute-done.4.side_ref, ...), custom_call_target="tpu_custom_call" | custom-call | tf_op jit(solution)/shard_map/pallas_call | solution.py:270
  (1 shorter events, 0.0 us)
Async XLA Ops:
  1.6 16.4 %collective-permute-start = (bf16[2,3,6,2,512]{4,3,2,1,0:T(2,128)(2,1)S(1)}, bf16[2,3,6,2,512]{4,3,2,1,0:T(2,128)(2,1)S(1)}, u32[]{:S(2)}, u32[]{:S(2)}) collective-permute-start(bf16[2,3,6,2,512]{4,3,2,1,0:T(2,128)(2,1)S(1)} %get-tuple-element.19), channel_id=1, source_target_pairs={{0,9},{1,10},{2,11},{3,12},{4,13},{5,14},{6,15},{7,8},{8,17},{9,18... | collective-permute-start | bytes 221192 | tf_op jit(solution)/shard_map/ppermute | solution.py:311
  5.2 12.7 %collective-permute-start.1 = (bf16[2,3,6,2,512]{4,3,2,1,0:T(2,128)(2,1)S(1)}, bf16[2,3,6,2,512]{4,3,2,1,0:T(2,128)(2,1)S(1)}, u32[]{:S(2)}, u32[]{:S(2)}) collective-permute-start(bf16[2,3,6,2,512]{4,3,2,1,0:T(2,128)(2,1)S(1)} %get-tuple-element.20), channel_id=1, source_target_pairs={{0,1},{1,2},{2,3},{3,4},{4,5},{5,6},{6,7},{7,0},{8,9},{9,10},{10,1... | collective-permute-start | bytes 221192 | tf_op jit(solution)/shard_map/ppermute | solution.py:301
  8.7 13.3 %collective-permute-start.2 = (bf16[2,3,6,2,512]{4,3,2,1,0:T(2,128)(2,1)S(1)}, bf16[2,3,6,2,512]{4,3,2,1,0:T(2,128)(2,1)S(1)}, u32[]{:S(2)}, u32[]{:S(2)}) collective-permute-start(bf16[2,3,6,2,512]{4,3,2,1,0:T(2,128)(2,1)S(1)} %get-tuple-element.21), channel_id=1, source_target_pairs={{0,8},{8,16},{16,24},{24,32},{32,40},{40,48},{48,56},{56,64},{64,7... | collective-permute-start | bytes 221192 | tf_op jit(solution)/shard_map/ppermute | solution.py:301
  12.0 1.0 %copy-start.1 = (bf16[512,512]{1,0:T(8,128)(2,1)S(1)}, bf16[512,512]{1,0:T(8,128)(2,1)}, u32[]{:S(2)}) copy-start(bf16[512,512]{1,0:T(8,128)(2,1)} %refs_1_.1) | copy-start | bytes 1572868
  24.5 3.8 %collective-permute-start.3 = (bf16[144,1792]{1,0:T(8,128)(2,1)S(1)}, bf16[144,1792]{1,0:T(8,128)(2,1)S(1)}, u32[]{:S(2)}, u32[]{:S(2)}) collective-permute-start(bf16[144,1792]{1,0:T(8,128)(2,1)S(1)} %get-tuple-element.25.factors_ref), channel_id=1, source_target_pairs={{0,8},{8,0},{1,9},{9,1},{2,10},{10,2},{3,11},{11,3},{4,12},{12,4},... | collective-permute-start | bytes 1548296 | tf_op jit(solution)/shard_map/ppermute | solution.py:323
  29.6 34.2 %copy-start = (bf16[2,6,12,512]{3,0,2,1:T(2,128)(2,1)S(1)}, bf16[2,6,12,512]{3,0,2,1:T(2,128)(2,1)}, u32[]{:S(2)}) copy-start(bf16[2,6,12,512]{3,0,2,1:T(2,128)(2,1)} %param.5) | copy-start | bytes 442372
  29.6 16.9 %all-to-all-start = ((bf16[8,384,128]{2,1,0:T(8,128)(2,1)}), bf16[8,384,128]{2,1,0:T(8,128)(2,1)S(1)}, u32[]{:S(2)}, u32[]{:S(2)}) async-start(bf16[8,384,128]{2,1,0:T(8,128)(2,1)} %get-tuple-element.33), calls=%async_computation | async-start | bytes 1572864 | tf_op jit(solution)/shard_map/all_to_all | solution.py:326
  35.9 19.2 %collective-permute-start.4 = (bf16[2,3,6,2,512]{4,3,2,1,0:T(2,128)(2,1)S(1)}, bf16[2,3,6,2,512]{4,3,2,1,0:T(2,128)(2,1)S(1)}, u32[]{:S(2)}, u32[]{:S(2)}) collective-permute-start(bf16[2,3,6,2,512]{4,3,2,1,0:T(2,128)(2,1)S(1)} %get-tuple-element.31), channel_id=1, source_target_pairs={{0,504},{8,0},{16,8},{24,16},{32,24},{40,32},{48,40},{56,48},{64,5... | collective-permute-start | bytes 221192 | tf_op jit(solution)/shard_map/ppermute | solution.py:301
  47.3 16.5 %all-to-all-start.1 = ((bf16[32,8,192]{2,1,0:T(8,128)(2,1)}), bf16[32,8,192]{2,1,0:T(8,128)(2,1)S(1)}, u32[]{:S(2)}, u32[]{:S(2)}) async-start(bf16[32,8,192]{2,1,0:T(8,128)(2,1)} %shard_map.64), calls=%async_computation.1 | async-start | bytes 262144 | tf_op jit(solution)/shard_map/all_to_all | solution.py:330
  55.3 8.5 %collective-permute-start.5 = (bf16[2,3,6,2,512]{4,3,2,1,0:T(2,128)(2,1)S(1)}, bf16[2,3,6,2,512]{4,3,2,1,0:T(2,128)(2,1)S(1)}, u32[]{:S(2)}, u32[]{:S(2)}) collective-permute-start(bf16[2,3,6,2,512]{4,3,2,1,0:T(2,128)(2,1)S(1)} %pad_maximum_fusion), channel_id=1, source_target_pairs={{0,7},{1,0},{2,1},{3,2},{4,3},{5,4},{6,5},{7,6},{8,15},{9,8},{10,9... | collective-permute-start | bytes 221192 | tf_op jit(solution)/shard_map/ppermute | solution.py:301
